TPU v7x, 512 devices: a whole 4x4x16 slice. The times are simulated.
512 devices in a mesh: dp: 4 (over x_hi, core), tp: 4 (over y), ep: 32 (over x_lo, z).
Axes of the slice: x: 4 (x_hi: 2, x_lo: 2; x = x_hi * 2 + x_lo), y: 4, z: 16, core: 2. Of those that a mesh axis runs over, the one named last changes fastest.
Arguments:
- queries: bfloat16 [384, 128, 576], P(('dp', 'ep'), 'tp'), may hold values from -24 to 24
- cache: bfloat16 [3072, 128, 576], P(('dp', 'tp', 'ep')), may hold values from -12 to 12
- tables: int32 [512, 6], P(('dp', 'tp', 'ep')), may hold values from 0 to 5, each once within a row
- lengths: int32 [4, 32, 3], P('dp', 'ep'), may hold values from 1 to 1024, 2048 in all within a row
- mig_cache: bfloat16 [1024, 128, 576], P(('dp', 'tp', 'ep')), may hold values from -12 to 12
- mig_src: int32 [32], P('ep'), may hold values from 0 to 3
- mig_dst: int32 [32], P('ep'), may hold values from 0 to 3, as said below
- mig_seq: int32 [32], P('ep'), may hold values from 0 to 2
- tokens: bfloat16 [8192, 3584], P(('dp', 'tp', 'ep')), may hold values from -6 to 6
- routes: int32 [8192, 2], P(('dp', 'tp', 'ep')), may hold values from 0 to 31, all different within a row; in each aligned block of 16 rows (0 to 15, 16 to 31, ...) at most 2 rows name the same one
- gates: float32 [8192, 2], P(('dp', 'tp', 'ep')), may hold values from 0.1 to 1
- gate_w: bfloat16 [32, 3584, 2048], P('ep', None, ('dp', 'tp')), may hold values from -0.09375 to 0.09375
- up_w: bfloat16 [32, 3584, 2048], P('ep', None, ('dp', 'tp')), may hold values from -0.09375 to 0.09375
- down_w: bfloat16 [32, 2048, 3584], P('ep', None, ('dp', 'tp')), may hold values from -0.125 to 0.125
Outputs:
- attn_out: bfloat16 [384, 128, 512], P(('dp', 'ep'), 'tp')
- moe_out: bfloat16 [8192, 3584], P(('dp', 'tp', 'ep'))
Inputs may be any that keep to these rules, and one draw needn't show every extreme that they name: `tables`: each device's row is an ordering of its 6 page ids. The lengths of each group's 3 requests sum to 2048. `mig_dst`: differs from mig_src at every index. `routes`: each row names 2 different experts; in the rows of one device no expert is named more than 2 times, a bound that some block reaches.
All inputs are finite; a program needn't handle non-finite values.
Results may differ from a plain program's by a relative error of at most 0.0058.
Values may be sent and summed in bfloat16 or wider, within the bound.
No kernel may reach another device: no remote copies, remote signals or barrier semaphores. Data moves between devices by JAX's collectives and lax.ppermute only.
A program may use at most 64 MiB of HBM per device.

v0:
```python
import jax
import jax.numpy as jnp
from jax import lax
from jax.sharding import PartitionSpec as P

KV_RANK = 512
ROPE_DIM = 64
PAGE = 128
SLOTS = 2


score_scale = 0.07216878364870322
neg_fill = -1e30


def broadcast(x, axis, root):
    mine = lax.axis_index(axis) == root
    return lax.psum(jnp.where(mine, x, jnp.zeros_like(x)), axis)


def per_device(
    queries,
    cache,
    tables,
    lengths,
    mig_cache,
    mig_src,
    mig_dst,
    mig_seq,
    tokens,
    routes,
    gates,
    gate_w,
    up_w,
    down_w,
):
    tensor_parallel_ranks = lax.axis_size("tp")
    rank_tp = lax.axis_index("tp")
    rank_dp = lax.axis_index("dp")
    row_width = KV_RANK + ROPE_DIM
    group_query = lax.all_gather(queries, "tp", axis=1, tiled=True)
    seqs_group = group_query.shape[0]
    moved_pages = broadcast(mig_cache, "dp", mig_src[0])
    own_pages = cache[tables.reshape(seqs_group, SLOTS)]
    chosen = (rank_dp == mig_dst[0]) & (jnp.arange(seqs_group) == mig_seq[0])
    key_rows = jnp.where(chosen[:, None, None, None], moved_pages[None], own_pages)
    key_rows = key_rows.reshape(seqs_group, SLOTS * PAGE, row_width)
    positions = (
        (jnp.arange(SLOTS)[:, None] * tensor_parallel_ranks + rank_tp) * PAGE
        + jnp.arange(PAGE)[None, :]
    ).reshape(-1)
    valid = positions[None, :] < lengths[0, 0][:, None]
    scores = (
        jnp.einsum("shc,skc->shk", group_query, key_rows, preferred_element_type=jnp.float32)
        * score_scale
    )
    masked = jnp.where(valid[:, None, :], scores, neg_fill)
    part_max = jnp.max(masked, axis=2)
    weights = jnp.where(valid[:, None, :], jnp.exp(masked - part_max[..., None]), 0.0).astype(
        jnp.bfloat16
    )
    part_sum = jnp.sum(weights.astype(jnp.float32), axis=2)
    part_acc = jnp.einsum(
        "shk,skc->shc", weights, key_rows[:, :, :KV_RANK], preferred_element_type=jnp.float32
    )
    most = lax.pmax(part_max, "tp")
    factor = jnp.exp(part_max - most)
    numerator, denominator = (
        lax.psum_scatter(part_acc * factor[..., None], "tp", scatter_dimension=1, tiled=True),
        lax.psum_scatter(part_sum * factor, "tp", scatter_dimension=1, tiled=True),
    )
    attn_out = (numerator / denominator[..., None]).astype(jnp.bfloat16)
    ranks_ep = lax.axis_size("ep")
    token_rows = tokens.shape[0]
    top_routes = routes.shape[1]
    width = tokens.shape[1]
    capacity = min(token_rows, max(2, 2 * token_rows * top_routes // ranks_ep))
    slots_all = ranks_ep * capacity
    flattened_index_list = routes.reshape(-1)
    matches = (flattened_index_list[:, None] == jnp.arange(ranks_ep)[None, :]).astype(jnp.int32)
    before = jnp.cumsum(matches, axis=0) - matches
    column = flattened_index_list * capacity + jnp.sum(before * matches, axis=1)
    places = (column[:, None] == jnp.arange(slots_all)[None, :]).reshape(
        token_rows, top_routes, slots_all
    )
    selected_entries = jnp.any(places, axis=1).astype(jnp.bfloat16)
    dispatched_rows = lax.dot_general(
        selected_entries, tokens, (((0,), (0,)), ((), ())), preferred_element_type=jnp.float32
    )
    dispatched_rows = dispatched_rows.astype(jnp.bfloat16).reshape(ranks_ep, capacity, width)
    weight_gate = gate_w[0]
    weight_up = up_w[0]
    weight_down = down_w[0]
    arrived = lax.all_to_all(dispatched_rows, "ep", split_axis=0, concat_axis=0, tiled=True)
    piece = lax.all_gather(arrived[None], ("dp", "tp"), axis=0, tiled=True)
    piece_rows = piece.reshape(-1, width)
    gate = jnp.dot(piece_rows, weight_gate, preferred_element_type=jnp.float32)
    upward = jnp.dot(piece_rows, weight_up, preferred_element_type=jnp.float32)
    hidden_piece = (jax.nn.silu(gate) * upward).astype(jnp.bfloat16)
    hidden = hidden_piece.reshape(piece.shape[:-1] + (weight_gate.shape[1],))
    group_size = hidden.shape[0]
    total_rows = group_size * slots_all
    output_column_slice = weight_down.shape[1]
    summed = jnp.dot(
        lax.all_gather(hidden, ("dp", "tp"), axis=3, tiled=True).reshape(total_rows, -1),
        weight_down,
        preferred_element_type=jnp.float32,
    )
    expert_out = summed.astype(jnp.bfloat16)
    full_rows = lax.all_to_all(
        expert_out.reshape(group_size, slots_all, output_column_slice),
        ("dp", "tp"),
        split_axis=0,
        concat_axis=2,
        tiled=True,
    )
    returned = lax.all_to_all(
        full_rows.reshape(ranks_ep, capacity, width), "ep", split_axis=0, concat_axis=0, tiled=True
    )
    returned_rows = returned.reshape(slots_all, width)
    mixed = jnp.zeros((token_rows, width), jnp.float32)
    for route in range(top_routes):
        chosen_rows = jnp.dot(
            places[:, route].astype(jnp.bfloat16), returned_rows, preferred_element_type=jnp.float32
        )
        mixed = mixed + gates[:, route : route + 1] * chosen_rows
    return (attn_out, mixed.astype(jnp.bfloat16))


def solution(mesh):
    in_specs = (
        P(("dp", "ep"), "tp", None),
        P(("dp", "tp", "ep"), None, None),
        P(("dp", "tp", "ep"), None),
        P("dp", "ep", None),
        P(("dp", "tp", "ep"), None, None),
        P("ep"),
        P("ep"),
        P("ep"),
        P(("dp", "tp", "ep"), None),
        P(("dp", "tp", "ep"), None),
        P(("dp", "tp", "ep"), None),
        P("ep", None, ("dp", "tp")),
        P("ep", None, ("dp", "tp")),
        P("ep", None, ("dp", "tp")),
    )
    out_specs = (P(("dp", "ep"), "tp", None), P(("dp", "tp", "ep"), None))
    return jax.shard_map(
        per_device, mesh=mesh, in_specs=in_specs, out_specs=out_specs, check_vma=False
    )
```

profile of v0, /device:TPU:1, one launch (start us, length us, event | category | flops | bytes accessed | tf_op | source)
XLA Modules:
  0.0 339.2 jit_solution(14545952207446981841)
XLA Ops:
  8.1 0.8 copy.49
  10.2 1.2 convolution_convert_fusion
  11.6 44.4 %all_to_all.25 = bf16[32,2,3584]{2,1,0:T(2,128)(2,1)} all-to-all(bf16[32,2,3584]{2,1,0:T(2,128)(2,1)S(1)} %reshape.139), channel_id=1, replica_groups=mesh['dp'=4,'tp'=4,'ep'=32] {'ep'}, dimensions={0} | all-to-all | bytes 917504 | tf_op jit(solution)/shard_map/all_to_all | solution.py:94
  57.7 77.9 %all-gather.6.cloned.1.call-done = bf16[512,2,3584]{2,1,0:T(2,128)(2,1)} async-done(((bf16[32,2,3584]{2,1,0:T(2,128)(2,1)}), bf16[512,2,3584]{2,1,0:T(2,128)(2,1)}) %all-gather.6.cloned.1.call-update) | async-done | bytes 7340048 | tf_op jit(solution)/shard_map/all_gather | solution.py:95
  135.6 15.4 %reshape.140 = bf16[1024,3584]{1,0:T(8,128)(2,1)} reshape(bf16[512,2,3584]{2,1,0:T(2,128)(2,1)} %all-gather.6.cloned.1.call-done) | data formatting | bytes 14680064 | tf_op jit(solution)/shard_map/reshape | solution.py:96
  151.0 5.3 %fusion.7 = f32[1024,128]{1,0:T(8,128)S(1)} fusion(bf16[1024,3584]{1,0:T(8,128)(2,1)} %reshape.140, bf16[1,3584,128]{2,1,0:T(8,128)(2,1)S(1)} %copy-done.6), kind=kOutput, calls=%fused_computation.16 | convolution fusion | flops 939524096 | bytes 8781824 | tf_op jit(solution)/shard_map/dot_general | solution.py:97
  156.4 2.8 fusion.2
  163.2 9.8 %all_gather.9 = bf16[3,128,576]{2,1,0:T(8,128)(2,1)S(1)} all-gather(bf16[3,32,576]{2,1,0:T(8,128)(2,1)S(1)} %copy-done.3), channel_id=1, replica_groups=mesh['dp'=4,'tp'=4,'ep'=32] {'tp'}, dimensions={1}, use_global_device_ids=true | all-gather | bytes 552960 | tf_op jit(solution)/shard_map/all_gather | solution.py:41
  173.2 1.9 copy.45
  175.1 1.1 bitcast_select_fusion
  176.7 8.1 %pmax.7 = f32[3,128]{1,0:T(4,128)S(1)} all-reduce(f32[3,128]{1,0:T(4,128)S(1)} %get-tuple-element.8), channel_id=1, replica_groups=mesh['dp'=4,'tp'=4,'ep'=32] {'tp'}, use_global_device_ids=true, to_apply=%region_2.3 | all-reduce | flops 384 | bytes 3072 | tf_op jit(solution)/shard_map/pmax | solution.py:66
  185.0 60.5 %all-gather.4.cloned.1.call-done = bf16[16,32,2,2048]{3,2,1,0:T(2,128)(2,1)} async-done(((bf16[16,32,2,128]{3,2,1,0:T(2,128)(2,1)}), bf16[16,32,2,2048]{3,2,1,0:T(2,128)(2,1)}) %all-gather.4.cloned.1.call-update) | async-done | bytes 4194320 | tf_op jit(solution)/shard_map/all_gather | solution.py:105
  245.5 7.2 %reshape.142 = bf16[1024,2048]{1,0:T(8,128)(2,1)} reshape(bf16[16,32,2,2048]{3,2,1,0:T(2,128)(2,1)} %all-gather.4.cloned.1.call-done) | data formatting | bytes 8388608 | tf_op jit(solution)/shard_map/reshape | solution.py:105
  252.8 3.6 %convolution_convert_fusion.1 = bf16[1024,224]{0,1:T(8,128)(2,1)S(1)} fusion(bf16[1024,2048]{1,0:T(8,128)(2,1)} %reshape.142, bf16[1,2048,224]{1,2,0:T(8,128)(2,1)S(1)} %copy-done), kind=kOutput, calls=%fused_computation.7 | convolution fusion | flops 939753472 | bytes 5570560 | tf_op jit(solution)/shard_map/dot_general | solution.py:104
  256.4 1.0 copy.51
  257.4 6.7 %all-to-all-start.1 = ((bf16[16,64,224]{2,1,0:T(8,128)(2,1)}), bf16[16,64,224]{2,1,0:T(8,128)(2,1)S(1)}, u32[]{:S(2)}, u32[]{:S(2)}) async-start(bf16[16,64,224]{2,1,0:T(8,128)(2,1)} %bitcast.13), calls=%async_computation.2 | async-start | bytes 1048576 | tf_op jit(solution)/shard_map/all_to_all | solution.py:110
  265.0 1.4 convolution_multiply_fusion.2
  266.4 9.4 %all-to-all-done.1 = bf16[16,64,224]{2,1,0:T(8,128)(2,1)S(1)} async-done(((bf16[16,64,224]{2,1,0:T(8,128)(2,1)}), bf16[16,64,224]{2,1,0:T(8,128)(2,1)S(1)}, u32[]{:S(2)}, u32[]{:S(2)}) %all-to-all-start.1) | async-done | bytes 458784 | tf_op jit(solution)/shard_map/all_to_all | solution.py:110
  276.1 1.7 reshape.144
  277.8 12.3 %all-to-all-start.2 = ((bf16[32,2,3584]{2,1,0:T(2,128)(2,1)}), bf16[32,2,3584]{2,1,0:T(2,128)(2,1)S(1)}, u32[]{:S(2)}, u32[]{:S(2)}) async-start(bf16[32,2,3584]{2,1,0:T(2,128)(2,1)} %reshape.144), calls=%async_computation.3 | async-start | bytes 917504 | tf_op jit(solution)/shard_map/all_to_all | solution.py:117
  290.1 4.7 %reduce-scatter.7.cloned.1.call-done = f32[32,3]{1,0:T(8,128)} async-done(((f32[128,3]{1,0:T(8,128)}), f32[32,3]{1,0:T(8,128)}) %reduce-scatter.7.cloned.1.call-update) | async-done | bytes 400
  295.6 33.2 %reduce-scatter.5.cloned.1.call-done = f32[3,32,512]{2,1,0:T(8,128)} async-done(((f32[3,128,512]{2,1,0:T(8,128)}), f32[3,32,512]{2,1,0:T(8,128)}) %reduce-scatter.5.cloned.1.call-update) | async-done | bytes 196624 | tf_op jit(solution)/shard_map/reduce_scatter | solution.py:69
  328.8 1.7 divide_convert_fusion
  330.8 0.8 fusion.1
  (61 shorter events, 8.3 us)
Async XLA Ops:
  8.0 244.8 %copy-start = (bf16[1,2048,224]{1,2,0:T(8,128)(2,1)S(1)}, bf16[1,2048,224]{1,2,0:T(8,128)(2,1)}, u32[]{:S(2)}) copy-start(bf16[1,2048,224]{1,2,0:T(8,128)(2,1)} %param.27) | copy-start | bytes 2752516
  8.0 127.6 %all-gather.6.cloned.1.call-start = ((), (), s32[]{:S(2)}) async-start(), calls=%async_computation.8 | async-start | bytes 7798784 | tf_op jit(solution)/shard_map/all_gather | solution.py:95
  56.1 117.1 %all-reduce.2.cloned.1.call-start = ((), (), s32[]{:S(2)}) async-start(), calls=%async_computation.5 | async-start | bytes 589824 | tf_op jit(solution)/shard_map/psum | solution.py:18
  57.6 93.4 %copy-start.6 = (bf16[1,3584,128]{2,1,0:T(8,128)(2,1)S(1)}, bf16[1,3584,128]{2,1,0:T(8,128)(2,1)}, u32[]{:S(2)}) copy-start(bf16[1,3584,128]{2,1,0:T(8,128)(2,1)} %param.25) | copy-start | bytes 2752516
  57.6 187.9 %all-gather.4.cloned.1.call-start = ((), (), s32[]{:S(2)}) async-start(), calls=%async_computation.7 | async-start | bytes 4456448 | tf_op jit(solution)/shard_map/all_gather | solution.py:105
  151.0 5.3 %copy-start.1 = (bf16[1024,3584]{1,0:T(8,128)(2,1)S(1)}, bf16[1024,3584]{1,0:T(8,128)(2,1)}, u32[]{:S(2)}) copy-start(bf16[1024,3584]{1,0:T(8,128)(2,1)} %reshape.140) | copy-start | bytes 22020100
  151.0 5.4 %copy-start.7 = (bf16[1,3584,128]{2,1,0:T(8,128)(2,1)S(1)}, bf16[1,3584,128]{2,1,0:T(8,128)(2,1)}, u32[]{:S(2)}) copy-start(bf16[1,3584,128]{2,1,0:T(8,128)(2,1)} %param.26) | copy-start | bytes 2752516
  156.4 4.6 %copy-start.8 = (s32[1,6]{1,0:T(1,128)S(1)}, s32[1,6]{1,0:T(1,128)}, u32[]{:S(2)}) copy-start(s32[1,6]{1,0:T(1,128)} %param.16) | copy-start | bytes 76
  156.4 5.5 %copy-start.2 = (bf16[6,128,576]{1,2,0:T(8,128)(2,1)S(1)}, bf16[6,128,576]{1,2,0:T(8,128)(2,1)}, u32[]{:S(2)}) copy-start(bf16[6,128,576]{1,2,0:T(8,128)(2,1)} %param.15) | copy-start | bytes 2654212
  156.4 6.9 %copy-start.3 = (bf16[3,32,576]{2,1,0:T(8,128)(2,1)S(1)}, bf16[3,32,576]{2,1,0:T(8,128)(2,1)}, u32[]{:S(2)}) copy-start(bf16[3,32,576]{2,1,0:T(8,128)(2,1)} %param.14) | copy-start | bytes 331780
  156.4 16.8 %copy-start.5 = (s32[1,1,3]{2,1,0:T(1,128)S(1)}, s32[1,1,3]{2,1,0:T(1,128)}, u32[]{:S(2)}) copy-start(s32[1,1,3]{2,1,0:T(1,128)} %param.17) | copy-start | bytes 40
  252.8 37.3 %copy-start.4 = (f32[16,2]{0,1:T(2,128)S(1)}, f32[16,2]{0,1:T(2,128)}, u32[]{:S(2)}) copy-start(f32[16,2]{0,1:T(2,128)} %param.24) | copy-start | bytes 388
  257.4 18.4 %all-to-all-start.1 = ((bf16[16,64,224]{2,1,0:T(8,128)(2,1)}), bf16[16,64,224]{2,1,0:T(8,128)(2,1)S(1)}, u32[]{:S(2)}, u32[]{:S(2)}) async-start(bf16[16,64,224]{2,1,0:T(8,128)(2,1)} %bitcast.13), calls=%async_computation.2 | async-start | bytes 1048576 | tf_op jit(solution)/shard_map/all_to_all | solution.py:110
  264.1 30.7 %reduce-scatter.7.cloned.1.call-start = ((), (), s32[]{:S(2)}) async-start(), calls=%async_computation.9 | async-start | bytes 81920
  264.9 63.8 %reduce-scatter.5.cloned.1.call-start = ((), (), s32[]{:S(2)}) async-start(), calls=%async_computation.6 | async-start | bytes 983040 | tf_op jit(solution)/shard_map/reduce_scatter | solution.py:69
  277.8 52.6 %all-to-all-start.2 = ((bf16[32,2,3584]{2,1,0:T(2,128)(2,1)}), bf16[32,2,3584]{2,1,0:T(2,128)(2,1)S(1)}, u32[]{:S(2)}, u32[]{:S(2)}) async-start(bf16[32,2,3584]{2,1,0:T(2,128)(2,1)} %reshape.144), calls=%async_computation.3 | async-start | bytes 917504 | tf_op jit(solution)/shard_map/all_to_all | solution.py:117
Sparse Core Ops, SparseCore 0:
  56.2 79.3 all-gather.5
  159.3 86.1 all-gather.3
Sparse Core Ops, SparseCore 1:
  59.5 72.9 all-reduce.1
  267.9 26.8 reduce-scatter.6
  297.8 30.9 reduce-scatter.4
where the time goes:
time: 341 us; the launch traced here: 339 us
  waiting for transfers between devices  186 us (55%)
  blocking collectives  62.4 us (18%)
  local copies, waits for them, and re-layouts  32.6 us (10%)
  starting transfers between devices  19.2 us (6%)
  between operations  17.8 us (5%)
  matrix products  15.7 us (5%)
  other arithmetic  5.67 us (2%)
    all_gather x1, waiting for transfers between devices, per_device(): piece = lax.all_gather(arrived[None], ('dp', 'tp'), axis=0, tiled=True)  77.9 us
    all_gather x1, waiting for transfers between devices, per_device(): lax.all_gather(hidden, ('dp', 'tp'), axis=3, tiled=True)  60.5 us
    all_to_all x1, blocking collectives, per_device(): lax.all_to_all(dispatched_rows, 'ep', split_axis=0, concat_axis=0, tiled=...  44.4 us
    reduce_scatter x1, waiting for transfers between devices, per_device(): lax.psum_scatter(part_acc * factor[..., None], 'tp', scatter_dimension=1,...  33.2 us
    reshape x1, local copies, waits for them, and re-layouts, per_device(): piece_rows = piece.reshape(-1, width)  15.4 us
    all_to_all x1, starting transfers between devices, per_device(): lax.all_to_all(full_rows.reshape(ranks_ep, capacity, width), 'ep', split_...  12.3 us
    all_gather x1, blocking collectives, per_device(): group_query = lax.all_gather(queries, 'tp', axis=1, tiled=True)  9.83 us
    all_to_all x1, waiting for transfers between devices, per_device(): lax.all_to_all(expert_out.reshape(group_size, slots_all, output_column_sl...  9.42 us
  transfers between devices with their start and end apart: 7, of which 5 were waited for; matrix products, arithmetic and copies ran while one was open for 11% of the time, Pallas kernels for 0%

commit v1 on v0

v1 whole, which is shorter than its diff:
```python
import jax
import jax.numpy as jnp
from jax import lax
from jax.experimental import pallas as pl
from jax.experimental.pallas import tpu as pltpu
from jax.sharding import PartitionSpec as P

KV_RANK = 512
ROPE_DIM = 64
PAGE = 128
SLOTS = 2
ROW = KV_RANK + ROPE_DIM
WIDE = 640
CAP = 2
N_TP = 4
N_DP = 4

score_scale = 0.07216878364870322
neg_fill = -1e30
f32 = jnp.float32
bf16 = jnp.bfloat16

VMEM = pl.BlockSpec(memory_space=pltpu.VMEM)
SMEM = pl.BlockSpec(memory_space=pltpu.SMEM)
ANY = pl.BlockSpec(memory_space=pl.ANY)


def params(mib):
    return pltpu.CompilerParams(vmem_limit_bytes=mib << 20)


def iota(shape, dim):
    return lax.broadcasted_iota(jnp.int32, shape, dim)


def route_slots(routes_ref):
    n = routes_ref.shape[1]
    sub, lane = iota((n, n), 0), iota((n, n), 1)
    rows = [routes_ref[k : k + 1, :].astype(f32) for k in range(2)]
    cols = [jnp.sum(jnp.where(sub == lane, r, 0.0), axis=1, keepdims=True) for r in rows]
    slot_rows, slot_cols = [], []
    for k in range(2):
        hits = jnp.where(cols[0] == rows[k], 1.0, 0.0) + jnp.where(cols[1] == rows[k], 1.0, 0.0)
        count = jnp.sum(jnp.where(sub < lane, hits, 0.0), axis=0, keepdims=True)
        slot_rows.append(rows[k] * CAP + count)
        hits = jnp.where(rows[0] == cols[k], 1.0, 0.0) + jnp.where(rows[1] == cols[k], 1.0, 0.0)
        count = jnp.sum(jnp.where(lane < sub, hits, 0.0), axis=1, keepdims=True)
        slot_cols.append(cols[k] * CAP + count)
    return slot_rows, slot_cols


def dispatch_kernel(routes_ref, tok_ref, out_ref):
    slot_rows, _ = route_slots(routes_ref)
    rows, quarter = out_ref.shape
    n = tok_ref.shape[0]
    place = iota((rows, n), 0)
    total = jnp.zeros((rows, quarter), f32)
    for q in range(4):
        t0 = slot_rows[0].astype(jnp.int32) * 4 + q
        t1 = slot_rows[1].astype(jnp.int32) * 4 + q
        pick = jnp.where((place == t0) | (place == t1), 1.0, 0.0).astype(bf16)
        total += jnp.dot(
            pick, tok_ref[:, q * quarter : (q + 1) * quarter], preferred_element_type=f32
        )
    out_ref[...] = total.astype(bf16)


def hidden_kernel(
    where_ref, b0, b1, b2, b3, w0, w1, w2, w3, out_ref, rows_ref, weights, sems
):
    rank_dp, rank_tp = where_ref[0], where_ref[1]
    depth, part = w0.shape[0] // 2, w0.shape[1]
    copies = []
    for rel, w in enumerate((w0, w1, w2, w3)):
        slot = rank_dp ^ rel
        for half in range(2):
            copy = pltpu.make_async_copy(
                w.at[pl.ds(half * depth, depth), :],
                weights.at[slot, :, pl.ds(half * part, part)],
                sems.at[rel, half],
            )
            copy.start()
            copies.append(copy)
    count, quarter = b0.shape
    slots = count // 4
    for k, b in enumerate((b0, b1, b2, b3)):
        base = pl.multiple_of(((rank_tp + N_TP - k) % N_TP) * slots, slots)
        block = b[...]
        for q in range(4):
            pick = jnp.where(
                iota((slots, count), 1) == iota((slots, count), 0) * 4 + q, 1.0, 0.0
            ).astype(bf16)
            rows_ref[pl.ds(base, slots), q * quarter : (q + 1) * quarter] = jnp.dot(
                pick, block, preferred_element_type=f32
            ).astype(bf16)
    for copy in copies:
        copy.wait()
    for i in range(N_DP):
        both = jnp.dot(rows_ref[...], weights[i], preferred_element_type=f32)
        gate, up = both[:, :part], both[:, part:]
        hidden = gate / (1.0 + jnp.exp(-gate)) * up
        out_ref[:, i * part : (i + 1) * part] = hidden.astype(bf16)


def down_kernel(where_ref, h0, h1, h2, h3, d0, d1, d2, d3, out_ref, hidden, weights, sems):
    rank_dp, rank_tp = where_ref[0], where_ref[1]
    cols = d0.shape[0]
    part = h0.shape[1] // N_DP
    copies = []
    for rel, d in enumerate((d0, d1, d2, d3)):
        base = pl.multiple_of((rank_dp ^ rel) * cols, 16)
        copy = pltpu.make_async_copy(d, weights.at[pl.ds(base, cols), :], sems.at[rel])
        copy.start()
        copies.append(copy)
    for k, h in enumerate((h0, h1, h2, h3)):
        source = (rank_tp + N_TP - k) % N_TP
        for i in range(N_DP):
            base = pl.multiple_of((i * N_TP + source) * part, part)
            hidden[:, pl.ds(base, part)] = h[:, i * part : (i + 1) * part]
    for copy in copies:
        copy.wait()
    out_ref[...] = lax.dot_general(
        hidden[...], weights[...], (((1,), (1,)), ((), ())), preferred_element_type=f32
    ).astype(bf16)


def combine_kernel(routes_ref, gates_ref, back_ref, out_ref):
    _, slot_cols = route_slots(routes_ref)
    n = out_ref.shape[0]
    slots = back_ref.shape[0] // N_TP
    part = back_ref.shape[1] // N_DP
    eye = iota((n, n), 0) == iota((n, n), 1)
    lane = iota((n, slots), 1)
    picks, gates = [], []
    for k in range(2):
        picks.append(
            jnp.where(lane == slot_cols[k].astype(jnp.int32), 1.0, 0.0).astype(bf16)
        )
        gates.append(
            jnp.sum(jnp.where(eye, gates_ref[k : k + 1, :], 0.0), axis=1, keepdims=True)
        )
    pieces = [None] * (N_TP * N_DP)
    for t in range(N_TP):
        block = back_ref[t * slots : (t + 1) * slots, :]
        mixed = gates[0] * jnp.dot(picks[0], block, preferred_element_type=f32) + gates[
            1
        ] * jnp.dot(picks[1], block, preferred_element_type=f32)
        for i in range(N_DP):
            pieces[i * N_TP + t] = mixed[:, i * part : (i + 1) * part]
    out_ref[...] = jnp.concatenate(pieces, axis=1).astype(bf16)


def split3(x):
    hi = x.astype(bf16)
    rest = x - hi.astype(f32)
    mid = rest.astype(bf16)
    low = (rest - mid.astype(f32)).astype(bf16)
    return hi, mid, low


def attend_kernel(
    where_ref, tables_ref, lengths_ref, q0, q1, q2, q3, cache, mig, o0, o1, o2, o3
):
    rank_tp = where_ref[1]
    heads = q0.shape[0] // 4
    for s in range(4):
        query = jnp.concatenate(
            [q[s * heads : (s + 1) * heads, :] for q in (q0, q1, q2, q3)], axis=0
        )
        total_heads = query.shape[0]
        if s < 3:
            length = lengths_ref[s].astype(f32)
        else:
            length = query[:, ROW : ROW + 1].astype(f32) * 256.0 + query[
                :, ROW + 1 : ROW + 2
            ].astype(f32)
        query = query[:, :ROW]
        keys, scores, valid = [], [], []
        for j in range(SLOTS):
            keys.append(cache[tables_ref[s * SLOTS + j]] if s < 3 else mig[j])
            score = jnp.dot(query, keys[j], preferred_element_type=f32) * score_scale
            place = ((j * N_TP + rank_tp) * PAGE + iota(score.shape, 1)).astype(f32)
            valid.append(place < length)
            scores.append(jnp.where(valid[j], score, neg_fill))
        top = jnp.max(jnp.maximum(scores[0], scores[1]), axis=1, keepdims=True)
        total = jnp.zeros((total_heads, 1), f32)
        acc = jnp.zeros((total_heads, KV_RANK), f32)
        for j in range(SLOTS):
            weight = jnp.where(valid[j], jnp.exp(scores[j] - top), 0.0).astype(bf16)
            total += jnp.sum(weight.astype(f32), axis=1, keepdims=True)
            acc += lax.dot_general(
                weight, keys[j][:KV_RANK, :], (((1,), (1,)), ((), ())), preferred_element_type=f32
            )
        some = total > 0.0
        safe = jnp.where(some, total, 1.0)
        mean = (acc / safe).astype(bf16)
        level = jnp.where(some, top + jnp.log(safe), neg_fill)
        hi, mid, low = split3(level)
        lane = iota((total_heads, WIDE - KV_RANK), 1)
        tail = jnp.where(
            lane == 0,
            hi.astype(f32),
            jnp.where(lane == 1, mid.astype(f32), jnp.where(lane == 2, low.astype(f32), 0.0)),
        ).astype(bf16)
        for k, o in enumerate((o0, o1, o2, o3)):
            o[s * heads : (s + 1) * heads, :KV_RANK] = mean[k * heads : (k + 1) * heads]
            o[s * heads : (s + 1) * heads, KV_RANK:] = tail[k * heads : (k + 1) * heads]


def merge_kernel(p0, p1, p2, p3, out_ref):
    levels = []
    for p in (p0, p1, p2, p3):
        tail = p[:, KV_RANK:].astype(f32)
        levels.append(tail[:, 0:1] + tail[:, 1:2] + tail[:, 2:3])
    most = jnp.maximum(jnp.maximum(levels[0], levels[1]), jnp.maximum(levels[2], levels[3]))
    numerator = jnp.zeros(out_ref.shape, f32)
    denominator = jnp.zeros((out_ref.shape[0], 1), f32)
    for p, level in zip((p0, p1, p2, p3), levels):
        factor = jnp.exp(level - most)
        denominator += factor
        numerator += factor * p[:, :KV_RANK].astype(f32)
    out_ref[...] = (numerator / denominator).astype(bf16)


def shift(x, k):
    return lax.ppermute(x, "tp", [(i, (i + k) % N_TP) for i in range(N_TP)])


def swap(x, bit):
    return lax.ppermute(x, "dp", [(i, i ^ bit) for i in range(N_DP)])


def per_device(
    queries,
    cache,
    tables,
    lengths,
    mig_cache,
    mig_src,
    mig_dst,
    mig_seq,
    tokens,
    routes,
    gates,
    gate_w,
    up_w,
    down_w,
):
    rank_tp = lax.axis_index("tp")
    rank_dp = lax.axis_index("dp")
    where = jnp.stack([rank_dp, rank_tp]).astype(jnp.int32)
    ranks_ep = lax.axis_size("ep")
    token_rows, width = tokens.shape
    slots_all = ranks_ep * CAP
    quarter = width // 4
    routes_t = routes.T
    gates_t = gates.T

    sent = pl.pallas_call(
        dispatch_kernel,
        out_shape=jax.ShapeDtypeStruct((slots_all * 4, quarter), bf16),
        in_specs=[VMEM] * 2,
        out_specs=VMEM,
        compiler_params=params(24),
    )(routes_t, tokens)
    arrived = lax.all_to_all(
        sent.reshape(ranks_ep, CAP * 4, quarter), "ep", split_axis=0, concat_axis=0, tiled=True
    ).reshape(slots_all * 4, quarter)

    first = jnp.concatenate([gate_w[0], up_w[0]], axis=0)
    first_x = swap(first, 2)
    first_c = swap(first, 1)
    first_xc = swap(first_x, 1)
    second = down_w[0].T
    second_c = swap(second, 1)

    heads = queries.shape[1]
    at_dst = rank_dp == mig_dst[0]
    picked = lax.dynamic_index_in_dim(queries, mig_seq[0], 0, keepdims=False)
    picked_len = lax.dynamic_index_in_dim(lengths[0, 0], mig_seq[0], 0, keepdims=False)
    lane = jnp.arange(WIDE - ROW)[None, :]
    tail = jnp.where(
        lane == 0, picked_len // 256, jnp.where(lane == 1, picked_len % 256, 0)
    ).astype(bf16)
    moving = jnp.concatenate([picked, jnp.broadcast_to(tail, (heads, WIDE - ROW))], axis=1)
    moving = jnp.where(at_dst, moving, jnp.zeros_like(moving))
    moving = moving + swap(moving, 1)
    moving = moving + swap(moving, 2)
    own = jnp.pad(queries.reshape(3 * heads, ROW), ((0, 0), (0, WIDE - ROW)))
    asked = jnp.concatenate([own, moving], axis=0)
    asks = [asked] + [shift(asked, k) for k in (1, 2, 3)]
    parts = pl.pallas_call(
        attend_kernel,
        out_shape=[jax.ShapeDtypeStruct((4 * heads, WIDE), bf16)] * 4,
        in_specs=[SMEM] * 3 + [VMEM] * 6,
        out_specs=[VMEM] * 4,
        compiler_params=params(32),
    )(
        where,
        tables.reshape(-1),
        lengths.reshape(-1),
        *asks,
        jnp.swapaxes(cache, 1, 2),
        jnp.swapaxes(mig_cache, 1, 2),
    )
    merged = pl.pallas_call(
        merge_kernel,
        out_shape=jax.ShapeDtypeStruct((4 * heads, KV_RANK), bf16),
        in_specs=[VMEM] * 4,
        out_specs=VMEM,
        compiler_params=params(16),
    )(parts[0], *[shift(parts[k], -k) for k in (1, 2, 3)])
    back = merged[3 * heads :]
    back = jnp.where(rank_dp == mig_src[0], back, jnp.zeros_like(back))
    back = back + swap(back, 1)
    back = back + swap(back, 2)
    chosen = at_dst & (jnp.arange(3) == mig_seq[0])
    attn_out = jnp.where(
        chosen[:, None, None], back[None], merged[: 3 * heads].reshape(3, heads, KV_RANK)
    )

    arrived, second_late = lax.optimization_barrier((arrived, second))
    second_x = swap(second_late, 2)
    second_xc = swap(second_x, 1)
    blocks = [arrived] + [shift(arrived, k) for k in (1, 2, 3)]
    part = gate_w.shape[2]
    rows = N_TP * slots_all
    hidden = pl.pallas_call(
        hidden_kernel,
        out_shape=jax.ShapeDtypeStruct((rows, N_DP * part), bf16),
        in_specs=[SMEM] + [VMEM] * 4 + [ANY] * 4,
        out_specs=VMEM,
        scratch_shapes=[
            pltpu.VMEM((rows, width), bf16),
            pltpu.VMEM((N_DP, width, 2 * part), bf16),
            pltpu.SemaphoreType.DMA((N_DP, 2)),
        ],
        compiler_params=params(40),
    )(where, *blocks, first, first_c, first_x, first_xc)
    hiddens = [hidden] + [shift(hidden, k) for k in (1, 2, 3)]
    cols = second.shape[0]
    expert_out = pl.pallas_call(
        down_kernel,
        out_shape=jax.ShapeDtypeStruct((rows, N_DP * cols), bf16),
        in_specs=[SMEM] + [VMEM] * 4 + [ANY] * 4,
        out_specs=VMEM,
        scratch_shapes=[
            pltpu.VMEM((rows, second.shape[1]), bf16),
            pltpu.VMEM((N_DP * cols, second.shape[1]), bf16),
            pltpu.SemaphoreType.DMA((N_DP,)),
        ],
        compiler_params=params(32),
    )(where, *hiddens, second, second_c, second_x, second_xc)
    returned = lax.all_to_all(
        expert_out.reshape(N_TP * ranks_ep, CAP, N_DP * cols),
        ("tp", "ep"),
        split_axis=0,
        concat_axis=0,
        tiled=True,
    ).reshape(rows, N_DP * cols)
    moe_out = pl.pallas_call(
        combine_kernel,
        out_shape=jax.ShapeDtypeStruct((token_rows, width), bf16),
        in_specs=[VMEM] * 3,
        out_specs=VMEM,
        compiler_params=params(16),
    )(routes_t, gates_t, returned)
    return (attn_out, moe_out)


def solution(mesh):
    in_specs = (
        P(("dp", "ep"), "tp", None),
        P(("dp", "tp", "ep"), None, None),
        P(("dp", "tp", "ep"), None),
        P("dp", "ep", None),
        P(("dp", "tp", "ep"), None, None),
        P("ep"),
        P("ep"),
        P("ep"),
        P(("dp", "tp", "ep"), None),
        P(("dp", "tp", "ep"), None),
        P(("dp", "tp", "ep"), None),
        P("ep", None, ("dp", "tp")),
        P("ep", None, ("dp", "tp")),
        P("ep", None, ("dp", "tp")),
    )
    out_specs = (P(("dp", "ep"), "tp", None), P(("dp", "tp", "ep"), None))
    return jax.shard_map(
        per_device, mesh=mesh, in_specs=in_specs, out_specs=out_specs, check_vma=False
    )
```

time: 341 us -> 222 us (0.65)
  waiting for transfers between devices: 186 us -> 73.8 us
  starting transfers between devices: 19.2 us -> 118 us
  blocking collectives: 62.4 us -> 0 us
  local copies, waits for them, and re-layouts: 32.6 us -> 4.49 us
  Pallas kernels: 0 us -> 16.3 us
  matrix products: 15.7 us -> 0 us
  between operations: 17.8 us -> 5.8 us
    all_gather x2 -> x0, waiting for transfers between devices: 138 us -> none  [the longest x1 77.9 us: per_device(): piece = lax.all_gather(arrived[None], ('dp', 'tp'), axis=0, tiled=True)]
    ppermute x0 -> x22, starting transfers between devices: none -> 81.8 us  [the longest x12 41.3 us: shift(): return lax.ppermute(x, 'tp', [(i, (i + k) % N_TP) for i in range(N_TP)])]
    ppermute x0 -> x22, waiting for transfers between devices: none -> 73.8 us  [the longest x10 41.5 us: swap(): return lax.ppermute(x, 'dp', [(i, i ^ bit) for i in range(N_DP)])]
    all_to_all x1 -> x0, blocking collectives: 44.4 us -> none  [per_device(): lax.all_to_all(dispatched_rows, 'ep', split_axis=0, concat_axis=0, tiled=...]
    reduce_scatter x1 -> x0, waiting for transfers between devices: 33.2 us -> none  [per_device(): lax.psum_scatter(part_acc * factor[..., None], 'tp', scatter_dimension=1,...]
    reshape x6 -> x2, local copies, waits for them, and re-layouts: 24.8 us -> 1.11 us  [the longest x1 0.94 us: per_device(): expert_out.reshape(N_TP * ranks_ep, CAP, N_DP * cols)]
    all_to_all x2, starting transfers between devices: 19 us -> 36.5 us  [the longest x1 21.3 us: per_device(): lax.all_to_all(expert_out.reshape(N_TP * ranks_ep, CAP, N_DP * cols), ('t...]
    pallas_call x0 -> x6, Pallas kernels: none -> 16.3 us  [the longest x1 6.94 us: per_device(): pl.pallas_call(hidden_kernel, out_shape=jax.ShapeDtypeStruct((rows, N_DP...]
  transfers between devices with their start and end apart: 7 -> 24, of which waited for: 5 -> 14; matrix products, arithmetic and copies ran while one was open for 11% -> 1% of each run, Pallas kernels for 0% -> 5%
where the time goes in v1:
time: 222 us; the launch traced here: 221 us
  starting transfers between devices  118 us (53%)
  waiting for transfers between devices  73.8 us (33%)
  Pallas kernels  16.3 us (7%)
  between operations  5.8 us (3%)
  local copies, waits for them, and re-layouts  4.49 us (2%)
  other arithmetic  2.57 us (1%)
    ppermute x10, waiting for transfers between devices, swap(): return lax.ppermute(x, 'dp', [(i, i ^ bit) for i in range(N_DP)])  41.5 us
    ppermute x12, starting transfers between devices, shift(): return lax.ppermute(x, 'tp', [(i, (i + k) % N_TP) for i in range(N_TP)])  41.3 us
    ppermute x10, starting transfers between devices, swap(): return lax.ppermute(x, 'dp', [(i, i ^ bit) for i in range(N_DP)])  40.5 us
    ppermute x12, waiting for transfers between devices, shift(): return lax.ppermute(x, 'tp', [(i, (i + k) % N_TP) for i in range(N_TP)])  32.3 us
    all_to_all x1, starting transfers between devices, per_device(): lax.all_to_all(expert_out.reshape(N_TP * ranks_ep, CAP, N_DP * cols), ('t...  21.3 us
    all_to_all x1, starting transfers between devices, per_device(): lax.all_to_all(sent.reshape(ranks_ep, CAP * 4, quarter), 'ep', split_axis...  15.2 us
    pallas_call x1, Pallas kernels, per_device(): pl.pallas_call(hidden_kernel, out_shape=jax.ShapeDtypeStruct((rows, N_DP...  6.94 us
  transfers between devices with their start and end apart: 24, of which 14 were waited for; matrix products, arithmetic and copies ran while one was open for 1% of the time, Pallas kernels for 5%

profile of v1, /device:TPU:1, one launch (start us, length us, event | category | flops | bytes accessed | tf_op | source)
XLA Modules:
  0.0 221.2 jit_solution(2950760748011749094)
XLA Ops:
  2.3 5.5 %collective-permute-start.14 = (bf16[7168,128]{1,0:T(8,128)(2,1)S(1)}, bf16[7168,128]{1,0:T(8,128)(2,1)}, u32[]{:S(2)}, u32[]{:S(2)}) collective-permute-start(bf16[7168,128]{1,0:T(8,128)(2,1)S(1)} %pad_maximum_fusion.w0), channel_id=1, source_target_pairs={{0,256},{128,384},{256,0},{384,128},{1,257},{129,385},{257,1},{385... | collective-permute-start | bytes 5505032 | tf_op jit(solution)/shard_map/ppermute | solution.py:230
  9.3 15.2 %all-to-all-start = ((bf16[32,8,896]{2,1,0:T(8,128)(2,1)}), bf16[32,8,896]{2,1,0:T(8,128)(2,1)S(1)}, u32[]{:S(2)}, u32[]{:S(2)}) async-start(bf16[32,8,896]{2,1,0:T(8,128)(2,1)} %bitcast.15), calls=%async_computation | async-start | bytes 917504 | tf_op jit(solution)/shard_map/all_to_all | solution.py:266
  24.6 3.1 %collective-permute-start.13 = (bf16[7168,128]{1,0:T(8,128)(2,1)S(1)}, bf16[7168,128]{1,0:T(8,128)(2,1)}, u32[]{:S(2)}, u32[]{:S(2)}) collective-permute-start(bf16[7168,128]{1,0:T(8,128)(2,1)S(1)} %pad_maximum_fusion.w0), channel_id=1, source_target_pairs={{0,128},{128,0},{256,384},{384,256},{1,129},{129,1},{257,385},{385... | collective-permute-start | bytes 5505032 | tf_op jit(solution)/shard_map/ppermute | solution.py:230
  27.7 20.6 %collective-permute-done.14.w2 = bf16[7168,128]{1,0:T(8,128)(2,1)} collective-permute-done((bf16[7168,128]{1,0:T(8,128)(2,1)S(1)}, bf16[7168,128]{1,0:T(8,128)(2,1)}, u32[]{:S(2)}, u32[]{:S(2)}) %collective-permute-start.14) | collective-permute-done | bytes 1835040 | tf_op jit(solution)/shard_map/ppermute | solution.py:230
  48.4 7.0 %collective-permute-start.15 = (bf16[7168,128]{1,0:T(8,128)(2,1)}, bf16[7168,128]{1,0:T(8,128)(2,1)}, u32[]{:S(2)}, u32[]{:S(2)}) collective-permute-start(bf16[7168,128]{1,0:T(8,128)(2,1)} %collective-permute-done.14.w2), channel_id=1, source_target_pairs={{0,128},{128,0},{256,384},{384,256},{1,129},{129,1},{257,385},{385... | collective-permute-start | bytes 5505032 | tf_op jit(solution)/shard_map/ppermute | solution.py:230
  55.4 4.9 %collective-permute-start.20 = (bf16[224,2048]{1,0:T(8,128)(2,1)S(1)}, bf16[224,2048]{1,0:T(8,128)(2,1)}, u32[]{:S(2)}, u32[]{:S(2)}) collective-permute-start(bf16[224,2048]{1,0:T(8,128)(2,1)S(1)} %bitcast.33), channel_id=1, source_target_pairs={{0,256},{128,384},{256,0},{384,128},{1,257},{129,385},{257,1},{385... | collective-permute-start | bytes 2752520 | tf_op jit(solution)/shard_map/ppermute | solution.py:230
  60.3 3.2 %collective-permute-start.10 = (bf16[256,896]{1,0:T(8,128)(2,1)S(1)}, bf16[256,896]{1,0:T(8,128)(2,1)S(1)}, u32[]{:S(2)}, u32[]{:S(2)}) collective-permute-start(bf16[256,896]{1,0:T(8,128)(2,1)S(1)} %bitcast.29), channel_id=1, source_target_pairs={{0,32},{32,64},{64,96},{96,0},{1,33},{33,65},{65,97},{97,1},{2,34}... | collective-permute-start | bytes 1376264 | tf_op jit(solution)/shard_map/ppermute | solution.py:226
  66.0 14.9 %collective-permute-done.20.d2 = bf16[224,2048]{1,0:T(8,128)(2,1)} collective-permute-done((bf16[224,2048]{1,0:T(8,128)(2,1)S(1)}, bf16[224,2048]{1,0:T(8,128)(2,1)}, u32[]{:S(2)}, u32[]{:S(2)}) %collective-permute-start.20) | collective-permute-done | bytes 917536 | tf_op jit(solution)/shard_map/ppermute | solution.py:230
  83.6 5.0 %collective-permute-start.11 = (bf16[256,896]{1,0:T(8,128)(2,1)S(1)}, bf16[256,896]{1,0:T(8,128)(2,1)}, u32[]{:S(2)}, u32[]{:S(2)}) collective-permute-start(bf16[256,896]{1,0:T(8,128)(2,1)S(1)} %bitcast.30), channel_id=1, source_target_pairs={{0,64},{32,96},{64,0},{96,32},{1,65},{33,97},{65,1},{97,33},{2,66}... | collective-permute-start | bytes 1376264 | tf_op jit(solution)/shard_map/ppermute | solution.py:226
  92.2 7.3 %collective-permute-done.11.b2 = bf16[256,896]{1,0:T(8,128)(2,1)} collective-permute-done((bf16[256,896]{1,0:T(8,128)(2,1)S(1)}, bf16[256,896]{1,0:T(8,128)(2,1)}, u32[]{:S(2)}, u32[]{:S(2)}) %collective-permute-start.11) | collective-permute-done | bytes 458784 | tf_op jit(solution)/shard_map/ppermute | solution.py:226
  99.5 10.2 %collective-permute-done.12.b3 = bf16[256,896]{1,0:T(8,128)(2,1)} collective-permute-done((bf16[256,896]{1,0:T(8,128)(2,1)S(1)}, bf16[256,896]{1,0:T(8,128)(2,1)}, u32[]{:S(2)}, u32[]{:S(2)}) %collective-permute-start.12) | collective-permute-done | bytes 458784 | tf_op jit(solution)/shard_map/ppermute | solution.py:226
  110.7 6.9 %shard_map.152.h0 = bf16[256,512]{1,0:T(8,128)(2,1)S(1)} custom-call(s32[2]{0:T(128)S(1)} %pad_add_fusion.where_ref, bf16[256,896]{1,0:T(8,128)(2,1)S(1)} %bitcast.32, bf16[256,896]{1,0:T(8,128)(2,1)S(1)} %copy-done.3, bf16[256,896]{1,0:T(8,128)(2,1)} %collective-permute-done.11.b2, bf16[256,896]{1,0:T(8,128)(2,1)} %collective-permute-done.12.b3, ...), custom_call_target="tpu_custom_call" | custom-call | tf_op jit(solution)/shard_map/pallas_call | solution.py:328
  117.6 3.2 %collective-permute-start.16 = (bf16[256,512]{1,0:T(8,128)(2,1)S(1)}, bf16[256,512]{1,0:T(8,128)(2,1)S(1)}, u32[]{:S(2)}, u32[]{:S(2)}) collective-permute-start(bf16[256,512]{1,0:T(8,128)(2,1)S(1)} %shard_map.152.h0), channel_id=1, source_target_pairs={{0,32},{32,64},{64,96},{96,0},{1,33},{33,65},{65,97},{97,1},{2,34}... | collective-permute-start | bytes 786440 | tf_op jit(solution)/shard_map/ppermute | solution.py:226
  120.8 4.5 %collective-permute-start.17 = (bf16[256,512]{1,0:T(8,128)(2,1)S(1)}, bf16[256,512]{1,0:T(8,128)(2,1)S(1)}, u32[]{:S(2)}, u32[]{:S(2)}) collective-permute-start(bf16[256,512]{1,0:T(8,128)(2,1)S(1)} %shard_map.152.h0), channel_id=1, source_target_pairs={{0,64},{32,96},{64,0},{96,32},{1,65},{33,97},{65,1},{97,33},{2,66}... | collective-permute-start | bytes 786440 | tf_op jit(solution)/shard_map/ppermute | solution.py:226
  136.0 4.1 %shard_map.153 = bf16[256,896]{1,0:T(8,128)(2,1)S(1)} custom-call(s32[2]{0:T(128)S(1)} %pad_add_fusion.where_ref, bf16[256,512]{1,0:T(8,128)(2,1)S(1)} %shard_map.152.h0, bf16[256,512]{1,0:T(8,128)(2,1)S(1)} %collective-permute-done.16.h1, bf16[256,512]{1,0:T(8,128)(2,1)S(1)} %collective-permute-done.17.h2, bf16[256,512]{1,0:T(8,128)(2,1)S(1)} %collective-permute-done.18.h3, ...), custom_call_target="tpu_custom_call" | custom-call | tf_op jit(solution)/shard_map/pallas_call | solution.py:342
  141.1 21.3 %all-to-all-start.1 = ((bf16[128,2,896]{2,1,0:T(2,128)(2,1)}), bf16[128,2,896]{2,1,0:T(2,128)(2,1)S(1)}, u32[]{:S(2)}, u32[]{:S(2)}) async-start(bf16[128,2,896]{2,1,0:T(2,128)(2,1)} %reshape.57), calls=%async_computation.1 | async-start | bytes 917504 | tf_op jit(solution)/shard_map/all_to_all | solution.py:354
  166.7 4.4 %collective-permute-start.1 = (bf16[32,640]{1,0:T(8,128)(2,1)S(1)}, bf16[32,640]{1,0:T(8,128)(2,1)S(1)}, u32[]{:S(2)}, u32[]{:S(2)}) collective-permute-start(bf16[32,640]{1,0:T(8,128)(2,1)S(1)} %fusion.4), channel_id=1, source_target_pairs={{0,256},{128,384},{256,0},{384,128},{1,257},{129,385},{257,1},{385... | collective-permute-start | bytes 122888 | tf_op jit(solution)/shard_map/ppermute | solution.py:230
  176.2 4.7 %collective-permute-start.3 = (bf16[128,640]{1,0:T(8,128)(2,1)S(1)}, bf16[128,640]{1,0:T(8,128)(2,1)S(1)}, u32[]{:S(2)}, u32[]{:S(2)}) collective-permute-start(bf16[128,640]{1,0:T(8,128)(2,1)S(1)} %fusion.1.q0), channel_id=1, source_target_pairs={{0,64},{32,96},{64,0},{96,32},{1,65},{33,97},{65,1},{97,33},{2,66}... | collective-permute-start | bytes 491528 | tf_op jit(solution)/shard_map/ppermute | solution.py:226
  183.9 4.0 %collective-permute-done.3.q2 = bf16[128,640]{1,0:T(8,128)(2,1)S(1)} collective-permute-done((bf16[128,640]{1,0:T(8,128)(2,1)S(1)}, bf16[128,640]{1,0:T(8,128)(2,1)S(1)}, u32[]{:S(2)}, u32[]{:S(2)}) %collective-permute-start.3) | collective-permute-done | bytes 163872 | tf_op jit(solution)/shard_map/ppermute | solution.py:226
  190.6 4.4 %collective-permute-start.5 = (bf16[128,640]{1,0:T(8,128)(2,1)S(1)}, bf16[128,640]{1,0:T(8,128)(2,1)S(1)}, u32[]{:S(2)}, u32[]{:S(2)}) collective-permute-start(bf16[128,640]{1,0:T(8,128)(2,1)S(1)} %get-tuple-element.9), channel_id=1, source_target_pairs={{0,96},{32,0},{64,32},{96,64},{1,97},{33,1},{65,33},{97,65},{2,98}... | collective-permute-start | bytes 491528 | tf_op jit(solution)/shard_map/ppermute | solution.py:226
  195.0 4.2 %collective-permute-start.6 = (bf16[128,640]{1,0:T(8,128)(2,1)S(1)}, bf16[128,640]{1,0:T(8,128)(2,1)S(1)}, u32[]{:S(2)}, u32[]{:S(2)}) collective-permute-start(bf16[128,640]{1,0:T(8,128)(2,1)S(1)} %get-tuple-element.10), channel_id=1, source_target_pairs={{0,64},{32,96},{64,0},{96,32},{1,65},{33,97},{65,1},{97,33},{2,66}... | collective-permute-start | bytes 491528 | tf_op jit(solution)/shard_map/ppermute | solution.py:226
  202.5 5.8 %collective-permute-done.7.p3 = bf16[128,640]{1,0:T(8,128)(2,1)S(1)} collective-permute-done((bf16[128,640]{1,0:T(8,128)(2,1)S(1)}, bf16[128,640]{1,0:T(8,128)(2,1)S(1)}, u32[]{:S(2)}, u32[]{:S(2)}) %collective-permute-start.7) | collective-permute-done | bytes 163872 | tf_op jit(solution)/shard_map/ppermute | solution.py:226
  208.7 3.4 %collective-permute-start.8 = (bf16[32,512]{1,0:T(8,128)(2,1)S(1)}, bf16[32,512]{1,0:T(8,128)(2,1)S(1)}, u32[]{:S(2)}, u32[]{:S(2)}) collective-permute-start(bf16[32,512]{1,0:T(8,128)(2,1)S(1)} %slice_select_fusion), channel_id=1, source_target_pairs={{0,128},{128,0},{256,384},{384,256},{1,129},{129,1},{257,385},{385... | collective-permute-start | bytes 98312 | tf_op jit(solution)/shard_map/ppermute | solution.py:230
  213.0 4.3 %collective-permute-start.9 = (bf16[32,512]{1,0:T(8,128)(2,1)S(1)}, bf16[32,512]{1,0:T(8,128)(2,1)S(1)}, u32[]{:S(2)}, u32[]{:S(2)}) collective-permute-start(bf16[32,512]{1,0:T(8,128)(2,1)S(1)} %fusion.3), channel_id=1, source_target_pairs={{0,256},{128,384},{256,0},{384,128},{1,257},{129,385},{257,1},{385... | collective-permute-start | bytes 98312 | tf_op jit(solution)/shard_map/ppermute | solution.py:230
  (70 shorter events, 43.2 us)
Async XLA Ops:
  2.3 46.0 %collective-permute-start.14 = (bf16[7168,128]{1,0:T(8,128)(2,1)S(1)}, bf16[7168,128]{1,0:T(8,128)(2,1)}, u32[]{:S(2)}, u32[]{:S(2)}) collective-permute-start(bf16[7168,128]{1,0:T(8,128)(2,1)S(1)} %pad_maximum_fusion.w0), channel_id=1, source_target_pairs={{0,256},{128,384},{256,0},{384,128},{1,257},{129,385},{257,1},{385... | collective-permute-start | bytes 5505032 | tf_op jit(solution)/shard_map/ppermute | solution.py:230
  9.3 46.1 %all-to-all-start = ((bf16[32,8,896]{2,1,0:T(8,128)(2,1)}), bf16[32,8,896]{2,1,0:T(8,128)(2,1)S(1)}, u32[]{:S(2)}, u32[]{:S(2)}) async-start(bf16[32,8,896]{2,1,0:T(8,128)(2,1)} %bitcast.15), calls=%async_computation | async-start | bytes 917504 | tf_op jit(solution)/shard_map/all_to_all | solution.py:266
  24.6 59.0 %collective-permute-start.13 = (bf16[7168,128]{1,0:T(8,128)(2,1)S(1)}, bf16[7168,128]{1,0:T(8,128)(2,1)}, u32[]{:S(2)}, u32[]{:S(2)}) collective-permute-start(bf16[7168,128]{1,0:T(8,128)(2,1)S(1)} %pad_maximum_fusion.w0), channel_id=1, source_target_pairs={{0,128},{128,0},{256,384},{384,256},{1,129},{129,1},{257,385},{385... | collective-permute-start | bytes 5505032 | tf_op jit(solution)/shard_map/ppermute | solution.py:230
  48.4 61.3 %collective-permute-start.15 = (bf16[7168,128]{1,0:T(8,128)(2,1)}, bf16[7168,128]{1,0:T(8,128)(2,1)}, u32[]{:S(2)}, u32[]{:S(2)}) collective-permute-start(bf16[7168,128]{1,0:T(8,128)(2,1)} %collective-permute-done.14.w2), channel_id=1, source_target_pairs={{0,128},{128,0},{256,384},{384,256},{1,129},{129,1},{257,385},{385... | collective-permute-start | bytes 5505032 | tf_op jit(solution)/shard_map/ppermute | solution.py:230
  55.4 25.5 %collective-permute-start.20 = (bf16[224,2048]{1,0:T(8,128)(2,1)S(1)}, bf16[224,2048]{1,0:T(8,128)(2,1)}, u32[]{:S(2)}, u32[]{:S(2)}) collective-permute-start(bf16[224,2048]{1,0:T(8,128)(2,1)S(1)} %bitcast.33), channel_id=1, source_target_pairs={{0,256},{128,384},{256,0},{384,128},{1,257},{129,385},{257,1},{385... | collective-permute-start | bytes 2752520 | tf_op jit(solution)/shard_map/ppermute | solution.py:230
  60.3 28.3 %collective-permute-start.10 = (bf16[256,896]{1,0:T(8,128)(2,1)S(1)}, bf16[256,896]{1,0:T(8,128)(2,1)S(1)}, u32[]{:S(2)}, u32[]{:S(2)}) collective-permute-start(bf16[256,896]{1,0:T(8,128)(2,1)S(1)} %bitcast.29), channel_id=1, source_target_pairs={{0,32},{32,64},{64,96},{96,0},{1,33},{33,65},{65,97},{97,1},{2,34}... | collective-permute-start | bytes 1376264 | tf_op jit(solution)/shard_map/ppermute | solution.py:226
  63.5 68.6 %collective-permute-start.19 = (bf16[224,2048]{1,0:T(8,128)(2,1)S(1)}, bf16[224,2048]{1,0:T(8,128)(2,1)}, u32[]{:S(2)}, u32[]{:S(2)}) collective-permute-start(bf16[224,2048]{1,0:T(8,128)(2,1)S(1)} %bitcast.34), channel_id=1, source_target_pairs={{0,128},{128,0},{256,384},{384,256},{1,129},{129,1},{257,385},{385... | collective-permute-start | bytes 2752520 | tf_op jit(solution)/shard_map/ppermute | solution.py:230
  81.0 51.2 %collective-permute-start.21 = (bf16[224,2048]{1,0:T(8,128)(2,1)}, bf16[224,2048]{1,0:T(8,128)(2,1)}, u32[]{:S(2)}, u32[]{:S(2)}) collective-permute-start(bf16[224,2048]{1,0:T(8,128)(2,1)} %collective-permute-done.20.d2), channel_id=1, source_target_pairs={{0,128},{128,0},{256,384},{384,256},{1,129},{129,1},{257,385},{385... | collective-permute-start | bytes 2752520 | tf_op jit(solution)/shard_map/ppermute | solution.py:230
  83.6 15.8 %collective-permute-start.11 = (bf16[256,896]{1,0:T(8,128)(2,1)S(1)}, bf16[256,896]{1,0:T(8,128)(2,1)}, u32[]{:S(2)}, u32[]{:S(2)}) collective-permute-start(bf16[256,896]{1,0:T(8,128)(2,1)S(1)} %bitcast.30), channel_id=1, source_target_pairs={{0,64},{32,96},{64,0},{96,32},{1,65},{33,97},{65,1},{97,33},{2,66}... | collective-permute-start | bytes 1376264 | tf_op jit(solution)/shard_map/ppermute | solution.py:226
  89.4 20.2 %collective-permute-start.12 = (bf16[256,896]{1,0:T(8,128)(2,1)S(1)}, bf16[256,896]{1,0:T(8,128)(2,1)}, u32[]{:S(2)}, u32[]{:S(2)}) collective-permute-start(bf16[256,896]{1,0:T(8,128)(2,1)S(1)} %bitcast.31), channel_id=1, source_target_pairs={{0,96},{32,0},{64,32},{96,64},{1,97},{33,1},{65,33},{97,65},{2,98}... | collective-permute-start | bytes 1376264 | tf_op jit(solution)/shard_map/ppermute | solution.py:226
  117.6 14.5 %collective-permute-start.16 = (bf16[256,512]{1,0:T(8,128)(2,1)S(1)}, bf16[256,512]{1,0:T(8,128)(2,1)S(1)}, u32[]{:S(2)}, u32[]{:S(2)}) collective-permute-start(bf16[256,512]{1,0:T(8,128)(2,1)S(1)} %shard_map.152.h0), channel_id=1, source_target_pairs={{0,32},{32,64},{64,96},{96,0},{1,33},{33,65},{65,97},{97,1},{2,34}... | collective-permute-start | bytes 786440 | tf_op jit(solution)/shard_map/ppermute | solution.py:226
  120.8 14.2 %collective-permute-start.17 = (bf16[256,512]{1,0:T(8,128)(2,1)S(1)}, bf16[256,512]{1,0:T(8,128)(2,1)S(1)}, u32[]{:S(2)}, u32[]{:S(2)}) collective-permute-start(bf16[256,512]{1,0:T(8,128)(2,1)S(1)} %shard_map.152.h0), channel_id=1, source_target_pairs={{0,64},{32,96},{64,0},{96,32},{1,65},{33,97},{65,1},{97,33},{2,66}... | collective-permute-start | bytes 786440 | tf_op jit(solution)/shard_map/ppermute | solution.py:226
  125.3 10.7 %collective-permute-start.18 = (bf16[256,512]{1,0:T(8,128)(2,1)S(1)}, bf16[256,512]{1,0:T(8,128)(2,1)S(1)}, u32[]{:S(2)}, u32[]{:S(2)}) collective-permute-start(bf16[256,512]{1,0:T(8,128)(2,1)S(1)} %shard_map.152.h0), channel_id=1, source_target_pairs={{0,96},{32,0},{64,32},{96,64},{1,97},{33,1},{65,33},{97,65},{2,98}... | collective-permute-start | bytes 786440 | tf_op jit(solution)/shard_map/ppermute | solution.py:226
  141.1 78.8 %all-to-all-start.1 = ((bf16[128,2,896]{2,1,0:T(2,128)(2,1)}), bf16[128,2,896]{2,1,0:T(2,128)(2,1)S(1)}, u32[]{:S(2)}, u32[]{:S(2)}) async-start(bf16[128,2,896]{2,1,0:T(2,128)(2,1)} %reshape.57), calls=%async_computation.1 | async-start | bytes 917504 | tf_op jit(solution)/shard_map/all_to_all | solution.py:354
  163.1 3.6 %collective-permute-start = (bf16[32,640]{1,0:T(8,128)(2,1)S(1)}, bf16[32,640]{1,0:T(8,128)(2,1)S(1)}, u32[]{:S(2)}, u32[]{:S(2)}) collective-permute-start(bf16[32,640]{1,0:T(8,128)(2,1)S(1)} %maximum_select_fusion), channel_id=1, source_target_pairs={{0,128},{128,0},{256,384},{384,256},{1,129},{129,1},{257,385},{385... | collective-permute-start | bytes 122888 | tf_op jit(solution)/shard_map/ppermute | solution.py:230
  166.7 6.8 %collective-permute-start.1 = (bf16[32,640]{1,0:T(8,128)(2,1)S(1)}, bf16[32,640]{1,0:T(8,128)(2,1)S(1)}, u32[]{:S(2)}, u32[]{:S(2)}) collective-permute-start(bf16[32,640]{1,0:T(8,128)(2,1)S(1)} %fusion.4), channel_id=1, source_target_pairs={{0,256},{128,384},{256,0},{384,128},{1,257},{129,385},{257,1},{385... | collective-permute-start | bytes 122888 | tf_op jit(solution)/shard_map/ppermute | solution.py:230
  173.6 10.3 %collective-permute-start.2 = (bf16[128,640]{1,0:T(8,128)(2,1)S(1)}, bf16[128,640]{1,0:T(8,128)(2,1)S(1)}, u32[]{:S(2)}, u32[]{:S(2)}) collective-permute-start(bf16[128,640]{1,0:T(8,128)(2,1)S(1)} %fusion.1.q0), channel_id=1, source_target_pairs={{0,32},{32,64},{64,96},{96,0},{1,33},{33,65},{65,97},{97,1},{2,34}... | collective-permute-start | bytes 491528 | tf_op jit(solution)/shard_map/ppermute | solution.py:226
  176.2 11.6 %collective-permute-start.3 = (bf16[128,640]{1,0:T(8,128)(2,1)S(1)}, bf16[128,640]{1,0:T(8,128)(2,1)S(1)}, u32[]{:S(2)}, u32[]{:S(2)}) collective-permute-start(bf16[128,640]{1,0:T(8,128)(2,1)S(1)} %fusion.1.q0), channel_id=1, source_target_pairs={{0,64},{32,96},{64,0},{96,32},{1,65},{33,97},{65,1},{97,33},{2,66}... | collective-permute-start | bytes 491528 | tf_op jit(solution)/shard_map/ppermute | solution.py:226
  181.0 7.3 %collective-permute-start.4 = (bf16[128,640]{1,0:T(8,128)(2,1)S(1)}, bf16[128,640]{1,0:T(8,128)(2,1)S(1)}, u32[]{:S(2)}, u32[]{:S(2)}) collective-permute-start(bf16[128,640]{1,0:T(8,128)(2,1)S(1)} %fusion.1.q0), channel_id=1, source_target_pairs={{0,96},{32,0},{64,32},{96,64},{1,97},{33,1},{65,33},{97,65},{2,98}... | collective-permute-start | bytes 491528 | tf_op jit(solution)/shard_map/ppermute | solution.py:226
  190.6 11.2 %collective-permute-start.5 = (bf16[128,640]{1,0:T(8,128)(2,1)S(1)}, bf16[128,640]{1,0:T(8,128)(2,1)S(1)}, u32[]{:S(2)}, u32[]{:S(2)}) collective-permute-start(bf16[128,640]{1,0:T(8,128)(2,1)S(1)} %get-tuple-element.9), channel_id=1, source_target_pairs={{0,96},{32,0},{64,32},{96,64},{1,97},{33,1},{65,33},{97,65},{2,98}... | collective-permute-start | bytes 491528 | tf_op jit(solution)/shard_map/ppermute | solution.py:226
  195.0 7.6 %collective-permute-start.6 = (bf16[128,640]{1,0:T(8,128)(2,1)S(1)}, bf16[128,640]{1,0:T(8,128)(2,1)S(1)}, u32[]{:S(2)}, u32[]{:S(2)}) collective-permute-start(bf16[128,640]{1,0:T(8,128)(2,1)S(1)} %get-tuple-element.10), channel_id=1, source_target_pairs={{0,64},{32,96},{64,0},{96,32},{1,65},{33,97},{65,1},{97,33},{2,66}... | collective-permute-start | bytes 491528 | tf_op jit(solution)/shard_map/ppermute | solution.py:226
  199.2 9.2 %collective-permute-start.7 = (bf16[128,640]{1,0:T(8,128)(2,1)S(1)}, bf16[128,640]{1,0:T(8,128)(2,1)S(1)}, u32[]{:S(2)}, u32[]{:S(2)}) collective-permute-start(bf16[128,640]{1,0:T(8,128)(2,1)S(1)} %get-tuple-element.11), channel_id=1, source_target_pairs={{0,32},{32,64},{64,96},{96,0},{1,33},{33,65},{65,97},{97,1},{2,34}... | collective-permute-start | bytes 491528 | tf_op jit(solution)/shard_map/ppermute | solution.py:226
  208.7 4.3 %collective-permute-start.8 = (bf16[32,512]{1,0:T(8,128)(2,1)S(1)}, bf16[32,512]{1,0:T(8,128)(2,1)S(1)}, u32[]{:S(2)}, u32[]{:S(2)}) collective-permute-start(bf16[32,512]{1,0:T(8,128)(2,1)S(1)} %slice_select_fusion), channel_id=1, source_target_pairs={{0,128},{128,0},{256,384},{384,256},{1,129},{129,1},{257,385},{385... | collective-permute-start | bytes 98312 | tf_op jit(solution)/shard_map/ppermute | solution.py:230
  213.0 6.2 %collective-permute-start.9 = (bf16[32,512]{1,0:T(8,128)(2,1)S(1)}, bf16[32,512]{1,0:T(8,128)(2,1)S(1)}, u32[]{:S(2)}, u32[]{:S(2)}) collective-permute-start(bf16[32,512]{1,0:T(8,128)(2,1)S(1)} %fusion.3), channel_id=1, source_target_pairs={{0,256},{128,384},{256,0},{384,128},{1,257},{129,385},{257,1},{385... | collective-permute-start | bytes 98312 | tf_op jit(solution)/shard_map/ppermute | solution.py:230
  (11 other events, 316.4 us)

commit v2 on v1

--- a/solution.py
+++ b/solution.py
@@ -66,10 +66,16 @@
 
 
 def hidden_kernel(
-    where_ref, b0, b1, b2, b3, w0, w1, w2, w3, out_ref, rows_ref, weights, sems
+    where_ref, b0, b1, b2, b3, w0, w1, w2, w3, out_ref, rows_ref, weights, sems,
+    held, block_sems,
 ):
     rank_dp, rank_tp = where_ref[0], where_ref[1]
     depth, part = w0.shape[0] // 2, w0.shape[1]
+    landing = []
+    for k, b in enumerate((b0, b1, b2, b3)):
+        copy = pltpu.make_async_copy(b, held.at[k], block_sems.at[k])
+        copy.start()
+        landing.append(copy)
     copies = []
     for rel, w in enumerate((w0, w1, w2, w3)):
         slot = rank_dp ^ rel
@@ -83,9 +89,10 @@
             copies.append(copy)
     count, quarter = b0.shape
     slots = count // 4
-    for k, b in enumerate((b0, b1, b2, b3)):
+    for k in range(N_TP):
         base = pl.multiple_of(((rank_tp + N_TP - k) % N_TP) * slots, slots)
-        block = b[...]
+        landing[k].wait()
+        block = held[k]
         for q in range(4):
             pick = jnp.where(
                 iota((slots, count), 1) == iota((slots, count), 0) * 4 + q, 1.0, 0.0
@@ -159,27 +166,60 @@
 
 
 def attend_kernel(
-    where_ref, tables_ref, lengths_ref, q0, q1, q2, q3, cache, mig, o0, o1, o2, o3
+    where_ref,
+    tables_ref,
+    lengths_ref,
+    a0,
+    a1,
+    a2,
+    a3,
+    pool,
+    m0,
+    m1,
+    m2,
+    m3,
+    o0,
+    o1,
+    o2,
+    o3,
+    pages,
+    sem,
+    asked,
+    cache,
+    sems,
 ):
-    rank_tp = where_ref[1]
-    heads = q0.shape[0] // 4
-    for s in range(4):
+    rank_dp, rank_tp = where_ref[0], where_ref[1]
+    source, target, moved = where_ref[2], where_ref[3], where_ref[4]
+    copies = [pltpu.make_async_copy(pool, cache, sems.at[N_TP])]
+    for k, a in enumerate((a0, a1, a2, a3)):
+        copies.append(pltpu.make_async_copy(a, asked.at[k], sems.at[k]))
+    for copy in copies:
+        copy.start()
+    for rel, m in enumerate((m0, m1, m2, m3)):
+
+        @pl.when(source == (rank_dp ^ rel))
+        def _(m=m):
+            copy = pltpu.make_async_copy(m, pages, sem)
+            copy.start()
+            copy.wait()
+
+    for copy in copies:
+        copy.wait()
+    q0, q1, q2, q3 = [asked[k] for k in range(N_TP)]
+    heads = q0.shape[0] // 3
+    for s in range(3):
         query = jnp.concatenate(
             [q[s * heads : (s + 1) * heads, :] for q in (q0, q1, q2, q3)], axis=0
         )
         total_heads = query.shape[0]
-        if s < 3:
-            length = lengths_ref[s].astype(f32)
-        else:
-            length = query[:, ROW : ROW + 1].astype(f32) * 256.0 + query[
-                :, ROW + 1 : ROW + 2
-            ].astype(f32)
-        query = query[:, :ROW]
+        length = lengths_ref[s]
+        use_moved = (rank_dp == target) & (moved == s)
         keys, scores, valid = [], [], []
         for j in range(SLOTS):
-            keys.append(cache[tables_ref[s * SLOTS + j]] if s < 3 else mig[j])
+            own = cache[tables_ref[s * SLOTS + j]]
+            keys.append(jnp.where(use_moved, pages[j * ROW : (j + 1) * ROW, :], own))
             score = jnp.dot(query, keys[j], preferred_element_type=f32) * score_scale
-            place = ((j * N_TP + rank_tp) * PAGE + iota(score.shape, 1)).astype(f32)
+            place = (j * N_TP + rank_tp) * PAGE + iota(score.shape, 1)
             valid.append(place < length)
             scores.append(jnp.where(valid[j], score, neg_fill))
         top = jnp.max(jnp.maximum(scores[0], scores[1]), axis=1, keepdims=True)
@@ -248,13 +288,15 @@
 ):
     rank_tp = lax.axis_index("tp")
     rank_dp = lax.axis_index("dp")
-    where = jnp.stack([rank_dp, rank_tp]).astype(jnp.int32)
+    where = jnp.stack([rank_dp, rank_tp, mig_src[0], mig_dst[0], mig_seq[0]]).astype(jnp.int32)
     ranks_ep = lax.axis_size("ep")
     token_rows, width = tokens.shape
     slots_all = ranks_ep * CAP
     quarter = width // 4
+    part = gate_w.shape[2]
     routes_t = routes.T
     gates_t = gates.T
+    after = lax.optimization_barrier
 
     sent = pl.pallas_call(
         dispatch_kernel,
@@ -267,90 +309,56 @@
         sent.reshape(ranks_ep, CAP * 4, quarter), "ep", split_axis=0, concat_axis=0, tiled=True
     ).reshape(slots_all * 4, quarter)
 
-    first = jnp.concatenate([gate_w[0], up_w[0]], axis=0)
+    gate, up, queries, down, pages, _ = after(
+        (gate_w[0], up_w[0], queries, down_w[0].T, jnp.swapaxes(mig_cache, 1, 2), sent)
+    )
+    first = jnp.concatenate([gate, up], axis=0)
     first_x = swap(first, 2)
     first_c = swap(first, 1)
+    down_c = swap(down, 1)
+    pages = pages.reshape(-1, PAGE)
+    pages_c = swap(pages, 1)
+    heads = queries.shape[1]
+    asked = queries.reshape(3 * heads, ROW)
+    asks = [shift(asked, k) for k in (1, 2, 3)]
+    arrived, first_c, down_c, where, *asks = after((arrived, first_c, down_c, where, *asks))
+
+    blocks = [shift(arrived, k) for k in (1, 2, 3)]
+    first_x, pages_c, *blocks = after((first_x, pages_c, *blocks))
     first_xc = swap(first_x, 1)
-    second = down_w[0].T
-    second_c = swap(second, 1)
-
-    heads = queries.shape[1]
-    at_dst = rank_dp == mig_dst[0]
-    picked = lax.dynamic_index_in_dim(queries, mig_seq[0], 0, keepdims=False)
-    picked_len = lax.dynamic_index_in_dim(lengths[0, 0], mig_seq[0], 0, keepdims=False)
-    lane = jnp.arange(WIDE - ROW)[None, :]
-    tail = jnp.where(
-        lane == 0, picked_len // 256, jnp.where(lane == 1, picked_len % 256, 0)
-    ).astype(bf16)
-    moving = jnp.concatenate([picked, jnp.broadcast_to(tail, (heads, WIDE - ROW))], axis=1)
-    moving = jnp.where(at_dst, moving, jnp.zeros_like(moving))
-    moving = moving + swap(moving, 1)
-    moving = moving + swap(moving, 2)
-    own = jnp.pad(queries.reshape(3 * heads, ROW), ((0, 0), (0, WIDE - ROW)))
-    asked = jnp.concatenate([own, moving], axis=0)
-    asks = [asked] + [shift(asked, k) for k in (1, 2, 3)]
-    parts = pl.pallas_call(
-        attend_kernel,
-        out_shape=[jax.ShapeDtypeStruct((4 * heads, WIDE), bf16)] * 4,
-        in_specs=[SMEM] * 3 + [VMEM] * 6,
-        out_specs=[VMEM] * 4,
-        compiler_params=params(32),
-    )(
-        where,
-        tables.reshape(-1),
-        lengths.reshape(-1),
-        *asks,
-        jnp.swapaxes(cache, 1, 2),
-        jnp.swapaxes(mig_cache, 1, 2),
-    )
-    merged = pl.pallas_call(
-        merge_kernel,
-        out_shape=jax.ShapeDtypeStruct((4 * heads, KV_RANK), bf16),
-        in_specs=[VMEM] * 4,
-        out_specs=VMEM,
-        compiler_params=params(16),
-    )(parts[0], *[shift(parts[k], -k) for k in (1, 2, 3)])
-    back = merged[3 * heads :]
-    back = jnp.where(rank_dp == mig_src[0], back, jnp.zeros_like(back))
-    back = back + swap(back, 1)
-    back = back + swap(back, 2)
-    chosen = at_dst & (jnp.arange(3) == mig_seq[0])
-    attn_out = jnp.where(
-        chosen[:, None, None], back[None], merged[: 3 * heads].reshape(3, heads, KV_RANK)
-    )
-
-    arrived, second_late = lax.optimization_barrier((arrived, second))
-    second_x = swap(second_late, 2)
-    second_xc = swap(second_x, 1)
-    blocks = [arrived] + [shift(arrived, k) for k in (1, 2, 3)]
-    part = gate_w.shape[2]
+    down_x = swap(after((down, first_x))[0], 2)
     rows = N_TP * slots_all
     hidden = pl.pallas_call(
         hidden_kernel,
         out_shape=jax.ShapeDtypeStruct((rows, N_DP * part), bf16),
-        in_specs=[SMEM] + [VMEM] * 4 + [ANY] * 4,
+        in_specs=[SMEM] + [ANY] * 8,
         out_specs=VMEM,
         scratch_shapes=[
             pltpu.VMEM((rows, width), bf16),
             pltpu.VMEM((N_DP, width, 2 * part), bf16),
             pltpu.SemaphoreType.DMA((N_DP, 2)),
+            pltpu.VMEM((N_TP,) + arrived.shape, bf16),
+            pltpu.SemaphoreType.DMA((N_TP,)),
         ],
-        compiler_params=params(40),
-    )(where, *blocks, first, first_c, first_x, first_xc)
+        compiler_params=params(58),
+    )(where, arrived, *blocks, first, first_c, first_x, first_xc)
+    pages_x = swap(after((pages, hidden))[0], 2)
     hiddens = [hidden] + [shift(hidden, k) for k in (1, 2, 3)]
-    cols = second.shape[0]
+    pages_x, *hiddens = after((pages_x, *hiddens))
+    down_xc = swap(after((down_x, *hiddens))[0], 1)
+    cols = down.shape[0]
     expert_out = pl.pallas_call(
         down_kernel,
         out_shape=jax.ShapeDtypeStruct((rows, N_DP * cols), bf16),
         in_specs=[SMEM] + [VMEM] * 4 + [ANY] * 4,
         out_specs=VMEM,
         scratch_shapes=[
-            pltpu.VMEM((rows, second.shape[1]), bf16),
-            pltpu.VMEM((N_DP * cols, second.shape[1]), bf16),
+            pltpu.VMEM((rows, down.shape[1]), bf16),
+            pltpu.VMEM((N_DP * cols, down.shape[1]), bf16),
             pltpu.SemaphoreType.DMA((N_DP,)),
         ],
         compiler_params=params(32),
-    )(where, *hiddens, second, second_c, second_x, second_xc)
+    )(where, *hiddens, down, down_c, down_x, down_xc)
     returned = lax.all_to_all(
         expert_out.reshape(N_TP * ranks_ep, CAP, N_DP * cols),
         ("tp", "ep"),
@@ -358,6 +366,41 @@
         concat_axis=0,
         tiled=True,
     ).reshape(rows, N_DP * cols)
+
+    pages_xc = swap(pages_x, 1)
+    parts = pl.pallas_call(
+        attend_kernel,
+        out_shape=[jax.ShapeDtypeStruct((3 * heads, WIDE), bf16)] * 4,
+        in_specs=[SMEM] * 3 + [ANY] * 9,
+        out_specs=[VMEM] * 4,
+        scratch_shapes=[
+            pltpu.VMEM((SLOTS * ROW, PAGE), bf16),
+            pltpu.SemaphoreType.DMA,
+            pltpu.VMEM((N_TP,) + asked.shape, bf16),
+            pltpu.VMEM((cache.shape[0], ROW, PAGE), bf16),
+            pltpu.SemaphoreType.DMA((N_TP + 1,)),
+        ],
+        compiler_params=params(32),
+    )(
+        where,
+        tables.reshape(-1),
+        lengths.reshape(-1),
+        asked,
+        *asks,
+        jnp.swapaxes(cache, 1, 2),
+        pages,
+        pages_c,
+        pages_x,
+        pages_xc,
+    )
+    merged = pl.pallas_call(
+        merge_kernel,
+        out_shape=jax.ShapeDtypeStruct((3 * heads, KV_RANK), bf16),
+        in_specs=[VMEM] * 4,
+        out_specs=VMEM,
+        compiler_params=params(16),
+    )(parts[0], *[shift(parts[k], -k) for k in (1, 2, 3)])
+    attn_out = merged.reshape(3, heads, KV_RANK)
     moe_out = pl.pallas_call(
         combine_kernel,
         out_shape=jax.ShapeDtypeStruct((token_rows, width), bf16),

time: 222 us -> 173 us (0.78)
  waiting for transfers between devices: 73.8 us -> 43.1 us
  starting transfers between devices: 118 us -> 99.2 us
  local copies, waits for them, and re-layouts: 4.49 us -> 8.48 us
  between operations: 5.8 us -> 2.97 us
  other arithmetic: 2.57 us -> 0 us
    ppermute x10 -> x9, waiting for transfers between devices: 41.5 us -> 9.78 us  [swap(): return lax.ppermute(x, 'dp', [(i, i ^ bit) for i in range(N_DP)])]
    all_to_all x1, starting transfers between devices: 21.3 us -> 9.85 us  [per_device(): lax.all_to_all(expert_out.reshape(N_TP * ranks_ep, CAP, N_DP * cols), ('t...]
    ppermute x12, waiting for transfers between devices: 32.3 us -> 23 us  [shift(): return lax.ppermute(x, 'tp', [(i, (i + k) % N_TP) for i in range(N_TP)])]
    all_to_all x1, waiting for transfers between devices: 0.01 us -> 7.01 us  [per_device(): lax.all_to_all(sent.reshape(ranks_ep, CAP * 4, quarter), 'ep', split_axis...]
    all_to_all x1, starting transfers between devices: 15.2 us -> 10.9 us  [per_device(): lax.all_to_all(sent.reshape(ranks_ep, CAP * 4, quarter), 'ep', split_axis...]
    ppermute x10 -> x9, starting transfers between devices: 40.5 us -> 36.9 us  [swap(): return lax.ppermute(x, 'dp', [(i, i ^ bit) for i in range(N_DP)])]
    all_to_all x1, waiting for transfers between devices: 0.01 us -> 3.31 us  [per_device(): lax.all_to_all(expert_out.reshape(N_TP * ranks_ep, CAP, N_DP * cols), ('t...]
    unnamed x22 -> x37, local copies, waits for them, and re-layouts: 1.85 us -> 4.74 us
  transfers between devices with their start and end apart: 24 -> 23, of which waited for: 14 -> 14; matrix products, arithmetic and copies ran while one was open for 1% -> 0% of each run, Pallas kernels for 5% -> 6%
where the time goes in v2:
time: 173 us; the launch traced here: 171 us
  starting transfers between devices  99.2 us (57%)
  waiting for transfers between devices  43.1 us (25%)
  Pallas kernels  16.7 us (10%)
  local copies, waits for them, and re-layouts  8.48 us (5%)
  between operations  2.97 us (2%)
    ppermute x12, starting transfers between devices, shift(): return lax.ppermute(x, 'tp', [(i, (i + k) % N_TP) for i in range(N_TP)])  41.5 us
    ppermute x9, starting transfers between devices, swap(): return lax.ppermute(x, 'dp', [(i, i ^ bit) for i in range(N_DP)])  36.9 us
    ppermute x12, waiting for transfers between devices, shift(): return lax.ppermute(x, 'tp', [(i, (i + k) % N_TP) for i in range(N_TP)])  23 us
    all_to_all x1, starting transfers between devices, per_device(): lax.all_to_all(sent.reshape(ranks_ep, CAP * 4, quarter), 'ep', split_axis...  10.9 us
    all_to_all x1, starting transfers between devices, per_device(): lax.all_to_all(expert_out.reshape(N_TP * ranks_ep, CAP, N_DP * cols), ('t...  9.85 us
    ppermute x9, waiting for transfers between devices, swap(): return lax.ppermute(x, 'dp', [(i, i ^ bit) for i in range(N_DP)])  9.78 us
    pallas_call x1, Pallas kernels, per_device(): pl.pallas_call(hidden_kernel, out_shape=jax.ShapeDtypeStruct((rows, N_DP...  7.29 us
    all_to_all x1, waiting for transfers between devices, per_device(): lax.all_to_all(sent.reshape(ranks_ep, CAP * 4, quarter), 'ep', split_axis...  7.01 us
  transfers between devices with their start and end apart: 23, of which 14 were waited for; matrix products, arithmetic and copies ran while one was open for 0% of the time, Pallas kernels for 6%

profile of v2, /device:TPU:1, one launch (start us, length us, event | category | flops | bytes accessed | tf_op | source)
XLA Modules:
  0.0 170.5 jit_solution(16065069776445127177)
XLA Ops:
  6.9 8.8 %collective-permute-start = (bf16[7168,128]{1,0:T(8,128)(2,1)}, bf16[7168,128]{1,0:T(8,128)(2,1)}, u32[]{:S(2)}, u32[]{:S(2)}) collective-permute-start(bf16[7168,128]{1,0:T(8,128)(2,1)} %constant_dynamic-update-slice_fusion.w0), channel_id=1, source_target_pairs={{0,128},{128,0},{256,384},{384,256},{1,129},{129,1},{257,385},{385... | collective-permute-start | bytes 5505032 | tf_op jit(solution)/shard_map/ppermute | solution.py:270
  15.7 10.9 %all-to-all-start = ((bf16[32,8,896]{2,1,0:T(8,128)(2,1)}), bf16[32,8,896]{2,1,0:T(8,128)(2,1)}, u32[]{:S(2)}, u32[]{:S(2)}) async-start(bf16[32,8,896]{2,1,0:T(8,128)(2,1)} %bitcast.1), calls=%async_computation | async-start | bytes 917504 | tf_op jit(solution)/shard_map/all_to_all | solution.py:308
  26.5 4.4 %collective-permute-start.5 = (bf16[7168,128]{1,0:T(8,128)(2,1)}, bf16[7168,128]{1,0:T(8,128)(2,1)}, u32[]{:S(2)}, u32[]{:S(2)}) collective-permute-start(bf16[7168,128]{1,0:T(8,128)(2,1)} %constant_dynamic-update-slice_fusion.w0), channel_id=1, source_target_pairs={{0,256},{128,384},{256,0},{384,128},{1,257},{129,385},{257,1},{385... | collective-permute-start | bytes 5505032 | tf_op jit(solution)/shard_map/ppermute | solution.py:270
  36.6 4.5 %collective-permute-start.3 = (bf16[96,576]{1,0:T(8,128)(2,1)S(1)}, bf16[96,576]{1,0:T(8,128)(2,1)S(1)}, u32[]{:S(2)}, u32[]{:S(2)}) collective-permute-start(bf16[96,576]{1,0:T(8,128)(2,1)S(1)} %bitcast.26), channel_id=1, source_target_pairs={{0,64},{32,96},{64,0},{96,32},{1,65},{33,97},{65,1},{97,33},{2,66}... | collective-permute-start | bytes 331784 | tf_op jit(solution)/shard_map/ppermute | solution.py:266
  41.7 3.3 %collective-permute-start.4 = (bf16[96,576]{1,0:T(8,128)(2,1)S(1)}, bf16[96,576]{1,0:T(8,128)(2,1)S(1)}, u32[]{:S(2)}, u32[]{:S(2)}) collective-permute-start(bf16[96,576]{1,0:T(8,128)(2,1)S(1)} %bitcast.27), channel_id=1, source_target_pairs={{0,96},{32,0},{64,32},{96,64},{1,97},{33,1},{65,33},{97,65},{2,98}... | collective-permute-start | bytes 331784 | tf_op jit(solution)/shard_map/ppermute | solution.py:266
  48.0 7.0 %all-to-all-done = bf16[32,8,896]{2,1,0:T(8,128)(2,1)} async-done(((bf16[32,8,896]{2,1,0:T(8,128)(2,1)}), bf16[32,8,896]{2,1,0:T(8,128)(2,1)}, u32[]{:S(2)}, u32[]{:S(2)}) %all-to-all-start) | async-done | bytes 458784 | tf_op jit(solution)/shard_map/all_to_all | solution.py:308
  58.2 4.5 %collective-permute-start.8 = (bf16[256,896]{1,0:T(8,128)(2,1)}, bf16[256,896]{1,0:T(8,128)(2,1)S(1)}, u32[]{:S(2)}, u32[]{:S(2)}) collective-permute-start(bf16[256,896]{1,0:T(8,128)(2,1)} %bitcast.2.b0), channel_id=1, source_target_pairs={{0,64},{32,96},{64,0},{96,32},{1,65},{33,97},{65,1},{97,33},{2,66}... | collective-permute-start | bytes 1376264 | tf_op jit(solution)/shard_map/ppermute | solution.py:266
  65.7 3.6 %collective-permute-start.6 = (bf16[1152,128]{1,0:T(8,128)(2,1)S(1)}, bf16[1152,128]{1,0:T(8,128)(2,1)S(1)}, u32[]{:S(2)}, u32[]{:S(2)}) collective-permute-start(bf16[1152,128]{1,0:T(8,128)(2,1)S(1)} %bitcast.22), channel_id=1, source_target_pairs={{0,128},{128,0},{256,384},{384,256},{1,129},{129,1},{257,385},{385... | collective-permute-start | bytes 884744 | tf_op jit(solution)/shard_map/ppermute | solution.py:270
  70.6 5.3 %collective-permute-done.5.w2 = bf16[7168,128]{1,0:T(8,128)(2,1)} collective-permute-done((bf16[7168,128]{1,0:T(8,128)(2,1)}, bf16[7168,128]{1,0:T(8,128)(2,1)}, u32[]{:S(2)}, u32[]{:S(2)}) %collective-permute-start.5) | collective-permute-done | bytes 1835040 | tf_op jit(solution)/shard_map/ppermute | solution.py:270
  75.9 4.7 %collective-permute-done.8.b2 = bf16[256,896]{1,0:T(8,128)(2,1)S(1)} collective-permute-done((bf16[256,896]{1,0:T(8,128)(2,1)}, bf16[256,896]{1,0:T(8,128)(2,1)S(1)}, u32[]{:S(2)}, u32[]{:S(2)}) %collective-permute-start.8) | collective-permute-done | bytes 458784 | tf_op jit(solution)/shard_map/ppermute | solution.py:266
  82.2 3.3 %collective-permute-start.10 = (bf16[7168,128]{1,0:T(8,128)(2,1)}, bf16[7168,128]{1,0:T(8,128)(2,1)}, u32[]{:S(2)}, u32[]{:S(2)}) collective-permute-start(bf16[7168,128]{1,0:T(8,128)(2,1)} %collective-permute-done.5.w2), channel_id=1, source_target_pairs={{0,128},{128,0},{256,384},{384,256},{1,129},{129,1},{257,385},{385... | collective-permute-start | bytes 5505032 | tf_op jit(solution)/shard_map/ppermute | solution.py:270
  85.6 4.4 %collective-permute-start.19 = (bf16[224,2048]{1,0:T(8,128)(2,1)S(1)}, bf16[224,2048]{1,0:T(8,128)(2,1)S(1)}, u32[]{:S(2)}, u32[]{:S(2)}) collective-permute-start(bf16[224,2048]{1,0:T(8,128)(2,1)S(1)} %bitcast.19), channel_id=1, source_target_pairs={{0,256},{128,384},{256,0},{384,128},{1,257},{129,385},{257,1},{385... | collective-permute-start | bytes 2752520 | tf_op jit(solution)/shard_map/ppermute | solution.py:270
  90.0 7.3 %shard_map.150.h0 = bf16[256,512]{1,0:T(8,128)(2,1)} custom-call(s32[5]{0:T(128)} %stack.11.where_ref, bf16[256,896]{1,0:T(8,128)(2,1)} %bitcast.2.b0, bf16[256,896]{1,0:T(8,128)(2,1)} %copy-done.15, bf16[256,896]{1,0:T(8,128)(2,1)} %copy-done.16, bf16[256,896]{1,0:T(8,128)(2,1)} %copy-done.17, bf16[7168,128]{1,0:T(8,128)(2,1)} %constant_dynamic-update-slice_fusion.w0, ...), custom_call_target="tpu_custom_call" | custom-call | tf_op jit(solution)/shard_map/pallas_call | solution.py:331
  97.3 3.7 %collective-permute-start.11 = (bf16[1152,128]{1,0:T(8,128)(2,1)S(1)}, bf16[1152,128]{1,0:T(8,128)(2,1)S(1)}, u32[]{:S(2)}, u32[]{:S(2)}) collective-permute-start(bf16[1152,128]{1,0:T(8,128)(2,1)S(1)} %bitcast.23), channel_id=1, source_target_pairs={{0,256},{128,384},{256,0},{384,128},{1,257},{129,385},{257,1},{385... | collective-permute-start | bytes 884744 | tf_op jit(solution)/shard_map/ppermute | solution.py:270
  101.0 4.1 %collective-permute-start.12 = (bf16[256,512]{1,0:T(8,128)(2,1)}, bf16[256,512]{1,0:T(8,128)(2,1)S(1)}, u32[]{:S(2)}, u32[]{:S(2)}) collective-permute-start(bf16[256,512]{1,0:T(8,128)(2,1)} %shard_map.150.h0), channel_id=1, source_target_pairs={{0,32},{32,64},{64,96},{96,0},{1,33},{33,65},{65,97},{97,1},{2,34}... | collective-permute-start | bytes 786440 | tf_op jit(solution)/shard_map/ppermute | solution.py:266
  105.1 3.2 %collective-permute-start.13 = (bf16[256,512]{1,0:T(8,128)(2,1)}, bf16[256,512]{1,0:T(8,128)(2,1)S(1)}, u32[]{:S(2)}, u32[]{:S(2)}) collective-permute-start(bf16[256,512]{1,0:T(8,128)(2,1)} %shard_map.150.h0), channel_id=1, source_target_pairs={{0,64},{32,96},{64,0},{96,32},{1,65},{33,97},{65,1},{97,33},{2,66}... | collective-permute-start | bytes 786440 | tf_op jit(solution)/shard_map/ppermute | solution.py:266
  108.4 3.3 %collective-permute-start.14 = (bf16[256,512]{1,0:T(8,128)(2,1)}, bf16[256,512]{1,0:T(8,128)(2,1)S(1)}, u32[]{:S(2)}, u32[]{:S(2)}) collective-permute-start(bf16[256,512]{1,0:T(8,128)(2,1)} %shard_map.150.h0), channel_id=1, source_target_pairs={{0,96},{32,0},{64,32},{96,64},{1,97},{33,1},{65,33},{97,65},{2,98}... | collective-permute-start | bytes 786440 | tf_op jit(solution)/shard_map/ppermute | solution.py:266
  111.7 6.3 %collective-permute-done.13.h2 = bf16[256,512]{1,0:T(8,128)(2,1)S(1)} collective-permute-done((bf16[256,512]{1,0:T(8,128)(2,1)}, bf16[256,512]{1,0:T(8,128)(2,1)S(1)}, u32[]{:S(2)}, u32[]{:S(2)}) %collective-permute-start.13) | collective-permute-done | bytes 262176 | tf_op jit(solution)/shard_map/ppermute | solution.py:266
  119.3 3.7 %collective-permute-start.20 = (bf16[224,2048]{1,0:T(8,128)(2,1)S(1)}, bf16[224,2048]{1,0:T(8,128)(2,1)S(1)}, u32[]{:S(2)}, u32[]{:S(2)}) collective-permute-start(bf16[224,2048]{1,0:T(8,128)(2,1)S(1)} %collective-permute-done.19.d2), channel_id=1, source_target_pairs={{0,128},{128,0},{256,384},{384,256},{1,129},{129,1},{257,385},{385... | collective-permute-start | bytes 2752520 | tf_op jit(solution)/shard_map/ppermute | solution.py:270
  130.2 9.8 %all-to-all-start.1 = ((bf16[128,2,896]{2,1,0:T(2,128)(2,1)}), bf16[128,2,896]{2,1,0:T(2,128)(2,1)}, u32[]{:S(2)}, u32[]{:S(2)}) async-start(bf16[128,2,896]{2,1,0:T(2,128)(2,1)} %reshape.38), calls=%async_computation.1 | async-start | bytes 917504 | tf_op jit(solution)/shard_map/all_to_all | solution.py:362
  146.6 4.4 %collective-permute-start.16 = (bf16[96,640]{1,0:T(8,128)(2,1)S(1)}, bf16[96,640]{1,0:T(8,128)(2,1)S(1)}, u32[]{:S(2)}, u32[]{:S(2)}) collective-permute-start(bf16[96,640]{1,0:T(8,128)(2,1)S(1)} %get-tuple-element.50), channel_id=1, source_target_pairs={{0,96},{32,0},{64,32},{96,64},{1,97},{33,1},{65,33},{97,65},{2,98}... | collective-permute-start | bytes 368648 | tf_op jit(solution)/shard_map/ppermute | solution.py:266
  155.9 4.1 %collective-permute-done.17.p2 = bf16[96,640]{1,0:T(8,128)(2,1)S(1)} collective-permute-done((bf16[96,640]{1,0:T(8,128)(2,1)S(1)}, bf16[96,640]{1,0:T(8,128)(2,1)S(1)}, u32[]{:S(2)}, u32[]{:S(2)}) %collective-permute-start.17) | collective-permute-done | bytes 122912 | tf_op jit(solution)/shard_map/ppermute | solution.py:266
  160.0 3.9 %collective-permute-done.18.p3 = bf16[96,640]{1,0:T(8,128)(2,1)S(1)} collective-permute-done((bf16[96,640]{1,0:T(8,128)(2,1)S(1)}, bf16[96,640]{1,0:T(8,128)(2,1)S(1)}, u32[]{:S(2)}, u32[]{:S(2)}) %collective-permute-start.18) | collective-permute-done | bytes 122912 | tf_op jit(solution)/shard_map/ppermute | solution.py:266
  164.9 3.3 %all-to-all-done.1 = bf16[128,2,896]{2,1,0:T(2,128)(2,1)} async-done(((bf16[128,2,896]{2,1,0:T(2,128)(2,1)}), bf16[128,2,896]{2,1,0:T(2,128)(2,1)}, u32[]{:S(2)}, u32[]{:S(2)}) %all-to-all-start.1) | async-done | bytes 458784 | tf_op jit(solution)/shard_map/all_to_all | solution.py:362
  (69 shorter events, 45.6 us)
Async XLA Ops:
  5.9 59.9 %copy-start.3 = (bf16[2,128,576]{1,2,0:T(8,128)(2,1)S(1)}, bf16[2,128,576]{1,2,0:T(8,128)(2,1)}, u32[]{:S(2)}) copy-start(bf16[2,128,576]{1,2,0:T(8,128)(2,1)} %param.18) | copy-start | bytes 884740
  6.9 48.1 %collective-permute-start = (bf16[7168,128]{1,0:T(8,128)(2,1)}, bf16[7168,128]{1,0:T(8,128)(2,1)}, u32[]{:S(2)}, u32[]{:S(2)}) collective-permute-start(bf16[7168,128]{1,0:T(8,128)(2,1)} %constant_dynamic-update-slice_fusion.w0), channel_id=1, source_target_pairs={{0,128},{128,0},{256,384},{384,256},{1,129},{129,1},{257,385},{385... | collective-permute-start | bytes 5505032 | tf_op jit(solution)/shard_map/ppermute | solution.py:270
  15.7 39.3 %all-to-all-start = ((bf16[32,8,896]{2,1,0:T(8,128)(2,1)}), bf16[32,8,896]{2,1,0:T(8,128)(2,1)}, u32[]{:S(2)}, u32[]{:S(2)}) async-start(bf16[32,8,896]{2,1,0:T(8,128)(2,1)} %bitcast.1), calls=%async_computation | async-start | bytes 917504 | tf_op jit(solution)/shard_map/all_to_all | solution.py:308
  26.5 49.3 %collective-permute-start.5 = (bf16[7168,128]{1,0:T(8,128)(2,1)}, bf16[7168,128]{1,0:T(8,128)(2,1)}, u32[]{:S(2)}, u32[]{:S(2)}) collective-permute-start(bf16[7168,128]{1,0:T(8,128)(2,1)} %constant_dynamic-update-slice_fusion.w0), channel_id=1, source_target_pairs={{0,256},{128,384},{256,0},{384,128},{1,257},{129,385},{257,1},{385... | collective-permute-start | bytes 5505032 | tf_op jit(solution)/shard_map/ppermute | solution.py:270
  30.9 17.1 %collective-permute-start.1 = (bf16[224,2048]{1,0:T(8,128)(2,1)S(1)}, bf16[224,2048]{1,0:T(8,128)(2,1)S(1)}, u32[]{:S(2)}, u32[]{:S(2)}) collective-permute-start(bf16[224,2048]{1,0:T(8,128)(2,1)S(1)} %bitcast.18), channel_id=1, source_target_pairs={{0,128},{128,0},{256,384},{384,256},{1,129},{129,1},{257,385},{385... | collective-permute-start | bytes 2752520 | tf_op jit(solution)/shard_map/ppermute | solution.py:270
  33.4 8.3 %collective-permute-start.2 = (bf16[96,576]{1,0:T(8,128)(2,1)S(1)}, bf16[96,576]{1,0:T(8,128)(2,1)S(1)}, u32[]{:S(2)}, u32[]{:S(2)}) collective-permute-start(bf16[96,576]{1,0:T(8,128)(2,1)S(1)} %bitcast.25), channel_id=1, source_target_pairs={{0,32},{32,64},{64,96},{96,0},{1,33},{33,65},{65,97},{97,1},{2,34}... | collective-permute-start | bytes 331784 | tf_op jit(solution)/shard_map/ppermute | solution.py:266
  36.6 10.9 %collective-permute-start.3 = (bf16[96,576]{1,0:T(8,128)(2,1)S(1)}, bf16[96,576]{1,0:T(8,128)(2,1)S(1)}, u32[]{:S(2)}, u32[]{:S(2)}) collective-permute-start(bf16[96,576]{1,0:T(8,128)(2,1)S(1)} %bitcast.26), channel_id=1, source_target_pairs={{0,64},{32,96},{64,0},{96,32},{1,65},{33,97},{65,1},{97,33},{2,66}... | collective-permute-start | bytes 331784 | tf_op jit(solution)/shard_map/ppermute | solution.py:266
  41.7 6.3 %collective-permute-start.4 = (bf16[96,576]{1,0:T(8,128)(2,1)S(1)}, bf16[96,576]{1,0:T(8,128)(2,1)S(1)}, u32[]{:S(2)}, u32[]{:S(2)}) collective-permute-start(bf16[96,576]{1,0:T(8,128)(2,1)S(1)} %bitcast.27), channel_id=1, source_target_pairs={{0,96},{32,0},{64,32},{96,64},{1,97},{33,1},{65,33},{97,65},{2,98}... | collective-permute-start | bytes 331784 | tf_op jit(solution)/shard_map/ppermute | solution.py:266
  55.0 20.9 %collective-permute-start.7 = (bf16[256,896]{1,0:T(8,128)(2,1)}, bf16[256,896]{1,0:T(8,128)(2,1)S(1)}, u32[]{:S(2)}, u32[]{:S(2)}) collective-permute-start(bf16[256,896]{1,0:T(8,128)(2,1)} %bitcast.2.b0), channel_id=1, source_target_pairs={{0,32},{32,64},{64,96},{96,0},{1,33},{33,65},{65,97},{97,1},{2,34}... | collective-permute-start | bytes 1376264 | tf_op jit(solution)/shard_map/ppermute | solution.py:266
  58.2 22.3 %collective-permute-start.8 = (bf16[256,896]{1,0:T(8,128)(2,1)}, bf16[256,896]{1,0:T(8,128)(2,1)S(1)}, u32[]{:S(2)}, u32[]{:S(2)}) collective-permute-start(bf16[256,896]{1,0:T(8,128)(2,1)} %bitcast.2.b0), channel_id=1, source_target_pairs={{0,64},{32,96},{64,0},{96,32},{1,65},{33,97},{65,1},{97,33},{2,66}... | collective-permute-start | bytes 1376264 | tf_op jit(solution)/shard_map/ppermute | solution.py:266
  62.7 19.5 %collective-permute-start.9 = (bf16[256,896]{1,0:T(8,128)(2,1)}, bf16[256,896]{1,0:T(8,128)(2,1)S(1)}, u32[]{:S(2)}, u32[]{:S(2)}) collective-permute-start(bf16[256,896]{1,0:T(8,128)(2,1)} %bitcast.2.b0), channel_id=1, source_target_pairs={{0,96},{32,0},{64,32},{96,64},{1,97},{33,1},{65,33},{97,65},{2,98}... | collective-permute-start | bytes 1376264 | tf_op jit(solution)/shard_map/ppermute | solution.py:266
  65.7 4.8 %collective-permute-start.6 = (bf16[1152,128]{1,0:T(8,128)(2,1)S(1)}, bf16[1152,128]{1,0:T(8,128)(2,1)S(1)}, u32[]{:S(2)}, u32[]{:S(2)}) collective-permute-start(bf16[1152,128]{1,0:T(8,128)(2,1)S(1)} %bitcast.22), channel_id=1, source_target_pairs={{0,128},{128,0},{256,384},{384,256},{1,129},{129,1},{257,385},{385... | collective-permute-start | bytes 884744 | tf_op jit(solution)/shard_map/ppermute | solution.py:270
  82.2 7.7 %collective-permute-start.10 = (bf16[7168,128]{1,0:T(8,128)(2,1)}, bf16[7168,128]{1,0:T(8,128)(2,1)}, u32[]{:S(2)}, u32[]{:S(2)}) collective-permute-start(bf16[7168,128]{1,0:T(8,128)(2,1)} %collective-permute-done.5.w2), channel_id=1, source_target_pairs={{0,128},{128,0},{256,384},{384,256},{1,129},{129,1},{257,385},{385... | collective-permute-start | bytes 5505032 | tf_op jit(solution)/shard_map/ppermute | solution.py:270
  85.6 33.7 %collective-permute-start.19 = (bf16[224,2048]{1,0:T(8,128)(2,1)S(1)}, bf16[224,2048]{1,0:T(8,128)(2,1)S(1)}, u32[]{:S(2)}, u32[]{:S(2)}) collective-permute-start(bf16[224,2048]{1,0:T(8,128)(2,1)S(1)} %bitcast.19), channel_id=1, source_target_pairs={{0,256},{128,384},{256,0},{384,128},{1,257},{129,385},{257,1},{385... | collective-permute-start | bytes 2752520 | tf_op jit(solution)/shard_map/ppermute | solution.py:270
  97.3 22.0 %collective-permute-start.11 = (bf16[1152,128]{1,0:T(8,128)(2,1)S(1)}, bf16[1152,128]{1,0:T(8,128)(2,1)S(1)}, u32[]{:S(2)}, u32[]{:S(2)}) collective-permute-start(bf16[1152,128]{1,0:T(8,128)(2,1)S(1)} %bitcast.23), channel_id=1, source_target_pairs={{0,256},{128,384},{256,0},{384,128},{1,257},{129,385},{257,1},{385... | collective-permute-start | bytes 884744 | tf_op jit(solution)/shard_map/ppermute | solution.py:270
  101.0 10.7 %collective-permute-start.12 = (bf16[256,512]{1,0:T(8,128)(2,1)}, bf16[256,512]{1,0:T(8,128)(2,1)S(1)}, u32[]{:S(2)}, u32[]{:S(2)}) collective-permute-start(bf16[256,512]{1,0:T(8,128)(2,1)} %shard_map.150.h0), channel_id=1, source_target_pairs={{0,32},{32,64},{64,96},{96,0},{1,33},{33,65},{65,97},{97,1},{2,34}... | collective-permute-start | bytes 786440 | tf_op jit(solution)/shard_map/ppermute | solution.py:266
  105.1 12.9 %collective-permute-start.13 = (bf16[256,512]{1,0:T(8,128)(2,1)}, bf16[256,512]{1,0:T(8,128)(2,1)S(1)}, u32[]{:S(2)}, u32[]{:S(2)}) collective-permute-start(bf16[256,512]{1,0:T(8,128)(2,1)} %shard_map.150.h0), channel_id=1, source_target_pairs={{0,64},{32,96},{64,0},{96,32},{1,65},{33,97},{65,1},{97,33},{2,66}... | collective-permute-start | bytes 786440 | tf_op jit(solution)/shard_map/ppermute | solution.py:266
  108.4 10.9 %collective-permute-start.14 = (bf16[256,512]{1,0:T(8,128)(2,1)}, bf16[256,512]{1,0:T(8,128)(2,1)S(1)}, u32[]{:S(2)}, u32[]{:S(2)}) collective-permute-start(bf16[256,512]{1,0:T(8,128)(2,1)} %shard_map.150.h0), channel_id=1, source_target_pairs={{0,96},{32,0},{64,32},{96,64},{1,97},{33,1},{65,33},{97,65},{2,98}... | collective-permute-start | bytes 786440 | tf_op jit(solution)/shard_map/ppermute | solution.py:266
  119.3 5.8 %collective-permute-start.20 = (bf16[224,2048]{1,0:T(8,128)(2,1)S(1)}, bf16[224,2048]{1,0:T(8,128)(2,1)S(1)}, u32[]{:S(2)}, u32[]{:S(2)}) collective-permute-start(bf16[224,2048]{1,0:T(8,128)(2,1)S(1)} %collective-permute-done.19.d2), channel_id=1, source_target_pairs={{0,128},{128,0},{256,384},{384,256},{1,129},{129,1},{257,385},{385... | collective-permute-start | bytes 2752520 | tf_op jit(solution)/shard_map/ppermute | solution.py:270
  130.2 38.0 %all-to-all-start.1 = ((bf16[128,2,896]{2,1,0:T(2,128)(2,1)}), bf16[128,2,896]{2,1,0:T(2,128)(2,1)}, u32[]{:S(2)}, u32[]{:S(2)}) async-start(bf16[128,2,896]{2,1,0:T(2,128)(2,1)} %reshape.38), calls=%async_computation.1 | async-start | bytes 917504 | tf_op jit(solution)/shard_map/all_to_all | solution.py:362
  140.0 3.8 %collective-permute-start.15 = (bf16[1152,128]{1,0:T(8,128)(2,1)S(1)}, bf16[1152,128]{1,0:T(8,128)(2,1)S(1)}, u32[]{:S(2)}, u32[]{:S(2)}) collective-permute-start(bf16[1152,128]{1,0:T(8,128)(2,1)S(1)} %collective-permute-done.11.m2), channel_id=1, source_target_pairs={{0,128},{128,0},{256,384},{384,256},{1,129},{129,1},{257,385},{385... | collective-permute-start | bytes 884744 | tf_op jit(solution)/shard_map/ppermute | solution.py:270
  146.6 9.2 %collective-permute-start.16 = (bf16[96,640]{1,0:T(8,128)(2,1)S(1)}, bf16[96,640]{1,0:T(8,128)(2,1)S(1)}, u32[]{:S(2)}, u32[]{:S(2)}) collective-permute-start(bf16[96,640]{1,0:T(8,128)(2,1)S(1)} %get-tuple-element.50), channel_id=1, source_target_pairs={{0,96},{32,0},{64,32},{96,64},{1,97},{33,1},{65,33},{97,65},{2,98}... | collective-permute-start | bytes 368648 | tf_op jit(solution)/shard_map/ppermute | solution.py:266
  151.1 8.9 %collective-permute-start.17 = (bf16[96,640]{1,0:T(8,128)(2,1)S(1)}, bf16[96,640]{1,0:T(8,128)(2,1)S(1)}, u32[]{:S(2)}, u32[]{:S(2)}) collective-permute-start(bf16[96,640]{1,0:T(8,128)(2,1)S(1)} %get-tuple-element.51), channel_id=1, source_target_pairs={{0,64},{32,96},{64,0},{96,32},{1,65},{33,97},{65,1},{97,33},{2,66}... | collective-permute-start | bytes 368648 | tf_op jit(solution)/shard_map/ppermute | solution.py:266
  153.1 10.8 %collective-permute-start.18 = (bf16[96,640]{1,0:T(8,128)(2,1)S(1)}, bf16[96,640]{1,0:T(8,128)(2,1)S(1)}, u32[]{:S(2)}, u32[]{:S(2)}) collective-permute-start(bf16[96,640]{1,0:T(8,128)(2,1)S(1)} %get-tuple-element.52), channel_id=1, source_target_pairs={{0,32},{32,64},{64,96},{96,0},{1,33},{33,65},{65,97},{97,1},{2,34}... | collective-permute-start | bytes 368648 | tf_op jit(solution)/shard_map/ppermute | solution.py:266
  (17 other events, 308.4 us)

commit v3 on v2

--- a/solution.py
+++ b/solution.py
@@ -49,7 +49,15 @@
     return slot_rows, slot_cols
 
 
-def dispatch_kernel(routes_ref, tok_ref, out_ref):
+def dispatch_kernel(routes_any, tok_any, out_ref, routes_ref, tok_ref, sems):
+    copies = [
+        pltpu.make_async_copy(routes_any, routes_ref, sems.at[0]),
+        pltpu.make_async_copy(tok_any, tok_ref, sems.at[1]),
+    ]
+    for copy in copies:
+        copy.start()
+    for copy in copies:
+        copy.wait()
     slot_rows, _ = route_slots(routes_ref)
     rows, quarter = out_ref.shape
     n = tok_ref.shape[0]
@@ -106,24 +114,24 @@
         both = jnp.dot(rows_ref[...], weights[i], preferred_element_type=f32)
         gate, up = both[:, :part], both[:, part:]
         hidden = gate / (1.0 + jnp.exp(-gate)) * up
-        out_ref[:, i * part : (i + 1) * part] = hidden.astype(bf16)
-
-
-def down_kernel(where_ref, h0, h1, h2, h3, d0, d1, d2, d3, out_ref, hidden, weights, sems):
-    rank_dp, rank_tp = where_ref[0], where_ref[1]
+        for copy in range(out_ref.shape[0]):
+            out_ref[copy, :, i * part : (i + 1) * part] = hidden.astype(bf16)
+
+
+def down_kernel(where_ref, parts, d0, d1, d2, d3, out_ref, hidden, weights, sems):
+    rank_dp = where_ref[0]
     cols = d0.shape[0]
-    part = h0.shape[1] // N_DP
+    part = parts.shape[2] // N_DP
     copies = []
     for rel, d in enumerate((d0, d1, d2, d3)):
         base = pl.multiple_of((rank_dp ^ rel) * cols, 16)
         copy = pltpu.make_async_copy(d, weights.at[pl.ds(base, cols), :], sems.at[rel])
         copy.start()
         copies.append(copy)
-    for k, h in enumerate((h0, h1, h2, h3)):
-        source = (rank_tp + N_TP - k) % N_TP
+    for t in range(N_TP):
         for i in range(N_DP):
-            base = pl.multiple_of((i * N_TP + source) * part, part)
-            hidden[:, pl.ds(base, part)] = h[:, i * part : (i + 1) * part]
+            base = (i * N_TP + t) * part
+            hidden[:, base : base + part] = parts[t, :, i * part : (i + 1) * part]
     for copy in copies:
         copy.wait()
     out_ref[...] = lax.dot_general(
@@ -171,8 +179,7 @@
     lengths_ref,
     a0,
     a1,
-    a2,
-    a3,
+    far,
     pool,
     m0,
     m1,
@@ -191,7 +198,9 @@
     rank_dp, rank_tp = where_ref[0], where_ref[1]
     source, target, moved = where_ref[2], where_ref[3], where_ref[4]
     copies = [pltpu.make_async_copy(pool, cache, sems.at[N_TP])]
-    for k, a in enumerate((a0, a1, a2, a3)):
+    rows = a0.shape[0]
+    pairs = (a0, a1, far.at[pl.ds(0, rows), :], far.at[pl.ds(rows, rows), :])
+    for k, a in enumerate(pairs):
         copies.append(pltpu.make_async_copy(a, asked.at[k], sems.at[k]))
     for copy in copies:
         copy.start()
@@ -301,9 +310,14 @@
     sent = pl.pallas_call(
         dispatch_kernel,
         out_shape=jax.ShapeDtypeStruct((slots_all * 4, quarter), bf16),
-        in_specs=[VMEM] * 2,
+        in_specs=[ANY] * 2,
         out_specs=VMEM,
-        compiler_params=params(24),
+        scratch_shapes=[
+            pltpu.VMEM(routes_t.shape, routes_t.dtype),
+            pltpu.VMEM(tokens.shape, tokens.dtype),
+            pltpu.SemaphoreType.DMA((2,)),
+        ],
+        compiler_params=params(58),
     )(routes_t, tokens)
     arrived = lax.all_to_all(
         sent.reshape(ranks_ep, CAP * 4, quarter), "ep", split_axis=0, concat_axis=0, tiled=True
@@ -317,20 +331,22 @@
     first_c = swap(first, 1)
     down_c = swap(down, 1)
     pages = pages.reshape(-1, PAGE)
-    pages_c = swap(pages, 1)
     heads = queries.shape[1]
     asked = queries.reshape(3 * heads, ROW)
-    asks = [shift(asked, k) for k in (1, 2, 3)]
-    arrived, first_c, down_c, where, *asks = after((arrived, first_c, down_c, where, *asks))
+    near = shift(asked, 1)
+    far = shift(jnp.concatenate([asked, near], axis=0), 2)
+    pages_c = swap(pages, 1)
+    arrived, down_c, pages_c, where, near = after((arrived, down_c, pages_c, where, near))
 
     blocks = [shift(arrived, k) for k in (1, 2, 3)]
-    first_x, pages_c, *blocks = after((first_x, pages_c, *blocks))
+    first_x, first_c, far, *blocks = after((first_x, first_c, far, *blocks))
+    asks = [near, far]
     first_xc = swap(first_x, 1)
     down_x = swap(after((down, first_x))[0], 2)
     rows = N_TP * slots_all
     hidden = pl.pallas_call(
         hidden_kernel,
-        out_shape=jax.ShapeDtypeStruct((rows, N_DP * part), bf16),
+        out_shape=jax.ShapeDtypeStruct((N_TP, rows, N_DP * part), bf16),
         in_specs=[SMEM] + [ANY] * 8,
         out_specs=VMEM,
         scratch_shapes=[
@@ -343,14 +359,14 @@
         compiler_params=params(58),
     )(where, arrived, *blocks, first, first_c, first_x, first_xc)
     pages_x = swap(after((pages, hidden))[0], 2)
-    hiddens = [hidden] + [shift(hidden, k) for k in (1, 2, 3)]
+    hiddens = [lax.all_to_all(hidden, "tp", split_axis=0, concat_axis=0, tiled=True)]
     pages_x, *hiddens = after((pages_x, *hiddens))
     down_xc = swap(after((down_x, *hiddens))[0], 1)
     cols = down.shape[0]
     expert_out = pl.pallas_call(
         down_kernel,
         out_shape=jax.ShapeDtypeStruct((rows, N_DP * cols), bf16),
-        in_specs=[SMEM] + [VMEM] * 4 + [ANY] * 4,
+        in_specs=[SMEM] + [VMEM] + [ANY] * 4,
         out_specs=VMEM,
         scratch_shapes=[
             pltpu.VMEM((rows, down.shape[1]), bf16),
@@ -371,7 +387,7 @@
     parts = pl.pallas_call(
         attend_kernel,
         out_shape=[jax.ShapeDtypeStruct((3 * heads, WIDE), bf16)] * 4,
-        in_specs=[SMEM] * 3 + [ANY] * 9,
+        in_specs=[SMEM] * 3 + [ANY] * 8,
         out_specs=[VMEM] * 4,
         scratch_shapes=[
             pltpu.VMEM((SLOTS * ROW, PAGE), bf16),

time: 173 us -> 167 us (0.965)
  starting transfers between devices: 99.2 us -> 91.4 us
  Pallas kernels: 16.7 us -> 18.5 us
    ppermute x9, waiting for transfers between devices: 9.78 us -> 27.3 us  [swap(): return lax.ppermute(x, 'dp', [(i, i ^ bit) for i in range(N_DP)])]
    ppermute x12 -> x8, starting transfers between devices: 41.5 us -> 26.6 us  [shift(): return lax.ppermute(x, 'tp', [(i, (i + k) % N_TP) for i in range(N_TP)])]
    ppermute x12 -> x8, waiting for transfers between devices: 23 us -> 13.2 us  [shift(): return lax.ppermute(x, 'tp', [(i, (i + k) % N_TP) for i in range(N_TP)])]
    ppermute x9, starting transfers between devices: 36.9 us -> 29.2 us  [swap(): return lax.ppermute(x, 'dp', [(i, i ^ bit) for i in range(N_DP)])]
    all_to_all x1, waiting for transfers between devices: 7.01 us -> 0.75 us  [per_device(): lax.all_to_all(sent.reshape(ranks_ep, CAP * 4, quarter), 'ep', split_axis...]
    all_to_all x1, starting transfers between devices: 10.9 us -> 17 us  [per_device(): lax.all_to_all(sent.reshape(ranks_ep, CAP * 4, quarter), 'ep', split_axis...]
    all_to_all x1, starting transfers between devices: 9.85 us -> 14.4 us  [per_device(): lax.all_to_all(expert_out.reshape(N_TP * ranks_ep, CAP, N_DP * cols), ('t...]
    all_to_all x0 -> x1, starting transfers between devices: none -> 4.13 us  [per_device(): lax.all_to_all(hidden, 'tp', split_axis=0, concat_axis=0, tiled=True)]
  transfers between devices with their start and end apart: 23 -> 20, of which waited for: 14 -> 12; matrix products, arithmetic and copies ran while one was open for 0% -> 2% of each run, Pallas kernels for 6% -> 7%
where the time goes in v3:
time: 167 us; the launch traced here: 165 us
  starting transfers between devices  91.4 us (55%)
  waiting for transfers between devices  44.1 us (26%)
  Pallas kernels  18.5 us (11%)
  local copies, waits for them, and re-layouts  7.11 us (4%)
  between operations  3.04 us (2%)
    ppermute x9, starting transfers between devices, swap(): return lax.ppermute(x, 'dp', [(i, i ^ bit) for i in range(N_DP)])  29.2 us
    ppermute x9, waiting for transfers between devices, swap(): return lax.ppermute(x, 'dp', [(i, i ^ bit) for i in range(N_DP)])  27.3 us
    ppermute x8, starting transfers between devices, shift(): return lax.ppermute(x, 'tp', [(i, (i + k) % N_TP) for i in range(N_TP)])  26.6 us
    all_to_all x1, starting transfers between devices, per_device(): lax.all_to_all(sent.reshape(ranks_ep, CAP * 4, quarter), 'ep', split_axis...  17 us
    all_to_all x1, starting transfers between devices, per_device(): lax.all_to_all(expert_out.reshape(N_TP * ranks_ep, CAP, N_DP * cols), ('t...  14.4 us
    ppermute x8, waiting for transfers between devices, shift(): return lax.ppermute(x, 'tp', [(i, (i + k) % N_TP) for i in range(N_TP)])  13.2 us
    pallas_call x1, Pallas kernels, per_device(): pl.pallas_call(hidden_kernel, out_shape=jax.ShapeDtypeStruct((N_TP, rows,...  7.65 us
    unnamed x47, local copies, waits for them, and re-layouts  4.4 us
  transfers between devices with their start and end apart: 20, of which 12 were waited for; matrix products, arithmetic and copies ran while one was open for 2% of the time, Pallas kernels for 7%

profile of v3, /device:TPU:1, one launch (start us, length us, event | category | flops | bytes accessed | tf_op | source)
XLA Modules:
  0.0 164.9 jit_solution(13717786051881674493)
XLA Ops:
  3.2 17.0 %all-to-all-start = ((bf16[32,8,896]{2,1,0:T(8,128)(2,1)}), bf16[32,8,896]{2,1,0:T(8,128)(2,1)S(1)}, u32[]{:S(2)}, u32[]{:S(2)}) async-start(bf16[32,8,896]{2,1,0:T(8,128)(2,1)} %bitcast.33), calls=%async_computation | async-start | bytes 917504 | tf_op jit(solution)/shard_map/all_to_all | solution.py:322
  22.6 4.3 %collective-permute-start.3 = (bf16[7168,128]{1,0:T(8,128)(2,1)}, bf16[7168,128]{1,0:T(8,128)(2,1)}, u32[]{:S(2)}, u32[]{:S(2)}) collective-permute-start(bf16[7168,128]{1,0:T(8,128)(2,1)} %constant_dynamic-update-slice_fusion.w0), channel_id=1, source_target_pairs={{0,256},{128,384},{256,0},{384,128},{1,257},{129,385},{257,1},{385... | collective-permute-start | bytes 5505032 | tf_op jit(solution)/shard_map/ppermute | solution.py:279
  27.0 3.1 %collective-permute-start.4 = (bf16[7168,128]{1,0:T(8,128)(2,1)}, bf16[7168,128]{1,0:T(8,128)(2,1)}, u32[]{:S(2)}, u32[]{:S(2)}) collective-permute-start(bf16[7168,128]{1,0:T(8,128)(2,1)} %constant_dynamic-update-slice_fusion.w0), channel_id=1, source_target_pairs={{0,128},{128,0},{256,384},{384,256},{1,129},{129,1},{257,385},{385... | collective-permute-start | bytes 5505032 | tf_op jit(solution)/shard_map/ppermute | solution.py:279
  32.1 3.2 %collective-permute-start.2 = (bf16[96,576]{1,0:T(8,128)(2,1)S(1)}, bf16[96,576]{1,0:T(8,128)(2,1)S(1)}, u32[]{:S(2)}, u32[]{:S(2)}) collective-permute-start(bf16[96,576]{1,0:T(8,128)(2,1)S(1)} %bitcast.22), channel_id=1, source_target_pairs={{0,32},{32,64},{64,96},{96,0},{1,33},{33,65},{65,97},{97,1},{2,34}... | collective-permute-start | bytes 331784 | tf_op jit(solution)/shard_map/ppermute | solution.py:275
  35.3 2.7 %collective-permute-start.1 = (bf16[1152,128]{1,0:T(8,128)(2,1)S(1)}, bf16[1152,128]{1,0:T(8,128)(2,1)S(1)}, u32[]{:S(2)}, u32[]{:S(2)}) collective-permute-start(bf16[1152,128]{1,0:T(8,128)(2,1)S(1)} %bitcast.25), channel_id=1, source_target_pairs={{0,128},{128,0},{256,384},{384,256},{1,129},{129,1},{257,385},{385... | collective-permute-start | bytes 884744 | tf_op jit(solution)/shard_map/ppermute | solution.py:279
  41.3 3.4 %collective-permute-start.5 = (bf16[192,576]{1,0:T(8,128)(2,1)}, bf16[192,576]{1,0:T(8,128)(2,1)S(1)}, u32[]{:S(2)}, u32[]{:S(2)}) collective-permute-start(bf16[192,576]{1,0:T(8,128)(2,1)} %pad_maximum_fusion), channel_id=1, source_target_pairs={{0,64},{32,96},{64,0},{96,32},{1,65},{33,97},{65,1},{97,33},{2,66}... | collective-permute-start | bytes 663560 | tf_op jit(solution)/shard_map/ppermute | solution.py:275
  48.0 3.2 %collective-permute-start.6 = (bf16[256,896]{1,0:T(8,128)(2,1)S(1)}, bf16[256,896]{1,0:T(8,128)(2,1)S(1)}, u32[]{:S(2)}, u32[]{:S(2)}) collective-permute-start(bf16[256,896]{1,0:T(8,128)(2,1)S(1)} %bitcast.34), channel_id=1, source_target_pairs={{0,32},{32,64},{64,96},{96,0},{1,33},{33,65},{65,97},{97,1},{2,34}... | collective-permute-start | bytes 1376264 | tf_op jit(solution)/shard_map/ppermute | solution.py:275
  51.2 4.5 %collective-permute-start.7 = (bf16[256,896]{1,0:T(8,128)(2,1)S(1)}, bf16[256,896]{1,0:T(8,128)(2,1)S(1)}, u32[]{:S(2)}, u32[]{:S(2)}) collective-permute-start(bf16[256,896]{1,0:T(8,128)(2,1)S(1)} %bitcast.35), channel_id=1, source_target_pairs={{0,64},{32,96},{64,0},{96,32},{1,65},{33,97},{65,1},{97,33},{2,66}... | collective-permute-start | bytes 1376264 | tf_op jit(solution)/shard_map/ppermute | solution.py:275
  55.8 3.0 %collective-permute-start.8 = (bf16[256,896]{1,0:T(8,128)(2,1)S(1)}, bf16[256,896]{1,0:T(8,128)(2,1)S(1)}, u32[]{:S(2)}, u32[]{:S(2)}) collective-permute-start(bf16[256,896]{1,0:T(8,128)(2,1)S(1)} %bitcast.36), channel_id=1, source_target_pairs={{0,96},{32,0},{64,32},{96,64},{1,97},{33,1},{65,33},{97,65},{2,98}... | collective-permute-start | bytes 1376264 | tf_op jit(solution)/shard_map/ppermute | solution.py:275
  58.8 12.8 %collective-permute-done.3.w2 = bf16[7168,128]{1,0:T(8,128)(2,1)} collective-permute-done((bf16[7168,128]{1,0:T(8,128)(2,1)}, bf16[7168,128]{1,0:T(8,128)(2,1)}, u32[]{:S(2)}, u32[]{:S(2)}) %collective-permute-start.3) | collective-permute-done | bytes 1835040 | tf_op jit(solution)/shard_map/ppermute | solution.py:279
  75.0 3.5 %collective-permute-start.9 = (bf16[7168,128]{1,0:T(8,128)(2,1)}, bf16[7168,128]{1,0:T(8,128)(2,1)S(1)}, u32[]{:S(2)}, u32[]{:S(2)}) collective-permute-start(bf16[7168,128]{1,0:T(8,128)(2,1)} %collective-permute-done.3.w2), channel_id=1, source_target_pairs={{0,128},{128,0},{256,384},{384,256},{1,129},{129,1},{257,385},{385... | collective-permute-start | bytes 5505032 | tf_op jit(solution)/shard_map/ppermute | solution.py:279
  78.4 4.4 %collective-permute-start.15 = (bf16[224,2048]{1,0:T(8,128)(2,1)S(1)}, bf16[224,2048]{1,0:T(8,128)(2,1)}, u32[]{:S(2)}, u32[]{:S(2)}) collective-permute-start(bf16[224,2048]{1,0:T(8,128)(2,1)S(1)} %bitcast.19), channel_id=1, source_target_pairs={{0,256},{128,384},{256,0},{384,128},{1,257},{129,385},{257,1},{385... | collective-permute-start | bytes 2752520 | tf_op jit(solution)/shard_map/ppermute | solution.py:279
  84.1 7.7 %shard_map.150 = bf16[4,256,512]{2,1,0:T(8,128)(2,1)} custom-call(s32[5]{0:T(128)} %stack.11.where_ref, bf16[256,896]{1,0:T(8,128)(2,1)} %bitcast.37, bf16[256,896]{1,0:T(8,128)(2,1)} %copy-done.20, bf16[256,896]{1,0:T(8,128)(2,1)} %copy-done.21, bf16[256,896]{1,0:T(8,128)(2,1)} %copy-done.22, bf16[7168,128]{1,0:T(8,128)(2,1)} %constant_dynamic-update-slice_fusion.w0, ...), custom_call_target="tpu_custom_call" | custom-call | tf_op jit(solution)/shard_map/pallas_call | solution.py:347
  91.8 4.1 %all-to-all-start.1 = ((bf16[4,256,512]{2,1,0:T(8,128)(2,1)}), bf16[4,256,512]{2,1,0:T(8,128)(2,1)S(1)}, u32[]{:S(2)}, u32[]{:S(2)}) async-start(bf16[4,256,512]{2,1,0:T(8,128)(2,1)} %shard_map.150), calls=%async_computation.1 | async-start | bytes 2097152 | tf_op jit(solution)/shard_map/all_to_all | solution.py:362
  95.9 3.5 %collective-permute-start.10 = (bf16[1152,128]{1,0:T(8,128)(2,1)S(1)}, bf16[1152,128]{1,0:T(8,128)(2,1)}, u32[]{:S(2)}, u32[]{:S(2)}) collective-permute-start(bf16[1152,128]{1,0:T(8,128)(2,1)S(1)} %bitcast.26), channel_id=1, source_target_pairs={{0,256},{128,384},{256,0},{384,128},{1,257},{129,385},{257,1},{385... | collective-permute-start | bytes 884744 | tf_op jit(solution)/shard_map/ppermute | solution.py:279
  99.4 10.8 %collective-permute-done.10.m2 = bf16[1152,128]{1,0:T(8,128)(2,1)} collective-permute-done((bf16[1152,128]{1,0:T(8,128)(2,1)S(1)}, bf16[1152,128]{1,0:T(8,128)(2,1)}, u32[]{:S(2)}, u32[]{:S(2)}) %collective-permute-start.10) | collective-permute-done | bytes 294944 | tf_op jit(solution)/shard_map/ppermute | solution.py:279
  110.6 3.2 %collective-permute-start.16 = (bf16[224,2048]{1,0:T(8,128)(2,1)}, bf16[224,2048]{1,0:T(8,128)(2,1)S(1)}, u32[]{:S(2)}, u32[]{:S(2)}) collective-permute-start(bf16[224,2048]{1,0:T(8,128)(2,1)} %collective-permute-done.15.d2), channel_id=1, source_target_pairs={{0,128},{128,0},{256,384},{384,256},{1,129},{129,1},{257,385},{385... | collective-permute-start | bytes 2752520 | tf_op jit(solution)/shard_map/ppermute | solution.py:279
  116.1 3.5 %shard_map.153 = bf16[256,896]{1,0:T(8,128)(2,1)S(1)} custom-call(s32[5]{0:T(128)S(1)} %copy-done.11, bf16[4,256,512]{2,1,0:T(8,128)(2,1)S(1)} %all-to-all-done.1.parts, bf16[224,2048]{1,0:T(8,128)(2,1)S(1)} %bitcast.20, bf16[224,2048]{1,0:T(8,128)(2,1)S(1)} %collective-permute-done.d1, bf16[224,2048]{1,0:T(8,128)(2,1)} %collective-permute-done.15.d2, ...), custom_call_target="tpu_custom_call" | custom-call | tf_op jit(solution)/shard_map/pallas_call | solution.py:366
  120.6 14.4 %all-to-all-start.2 = ((bf16[128,2,896]{2,1,0:T(2,128)(2,1)}), bf16[128,2,896]{2,1,0:T(2,128)(2,1)S(1)}, u32[]{:S(2)}, u32[]{:S(2)}) async-start(bf16[128,2,896]{2,1,0:T(2,128)(2,1)} %reshape.38), calls=%async_computation.2 | async-start | bytes 917504 | tf_op jit(solution)/shard_map/all_to_all | solution.py:378
  140.0 2.8 %shard_map.151 = (bf16[96,640]{1,0:T(8,128)(2,1)S(1)}, bf16[96,640]{1,0:T(8,128)(2,1)S(1)}, bf16[96,640]{1,0:T(8,128)(2,1)S(1)}, bf16[96,640]{1,0:T(8,128)(2,1)S(1)}) custom-call(s32[5]{0:T(128)S(1)} %copy-done.11, s32[6]{0:T(128)S(1)} %bitcast.31, s32[3]{0:T(128)S(1)} %bitcast.32, bf16[96,576]{1,0:T(8,128)(2,1)S(1)} %bitcast.24, ...), custom_call_target="tpu_custom_call" | custom-call | tf_op jit(solution)/shard_map/pallas_call | solution.py:387
  142.8 4.5 %collective-permute-start.12 = (bf16[96,640]{1,0:T(8,128)(2,1)S(1)}, bf16[96,640]{1,0:T(8,128)(2,1)S(1)}, u32[]{:S(2)}, u32[]{:S(2)}) collective-permute-start(bf16[96,640]{1,0:T(8,128)(2,1)S(1)} %get-tuple-element.45), channel_id=1, source_target_pairs={{0,96},{32,0},{64,32},{96,64},{1,97},{33,1},{65,33},{97,65},{2,98}... | collective-permute-start | bytes 368648 | tf_op jit(solution)/shard_map/ppermute | solution.py:275
  149.4 2.7 %collective-permute-start.14 = (bf16[96,640]{1,0:T(8,128)(2,1)S(1)}, bf16[96,640]{1,0:T(8,128)(2,1)S(1)}, u32[]{:S(2)}, u32[]{:S(2)}) collective-permute-start(bf16[96,640]{1,0:T(8,128)(2,1)S(1)} %get-tuple-element.47), channel_id=1, source_target_pairs={{0,32},{32,64},{64,96},{96,0},{1,33},{33,65},{65,97},{97,1},{2,34}... | collective-permute-start | bytes 368648 | tf_op jit(solution)/shard_map/ppermute | solution.py:275
  152.1 4.1 %collective-permute-done.13.p2 = bf16[96,640]{1,0:T(8,128)(2,1)S(1)} collective-permute-done((bf16[96,640]{1,0:T(8,128)(2,1)S(1)}, bf16[96,640]{1,0:T(8,128)(2,1)S(1)}, u32[]{:S(2)}, u32[]{:S(2)}) %collective-permute-start.13) | collective-permute-done | bytes 122912 | tf_op jit(solution)/shard_map/ppermute | solution.py:275
  156.2 3.9 %collective-permute-done.14.p3 = bf16[96,640]{1,0:T(8,128)(2,1)S(1)} collective-permute-done((bf16[96,640]{1,0:T(8,128)(2,1)S(1)}, bf16[96,640]{1,0:T(8,128)(2,1)S(1)}, u32[]{:S(2)}, u32[]{:S(2)}) %collective-permute-start.14) | collective-permute-done | bytes 122912 | tf_op jit(solution)/shard_map/ppermute | solution.py:275
  (74 shorter events, 31.4 us)
Async XLA Ops:
  3.2 44.9 %all-to-all-start = ((bf16[32,8,896]{2,1,0:T(8,128)(2,1)}), bf16[32,8,896]{2,1,0:T(8,128)(2,1)S(1)}, u32[]{:S(2)}, u32[]{:S(2)}) async-start(bf16[32,8,896]{2,1,0:T(8,128)(2,1)} %bitcast.33), calls=%async_computation | async-start | bytes 917504 | tf_op jit(solution)/shard_map/all_to_all | solution.py:322
  22.6 49.0 %collective-permute-start.3 = (bf16[7168,128]{1,0:T(8,128)(2,1)}, bf16[7168,128]{1,0:T(8,128)(2,1)}, u32[]{:S(2)}, u32[]{:S(2)}) collective-permute-start(bf16[7168,128]{1,0:T(8,128)(2,1)} %constant_dynamic-update-slice_fusion.w0), channel_id=1, source_target_pairs={{0,256},{128,384},{256,0},{384,128},{1,257},{129,385},{257,1},{385... | collective-permute-start | bytes 5505032 | tf_op jit(solution)/shard_map/ppermute | solution.py:279
  27.0 44.6 %collective-permute-start.4 = (bf16[7168,128]{1,0:T(8,128)(2,1)}, bf16[7168,128]{1,0:T(8,128)(2,1)}, u32[]{:S(2)}, u32[]{:S(2)}) collective-permute-start(bf16[7168,128]{1,0:T(8,128)(2,1)} %constant_dynamic-update-slice_fusion.w0), channel_id=1, source_target_pairs={{0,128},{128,0},{256,384},{384,256},{1,129},{129,1},{257,385},{385... | collective-permute-start | bytes 5505032 | tf_op jit(solution)/shard_map/ppermute | solution.py:279
  30.2 17.1 %collective-permute-start = (bf16[224,2048]{1,0:T(8,128)(2,1)S(1)}, bf16[224,2048]{1,0:T(8,128)(2,1)S(1)}, u32[]{:S(2)}, u32[]{:S(2)}) collective-permute-start(bf16[224,2048]{1,0:T(8,128)(2,1)S(1)} %bitcast.18), channel_id=1, source_target_pairs={{0,128},{128,0},{256,384},{384,256},{1,129},{129,1},{257,385},{385... | collective-permute-start | bytes 2752520 | tf_op jit(solution)/shard_map/ppermute | solution.py:279
  32.1 7.7 %collective-permute-start.2 = (bf16[96,576]{1,0:T(8,128)(2,1)S(1)}, bf16[96,576]{1,0:T(8,128)(2,1)S(1)}, u32[]{:S(2)}, u32[]{:S(2)}) collective-permute-start(bf16[96,576]{1,0:T(8,128)(2,1)S(1)} %bitcast.22), channel_id=1, source_target_pairs={{0,32},{32,64},{64,96},{96,0},{1,33},{33,65},{65,97},{97,1},{2,34}... | collective-permute-start | bytes 331784 | tf_op jit(solution)/shard_map/ppermute | solution.py:275
  35.3 12.0 %collective-permute-start.1 = (bf16[1152,128]{1,0:T(8,128)(2,1)S(1)}, bf16[1152,128]{1,0:T(8,128)(2,1)S(1)}, u32[]{:S(2)}, u32[]{:S(2)}) collective-permute-start(bf16[1152,128]{1,0:T(8,128)(2,1)S(1)} %bitcast.25), channel_id=1, source_target_pairs={{0,128},{128,0},{256,384},{384,256},{1,129},{129,1},{257,385},{385... | collective-permute-start | bytes 884744 | tf_op jit(solution)/shard_map/ppermute | solution.py:279
  41.3 14.5 %collective-permute-start.5 = (bf16[192,576]{1,0:T(8,128)(2,1)}, bf16[192,576]{1,0:T(8,128)(2,1)S(1)}, u32[]{:S(2)}, u32[]{:S(2)}) collective-permute-start(bf16[192,576]{1,0:T(8,128)(2,1)} %pad_maximum_fusion), channel_id=1, source_target_pairs={{0,64},{32,96},{64,0},{96,32},{1,65},{33,97},{65,1},{97,33},{2,66}... | collective-permute-start | bytes 663560 | tf_op jit(solution)/shard_map/ppermute | solution.py:275
  47.3 44.5 %copy-start.7 = (bf16[1152,128]{1,0:T(8,128)(2,1)}, bf16[1152,128]{1,0:T(8,128)(2,1)S(1)}, u32[]{:S(2)}) copy-start(bf16[1152,128]{1,0:T(8,128)(2,1)S(1)} %collective-permute-done.1.m1) | copy-start | bytes 884740
  48.0 34.8 %copy-start.17 = (bf16[32,8,896]{2,1,0:T(8,128)(2,1)}, bf16[32,8,896]{2,1,0:T(8,128)(2,1)S(1)}, u32[]{:S(2)}) copy-start(bf16[32,8,896]{2,1,0:T(8,128)(2,1)S(1)} %all-to-all-done) | copy-start | bytes 1376260
  48.0 23.6 %collective-permute-start.6 = (bf16[256,896]{1,0:T(8,128)(2,1)S(1)}, bf16[256,896]{1,0:T(8,128)(2,1)S(1)}, u32[]{:S(2)}, u32[]{:S(2)}) collective-permute-start(bf16[256,896]{1,0:T(8,128)(2,1)S(1)} %bitcast.34), channel_id=1, source_target_pairs={{0,32},{32,64},{64,96},{96,0},{1,33},{33,65},{65,97},{97,1},{2,34}... | collective-permute-start | bytes 1376264 | tf_op jit(solution)/shard_map/ppermute | solution.py:275
  51.2 21.4 %collective-permute-start.7 = (bf16[256,896]{1,0:T(8,128)(2,1)S(1)}, bf16[256,896]{1,0:T(8,128)(2,1)S(1)}, u32[]{:S(2)}, u32[]{:S(2)}) collective-permute-start(bf16[256,896]{1,0:T(8,128)(2,1)S(1)} %bitcast.35), channel_id=1, source_target_pairs={{0,64},{32,96},{64,0},{96,32},{1,65},{33,97},{65,1},{97,33},{2,66}... | collective-permute-start | bytes 1376264 | tf_op jit(solution)/shard_map/ppermute | solution.py:275
  55.8 36.0 %copy-start.9 = (bf16[192,576]{1,0:T(8,128)(2,1)}, bf16[192,576]{1,0:T(8,128)(2,1)S(1)}, u32[]{:S(2)}) copy-start(bf16[192,576]{1,0:T(8,128)(2,1)S(1)} %collective-permute-done.5.far) | copy-start | bytes 663556
  55.8 19.2 %collective-permute-start.8 = (bf16[256,896]{1,0:T(8,128)(2,1)S(1)}, bf16[256,896]{1,0:T(8,128)(2,1)S(1)}, u32[]{:S(2)}, u32[]{:S(2)}) collective-permute-start(bf16[256,896]{1,0:T(8,128)(2,1)S(1)} %bitcast.36), channel_id=1, source_target_pairs={{0,96},{32,0},{64,32},{96,64},{1,97},{33,1},{65,33},{97,65},{2,98}... | collective-permute-start | bytes 1376264 | tf_op jit(solution)/shard_map/ppermute | solution.py:275
  75.0 7.8 %collective-permute-start.9 = (bf16[7168,128]{1,0:T(8,128)(2,1)}, bf16[7168,128]{1,0:T(8,128)(2,1)S(1)}, u32[]{:S(2)}, u32[]{:S(2)}) collective-permute-start(bf16[7168,128]{1,0:T(8,128)(2,1)} %collective-permute-done.3.w2), channel_id=1, source_target_pairs={{0,128},{128,0},{256,384},{384,256},{1,129},{129,1},{257,385},{385... | collective-permute-start | bytes 5505032 | tf_op jit(solution)/shard_map/ppermute | solution.py:279
  78.4 32.2 %collective-permute-start.15 = (bf16[224,2048]{1,0:T(8,128)(2,1)S(1)}, bf16[224,2048]{1,0:T(8,128)(2,1)}, u32[]{:S(2)}, u32[]{:S(2)}) collective-permute-start(bf16[224,2048]{1,0:T(8,128)(2,1)S(1)} %bitcast.19), channel_id=1, source_target_pairs={{0,256},{128,384},{256,0},{384,128},{1,257},{129,385},{257,1},{385... | collective-permute-start | bytes 2752520 | tf_op jit(solution)/shard_map/ppermute | solution.py:279
  91.8 24.4 %copy-start.11 = (s32[5]{0:T(128)S(1)}, s32[5]{0:T(128)}, u32[]{:S(2)}) copy-start(s32[5]{0:T(128)} %stack.11.where_ref) | copy-start | bytes 64
  91.8 18.9 %all-to-all-start.1 = ((bf16[4,256,512]{2,1,0:T(8,128)(2,1)}), bf16[4,256,512]{2,1,0:T(8,128)(2,1)S(1)}, u32[]{:S(2)}, u32[]{:S(2)}) async-start(bf16[4,256,512]{2,1,0:T(8,128)(2,1)} %shard_map.150), calls=%async_computation.1 | async-start | bytes 2097152 | tf_op jit(solution)/shard_map/all_to_all | solution.py:362
  95.9 14.3 %collective-permute-start.10 = (bf16[1152,128]{1,0:T(8,128)(2,1)S(1)}, bf16[1152,128]{1,0:T(8,128)(2,1)}, u32[]{:S(2)}, u32[]{:S(2)}) collective-permute-start(bf16[1152,128]{1,0:T(8,128)(2,1)S(1)} %bitcast.26), channel_id=1, source_target_pairs={{0,256},{128,384},{256,0},{384,128},{1,257},{129,385},{257,1},{385... | collective-permute-start | bytes 884744 | tf_op jit(solution)/shard_map/ppermute | solution.py:279
  110.6 5.5 %collective-permute-start.16 = (bf16[224,2048]{1,0:T(8,128)(2,1)}, bf16[224,2048]{1,0:T(8,128)(2,1)S(1)}, u32[]{:S(2)}, u32[]{:S(2)}) collective-permute-start(bf16[224,2048]{1,0:T(8,128)(2,1)} %collective-permute-done.15.d2), channel_id=1, source_target_pairs={{0,128},{128,0},{256,384},{384,256},{1,129},{129,1},{257,385},{385... | collective-permute-start | bytes 2752520 | tf_op jit(solution)/shard_map/ppermute | solution.py:279
  120.6 42.9 %all-to-all-start.2 = ((bf16[128,2,896]{2,1,0:T(2,128)(2,1)}), bf16[128,2,896]{2,1,0:T(2,128)(2,1)S(1)}, u32[]{:S(2)}, u32[]{:S(2)}) async-start(bf16[128,2,896]{2,1,0:T(2,128)(2,1)} %reshape.38), calls=%async_computation.2 | async-start | bytes 917504 | tf_op jit(solution)/shard_map/all_to_all | solution.py:378
  135.1 4.0 %collective-permute-start.11 = (bf16[1152,128]{1,0:T(8,128)(2,1)}, bf16[1152,128]{1,0:T(8,128)(2,1)S(1)}, u32[]{:S(2)}, u32[]{:S(2)}) collective-permute-start(bf16[1152,128]{1,0:T(8,128)(2,1)} %collective-permute-done.10.m2), channel_id=1, source_target_pairs={{0,128},{128,0},{256,384},{384,256},{1,129},{129,1},{257,385},{385... | collective-permute-start | bytes 884744 | tf_op jit(solution)/shard_map/ppermute | solution.py:279
  142.8 9.3 %collective-permute-start.12 = (bf16[96,640]{1,0:T(8,128)(2,1)S(1)}, bf16[96,640]{1,0:T(8,128)(2,1)S(1)}, u32[]{:S(2)}, u32[]{:S(2)}) collective-permute-start(bf16[96,640]{1,0:T(8,128)(2,1)S(1)} %get-tuple-element.45), channel_id=1, source_target_pairs={{0,96},{32,0},{64,32},{96,64},{1,97},{33,1},{65,33},{97,65},{2,98}... | collective-permute-start | bytes 368648 | tf_op jit(solution)/shard_map/ppermute | solution.py:275
  147.3 8.9 %collective-permute-start.13 = (bf16[96,640]{1,0:T(8,128)(2,1)S(1)}, bf16[96,640]{1,0:T(8,128)(2,1)S(1)}, u32[]{:S(2)}, u32[]{:S(2)}) collective-permute-start(bf16[96,640]{1,0:T(8,128)(2,1)S(1)} %get-tuple-element.46), channel_id=1, source_target_pairs={{0,64},{32,96},{64,0},{96,32},{1,65},{33,97},{65,1},{97,33},{2,66}... | collective-permute-start | bytes 368648 | tf_op jit(solution)/shard_map/ppermute | solution.py:275
  149.4 10.8 %collective-permute-start.14 = (bf16[96,640]{1,0:T(8,128)(2,1)S(1)}, bf16[96,640]{1,0:T(8,128)(2,1)S(1)}, u32[]{:S(2)}, u32[]{:S(2)}) collective-permute-start(bf16[96,640]{1,0:T(8,128)(2,1)S(1)} %get-tuple-element.47), channel_id=1, source_target_pairs={{0,32},{32,64},{64,96},{96,0},{1,33},{33,65},{65,97},{97,1},{2,34}... | collective-permute-start | bytes 368648 | tf_op jit(solution)/shard_map/ppermute | solution.py:275
  (19 other events, 249.5 us)

commit v4 on v3

--- a/solution.py
+++ b/solution.py
@@ -73,49 +73,34 @@
     out_ref[...] = total.astype(bf16)
 
 
-def hidden_kernel(
-    where_ref, b0, b1, b2, b3, w0, w1, w2, w3, out_ref, rows_ref, weights, sems,
-    held, block_sems,
-):
+def hidden_kernel(where_ref, b0, b1, b2, b3, w0, w1, w2, w3, out_ref, rows_ref):
     rank_dp, rank_tp = where_ref[0], where_ref[1]
     depth, part = w0.shape[0] // 2, w0.shape[1]
-    landing = []
-    for k, b in enumerate((b0, b1, b2, b3)):
-        copy = pltpu.make_async_copy(b, held.at[k], block_sems.at[k])
-        copy.start()
-        landing.append(copy)
-    copies = []
-    for rel, w in enumerate((w0, w1, w2, w3)):
-        slot = rank_dp ^ rel
-        for half in range(2):
-            copy = pltpu.make_async_copy(
-                w.at[pl.ds(half * depth, depth), :],
-                weights.at[slot, :, pl.ds(half * part, part)],
-                sems.at[rel, half],
-            )
-            copy.start()
-            copies.append(copy)
     count, quarter = b0.shape
     slots = count // 4
-    for k in range(N_TP):
+    for k, b in enumerate((b0, b1, b2, b3)):
         base = pl.multiple_of(((rank_tp + N_TP - k) % N_TP) * slots, slots)
-        landing[k].wait()
-        block = held[k]
+        block = b[...]
+        row = iota((count, count), 0)
+        pick = jnp.where(
+            iota((count, count), 1) == (row % slots) * 4 + row // slots, 1.0, 0.0
+        ).astype(bf16)
+        sorted_rows = jnp.dot(pick, block, preferred_element_type=f32).astype(bf16)
         for q in range(4):
-            pick = jnp.where(
-                iota((slots, count), 1) == iota((slots, count), 0) * 4 + q, 1.0, 0.0
-            ).astype(bf16)
-            rows_ref[pl.ds(base, slots), q * quarter : (q + 1) * quarter] = jnp.dot(
-                pick, block, preferred_element_type=f32
-            ).astype(bf16)
-    for copy in copies:
-        copy.wait()
-    for i in range(N_DP):
-        both = jnp.dot(rows_ref[...], weights[i], preferred_element_type=f32)
+            rows_ref[pl.ds(base, slots), q * quarter : (q + 1) * quarter] = sorted_rows[
+                q * slots : (q + 1) * slots
+            ]
+    for rel, w in enumerate((w0, w1, w2, w3)):
+        both = jnp.dot(
+            rows_ref[...],
+            jnp.concatenate([w[:depth, :], w[depth:, :]], axis=1),
+            preferred_element_type=f32,
+        )
         gate, up = both[:, :part], both[:, part:]
-        hidden = gate / (1.0 + jnp.exp(-gate)) * up
+        hidden = (gate / (1.0 + jnp.exp(-gate)) * up).astype(bf16)
+        base = pl.multiple_of((rank_dp ^ rel) * part, part)
         for copy in range(out_ref.shape[0]):
-            out_ref[copy, :, i * part : (i + 1) * part] = hidden.astype(bf16)
+            out_ref[copy, :, pl.ds(base, part)] = hidden
 
 
 def down_kernel(where_ref, parts, d0, d1, d2, d3, out_ref, hidden, weights, sems):
@@ -347,16 +332,10 @@
     hidden = pl.pallas_call(
         hidden_kernel,
         out_shape=jax.ShapeDtypeStruct((N_TP, rows, N_DP * part), bf16),
-        in_specs=[SMEM] + [ANY] * 8,
+        in_specs=[SMEM] + [VMEM] * 8,
         out_specs=VMEM,
-        scratch_shapes=[
-            pltpu.VMEM((rows, width), bf16),
-            pltpu.VMEM((N_DP, width, 2 * part), bf16),
-            pltpu.SemaphoreType.DMA((N_DP, 2)),
-            pltpu.VMEM((N_TP,) + arrived.shape, bf16),
-            pltpu.SemaphoreType.DMA((N_TP,)),
-        ],
-        compiler_params=params(58),
+        scratch_shapes=[pltpu.VMEM((rows, width), bf16)],
+        compiler_params=params(24),
     )(where, arrived, *blocks, first, first_c, first_x, first_xc)
     pages_x = swap(after((pages, hidden))[0], 2)
     hiddens = [lax.all_to_all(hidden, "tp", split_axis=0, concat_axis=0, tiled=True)]

time: 167 us -> 165 us (0.988)
  waiting for transfers between devices: 44.1 us -> 49.2 us
  local copies, waits for them, and re-layouts: 7.11 us -> 2.79 us
  starting transfers between devices: 91.4 us -> 89.7 us
    unnamed x47 -> x17, local copies, waits for them, and re-layouts: 4.4 us -> 1.46 us
    all_to_all x1, waiting for transfers between devices: 0.75 us -> 2.87 us  [per_device(): lax.all_to_all(sent.reshape(ranks_ep, CAP * 4, quarter), 'ep', split_axis...]
    pallas_call x1, Pallas kernels: 7.65 us -> 5.92 us  [per_device(): pl.pallas_call(hidden_kernel, out_shape=jax.ShapeDtypeStruct((N_TP, rows,...]
  transfers between devices with their start and end apart: 20 -> 20, of which waited for: 12 -> 11; matrix products, arithmetic and copies ran while one was open for 2% -> 1% of each run, Pallas kernels for 7% -> 6%
where the time goes in v4:
time: 165 us; the launch traced here: 163 us
  starting transfers between devices  89.7 us (54%)
  waiting for transfers between devices  49.2 us (30%)
  Pallas kernels  17.3 us (10%)
  between operations  2.89 us (2%)
  local copies, waits for them, and re-layouts  2.79 us (2%)
    ppermute x9, starting transfers between devices, swap(): return lax.ppermute(x, 'dp', [(i, i ^ bit) for i in range(N_DP)])  28.8 us
    ppermute x9, waiting for transfers between devices, swap(): return lax.ppermute(x, 'dp', [(i, i ^ bit) for i in range(N_DP)])  28.5 us
    ppermute x8, starting transfers between devices, shift(): return lax.ppermute(x, 'tp', [(i, (i + k) % N_TP) for i in range(N_TP)])  26.6 us
    all_to_all x1, starting transfers between devices, per_device(): lax.all_to_all(sent.reshape(ranks_ep, CAP * 4, quarter), 'ep', split_axis...  17 us
    ppermute x8, waiting for transfers between devices, shift(): return lax.ppermute(x, 'tp', [(i, (i + k) % N_TP) for i in range(N_TP)])  14.7 us
    all_to_all x1, starting transfers between devices, per_device(): lax.all_to_all(expert_out.reshape(N_TP * ranks_ep, CAP, N_DP * cols), ('t...  13.2 us
    pallas_call x1, Pallas kernels, per_device(): pl.pallas_call(hidden_kernel, out_shape=jax.ShapeDtypeStruct((N_TP, rows,...  5.92 us
    all_to_all x1, starting transfers between devices, per_device(): lax.all_to_all(hidden, 'tp', split_axis=0, concat_axis=0, tiled=True)  4.11 us
  transfers between devices with their start and end apart: 20, of which 11 were waited for; matrix products, arithmetic and copies ran while one was open for 1% of the time, Pallas kernels for 6%

profile of v4, /device:TPU:1, one launch (start us, length us, event | category | flops | bytes accessed | tf_op | source)
XLA Modules:
  0.0 162.6 jit_solution(6522589063800315627)
XLA Ops:
  3.1 17.0 %all-to-all-start = ((bf16[32,8,896]{2,1,0:T(8,128)(2,1)}), bf16[32,8,896]{2,1,0:T(8,128)(2,1)S(1)}, u32[]{:S(2)}, u32[]{:S(2)}) async-start(bf16[32,8,896]{2,1,0:T(8,128)(2,1)} %bitcast.34), calls=%async_computation | async-start | bytes 917504 | tf_op jit(solution)/shard_map/all_to_all | solution.py:307
  21.6 4.4 %collective-permute-start.3 = (bf16[7168,128]{1,0:T(8,128)(2,1)S(1)}, bf16[7168,128]{1,0:T(8,128)(2,1)}, u32[]{:S(2)}, u32[]{:S(2)}) collective-permute-start(bf16[7168,128]{1,0:T(8,128)(2,1)S(1)} %constant_dynamic-update-slice_fusion.w0), channel_id=1, source_target_pairs={{0,256},{128,384},{256,0},{384,128},{1,257},{129,385},{257,1},{385... | collective-permute-start | bytes 5505032 | tf_op jit(solution)/shard_map/ppermute | solution.py:264
  26.0 3.1 %collective-permute-start.4 = (bf16[7168,128]{1,0:T(8,128)(2,1)S(1)}, bf16[7168,128]{1,0:T(8,128)(2,1)}, u32[]{:S(2)}, u32[]{:S(2)}) collective-permute-start(bf16[7168,128]{1,0:T(8,128)(2,1)S(1)} %constant_dynamic-update-slice_fusion.w0), channel_id=1, source_target_pairs={{0,128},{128,0},{256,384},{384,256},{1,129},{129,1},{257,385},{385... | collective-permute-start | bytes 5505032 | tf_op jit(solution)/shard_map/ppermute | solution.py:264
  31.1 3.2 %collective-permute-start.2 = (bf16[96,576]{1,0:T(8,128)(2,1)S(1)}, bf16[96,576]{1,0:T(8,128)(2,1)S(1)}, u32[]{:S(2)}, u32[]{:S(2)}) collective-permute-start(bf16[96,576]{1,0:T(8,128)(2,1)S(1)} %bitcast.26), channel_id=1, source_target_pairs={{0,32},{32,64},{64,96},{96,0},{1,33},{33,65},{65,97},{97,1},{2,34}... | collective-permute-start | bytes 331784 | tf_op jit(solution)/shard_map/ppermute | solution.py:260
  39.6 3.4 %collective-permute-start.5 = (bf16[192,576]{1,0:T(8,128)(2,1)}, bf16[192,576]{1,0:T(8,128)(2,1)}, u32[]{:S(2)}, u32[]{:S(2)}) collective-permute-start(bf16[192,576]{1,0:T(8,128)(2,1)} %pad_maximum_fusion), channel_id=1, source_target_pairs={{0,64},{32,96},{64,0},{96,32},{1,65},{33,97},{65,1},{97,33},{2,66}... | collective-permute-start | bytes 663560 | tf_op jit(solution)/shard_map/ppermute | solution.py:260
  45.1 2.9 %all-to-all-done = bf16[32,8,896]{2,1,0:T(8,128)(2,1)S(1)} async-done(((bf16[32,8,896]{2,1,0:T(8,128)(2,1)}), bf16[32,8,896]{2,1,0:T(8,128)(2,1)S(1)}, u32[]{:S(2)}, u32[]{:S(2)}) %all-to-all-start) | async-done | bytes 458784 | tf_op jit(solution)/shard_map/all_to_all | solution.py:307
  47.9 3.2 %collective-permute-start.6 = (bf16[256,896]{1,0:T(8,128)(2,1)S(1)}, bf16[256,896]{1,0:T(8,128)(2,1)S(1)}, u32[]{:S(2)}, u32[]{:S(2)}) collective-permute-start(bf16[256,896]{1,0:T(8,128)(2,1)S(1)} %bitcast.18), channel_id=1, source_target_pairs={{0,32},{32,64},{64,96},{96,0},{1,33},{33,65},{65,97},{97,1},{2,34}... | collective-permute-start | bytes 1376264 | tf_op jit(solution)/shard_map/ppermute | solution.py:260
  51.1 4.5 %collective-permute-start.7 = (bf16[256,896]{1,0:T(8,128)(2,1)S(1)}, bf16[256,896]{1,0:T(8,128)(2,1)S(1)}, u32[]{:S(2)}, u32[]{:S(2)}) collective-permute-start(bf16[256,896]{1,0:T(8,128)(2,1)S(1)} %bitcast.19), channel_id=1, source_target_pairs={{0,64},{32,96},{64,0},{96,32},{1,65},{33,97},{65,1},{97,33},{2,66}... | collective-permute-start | bytes 1376264 | tf_op jit(solution)/shard_map/ppermute | solution.py:260
  55.7 3.0 %collective-permute-start.8 = (bf16[256,896]{1,0:T(8,128)(2,1)S(1)}, bf16[256,896]{1,0:T(8,128)(2,1)S(1)}, u32[]{:S(2)}, u32[]{:S(2)}) collective-permute-start(bf16[256,896]{1,0:T(8,128)(2,1)S(1)} %bitcast.20), channel_id=1, source_target_pairs={{0,96},{32,0},{64,32},{96,64},{1,97},{33,1},{65,33},{97,65},{2,98}... | collective-permute-start | bytes 1376264 | tf_op jit(solution)/shard_map/ppermute | solution.py:260
  58.7 11.3 %collective-permute-done.3.w2 = bf16[7168,128]{1,0:T(8,128)(2,1)} collective-permute-done((bf16[7168,128]{1,0:T(8,128)(2,1)S(1)}, bf16[7168,128]{1,0:T(8,128)(2,1)}, u32[]{:S(2)}, u32[]{:S(2)}) %collective-permute-start.3) | collective-permute-done | bytes 1835040 | tf_op jit(solution)/shard_map/ppermute | solution.py:264
  74.8 3.5 %collective-permute-start.9 = (bf16[7168,128]{1,0:T(8,128)(2,1)}, bf16[7168,128]{1,0:T(8,128)(2,1)S(1)}, u32[]{:S(2)}, u32[]{:S(2)}) collective-permute-start(bf16[7168,128]{1,0:T(8,128)(2,1)} %collective-permute-done.3.w2), channel_id=1, source_target_pairs={{0,128},{128,0},{256,384},{384,256},{1,129},{129,1},{257,385},{385... | collective-permute-start | bytes 5505032 | tf_op jit(solution)/shard_map/ppermute | solution.py:264
  78.3 4.4 %collective-permute-start.15 = (bf16[224,2048]{1,0:T(8,128)(2,1)S(1)}, bf16[224,2048]{1,0:T(8,128)(2,1)}, u32[]{:S(2)}, u32[]{:S(2)}) collective-permute-start(bf16[224,2048]{1,0:T(8,128)(2,1)S(1)} %bitcast.23), channel_id=1, source_target_pairs={{0,256},{128,384},{256,0},{384,128},{1,257},{129,385},{257,1},{385... | collective-permute-start | bytes 2752520 | tf_op jit(solution)/shard_map/ppermute | solution.py:264
  82.7 5.9 %shard_map.150 = bf16[4,256,512]{2,1,0:T(8,128)(2,1)} custom-call(s32[5]{0:T(128)S(1)} %stack.11.where_ref, bf16[256,896]{1,0:T(8,128)(2,1)S(1)} %bitcast.21, bf16[256,896]{1,0:T(8,128)(2,1)S(1)} %collective-permute-done.6.b1, bf16[256,896]{1,0:T(8,128)(2,1)S(1)} %collective-permute-done.7.b2, bf16[256,896]{1,0:T(8,128)(2,1)S(1)} %collective-permute-done.8.b3, ...), custom_call_target="tpu_custom_call" | custom-call | tf_op jit(solution)/shard_map/pallas_call | solution.py:332
  88.6 4.1 %all-to-all-start.1 = ((bf16[4,256,512]{2,1,0:T(8,128)(2,1)}), bf16[4,256,512]{2,1,0:T(8,128)(2,1)S(1)}, u32[]{:S(2)}, u32[]{:S(2)}) async-start(bf16[4,256,512]{2,1,0:T(8,128)(2,1)} %shard_map.150), calls=%async_computation.1 | async-start | bytes 2097152 | tf_op jit(solution)/shard_map/all_to_all | solution.py:341
  92.7 3.6 %collective-permute-start.10 = (bf16[1152,128]{1,0:T(8,128)(2,1)}, bf16[1152,128]{1,0:T(8,128)(2,1)S(1)}, u32[]{:S(2)}, u32[]{:S(2)}) collective-permute-start(bf16[1152,128]{1,0:T(8,128)(2,1)} %bitcast.8.m0), channel_id=1, source_target_pairs={{0,256},{128,384},{256,0},{384,128},{1,257},{129,385},{257,1},{385... | collective-permute-start | bytes 884744 | tf_op jit(solution)/shard_map/ppermute | solution.py:264
  96.3 13.7 %collective-permute-done.10.m2 = bf16[1152,128]{1,0:T(8,128)(2,1)S(1)} collective-permute-done((bf16[1152,128]{1,0:T(8,128)(2,1)}, bf16[1152,128]{1,0:T(8,128)(2,1)S(1)}, u32[]{:S(2)}, u32[]{:S(2)}) %collective-permute-start.10) | collective-permute-done | bytes 294944 | tf_op jit(solution)/shard_map/ppermute | solution.py:264
  115.0 3.5 %shard_map.153 = bf16[256,896]{1,0:T(8,128)(2,1)S(1)} custom-call(s32[5]{0:T(128)S(1)} %stack.11.where_ref, bf16[4,256,512]{2,1,0:T(8,128)(2,1)S(1)} %all-to-all-done.1.parts, bf16[224,2048]{1,0:T(8,128)(2,1)S(1)} %bitcast.24, bf16[224,2048]{1,0:T(8,128)(2,1)} %collective-permute-done.d1, bf16[224,2048]{1,0:T(8,128)(2,1)} %collective-permute-done.15.d2, ...), custom_call_target="tpu_custom_call" | custom-call | tf_op jit(solution)/shard_map/pallas_call | solution.py:345
  119.5 13.2 %all-to-all-start.2 = ((bf16[128,2,896]{2,1,0:T(2,128)(2,1)}), bf16[128,2,896]{2,1,0:T(2,128)(2,1)S(1)}, u32[]{:S(2)}, u32[]{:S(2)}) async-start(bf16[128,2,896]{2,1,0:T(2,128)(2,1)} %reshape.38), calls=%async_computation.2 | async-start | bytes 917504 | tf_op jit(solution)/shard_map/all_to_all | solution.py:357
  136.5 3.4 %shard_map.151 = (bf16[96,640]{1,0:T(8,128)(2,1)S(1)}, bf16[96,640]{1,0:T(8,128)(2,1)S(1)}, bf16[96,640]{1,0:T(8,128)(2,1)S(1)}, bf16[96,640]{1,0:T(8,128)(2,1)S(1)}) custom-call(s32[5]{0:T(128)S(1)} %stack.11.where_ref, s32[6]{0:T(128)S(1)} %bitcast.32, s32[3]{0:T(128)S(1)} %bitcast.33, bf16[96,576]{1,0:T(8,128)(2,1)S(1)} %bitcast.28, ...), custom_call_target="tpu_custom_call" | custom-call | tf_op jit(solution)/shard_map/pallas_call | solution.py:366
  139.9 4.5 %collective-permute-start.12 = (bf16[96,640]{1,0:T(8,128)(2,1)S(1)}, bf16[96,640]{1,0:T(8,128)(2,1)S(1)}, u32[]{:S(2)}, u32[]{:S(2)}) collective-permute-start(bf16[96,640]{1,0:T(8,128)(2,1)S(1)} %get-tuple-element.45), channel_id=1, source_target_pairs={{0,96},{32,0},{64,32},{96,64},{1,97},{33,1},{65,33},{97,65},{2,98}... | collective-permute-start | bytes 368648 | tf_op jit(solution)/shard_map/ppermute | solution.py:260
  146.5 2.7 %collective-permute-start.14 = (bf16[96,640]{1,0:T(8,128)(2,1)S(1)}, bf16[96,640]{1,0:T(8,128)(2,1)S(1)}, u32[]{:S(2)}, u32[]{:S(2)}) collective-permute-start(bf16[96,640]{1,0:T(8,128)(2,1)S(1)} %get-tuple-element.47), channel_id=1, source_target_pairs={{0,32},{32,64},{64,96},{96,0},{1,33},{33,65},{65,97},{97,1},{2,34}... | collective-permute-start | bytes 368648 | tf_op jit(solution)/shard_map/ppermute | solution.py:260
  149.2 4.0 %collective-permute-done.13.p2 = bf16[96,640]{1,0:T(8,128)(2,1)S(1)} collective-permute-done((bf16[96,640]{1,0:T(8,128)(2,1)S(1)}, bf16[96,640]{1,0:T(8,128)(2,1)S(1)}, u32[]{:S(2)}, u32[]{:S(2)}) %collective-permute-start.13) | collective-permute-done | bytes 122912 | tf_op jit(solution)/shard_map/ppermute | solution.py:260
  153.2 4.0 %collective-permute-done.14.p3 = bf16[96,640]{1,0:T(8,128)(2,1)S(1)} collective-permute-done((bf16[96,640]{1,0:T(8,128)(2,1)S(1)}, bf16[96,640]{1,0:T(8,128)(2,1)S(1)}, u32[]{:S(2)}, u32[]{:S(2)}) %collective-permute-start.14) | collective-permute-done | bytes 122912 | tf_op jit(solution)/shard_map/ppermute | solution.py:260
  158.2 3.1 %all-to-all-done.2 = bf16[128,2,896]{2,1,0:T(2,128)(2,1)S(1)} async-done(((bf16[128,2,896]{2,1,0:T(2,128)(2,1)}), bf16[128,2,896]{2,1,0:T(2,128)(2,1)S(1)}, u32[]{:S(2)}, u32[]{:S(2)}) %all-to-all-start.2) | async-done | bytes 458784 | tf_op jit(solution)/shard_map/all_to_all | solution.py:357
  (44 shorter events, 30.1 us)
Async XLA Ops:
  3.1 44.9 %all-to-all-start = ((bf16[32,8,896]{2,1,0:T(8,128)(2,1)}), bf16[32,8,896]{2,1,0:T(8,128)(2,1)S(1)}, u32[]{:S(2)}, u32[]{:S(2)}) async-start(bf16[32,8,896]{2,1,0:T(8,128)(2,1)} %bitcast.34), calls=%async_computation | async-start | bytes 917504 | tf_op jit(solution)/shard_map/all_to_all | solution.py:307
  21.6 48.4 %collective-permute-start.3 = (bf16[7168,128]{1,0:T(8,128)(2,1)S(1)}, bf16[7168,128]{1,0:T(8,128)(2,1)}, u32[]{:S(2)}, u32[]{:S(2)}) collective-permute-start(bf16[7168,128]{1,0:T(8,128)(2,1)S(1)} %constant_dynamic-update-slice_fusion.w0), channel_id=1, source_target_pairs={{0,256},{128,384},{256,0},{384,128},{1,257},{129,385},{257,1},{385... | collective-permute-start | bytes 5505032 | tf_op jit(solution)/shard_map/ppermute | solution.py:264
  26.0 44.0 %collective-permute-start.4 = (bf16[7168,128]{1,0:T(8,128)(2,1)S(1)}, bf16[7168,128]{1,0:T(8,128)(2,1)}, u32[]{:S(2)}, u32[]{:S(2)}) collective-permute-start(bf16[7168,128]{1,0:T(8,128)(2,1)S(1)} %constant_dynamic-update-slice_fusion.w0), channel_id=1, source_target_pairs={{0,128},{128,0},{256,384},{384,256},{1,129},{129,1},{257,385},{385... | collective-permute-start | bytes 5505032 | tf_op jit(solution)/shard_map/ppermute | solution.py:264
  29.1 15.9 %collective-permute-start = (bf16[224,2048]{1,0:T(8,128)(2,1)S(1)}, bf16[224,2048]{1,0:T(8,128)(2,1)}, u32[]{:S(2)}, u32[]{:S(2)}) collective-permute-start(bf16[224,2048]{1,0:T(8,128)(2,1)S(1)} %bitcast.22), channel_id=1, source_target_pairs={{0,128},{128,0},{256,384},{384,256},{1,129},{129,1},{257,385},{385... | collective-permute-start | bytes 2752520 | tf_op jit(solution)/shard_map/ppermute | solution.py:264
  31.1 7.7 %collective-permute-start.2 = (bf16[96,576]{1,0:T(8,128)(2,1)S(1)}, bf16[96,576]{1,0:T(8,128)(2,1)S(1)}, u32[]{:S(2)}, u32[]{:S(2)}) collective-permute-start(bf16[96,576]{1,0:T(8,128)(2,1)S(1)} %bitcast.26), channel_id=1, source_target_pairs={{0,32},{32,64},{64,96},{96,0},{1,33},{33,65},{65,97},{97,1},{2,34}... | collective-permute-start | bytes 331784 | tf_op jit(solution)/shard_map/ppermute | solution.py:260
  34.3 10.8 %collective-permute-start.1 = (bf16[1152,128]{1,0:T(8,128)(2,1)}, bf16[1152,128]{1,0:T(8,128)(2,1)}, u32[]{:S(2)}, u32[]{:S(2)}) collective-permute-start(bf16[1152,128]{1,0:T(8,128)(2,1)} %bitcast.8.m0), channel_id=1, source_target_pairs={{0,128},{128,0},{256,384},{384,256},{1,129},{129,1},{257,385},{385... | collective-permute-start | bytes 884744 | tf_op jit(solution)/shard_map/ppermute | solution.py:264
  39.6 16.1 %collective-permute-start.5 = (bf16[192,576]{1,0:T(8,128)(2,1)}, bf16[192,576]{1,0:T(8,128)(2,1)}, u32[]{:S(2)}, u32[]{:S(2)}) collective-permute-start(bf16[192,576]{1,0:T(8,128)(2,1)} %pad_maximum_fusion), channel_id=1, source_target_pairs={{0,64},{32,96},{64,0},{96,32},{1,65},{33,97},{65,1},{97,33},{2,66}... | collective-permute-start | bytes 663560 | tf_op jit(solution)/shard_map/ppermute | solution.py:260
  47.9 22.1 %collective-permute-start.6 = (bf16[256,896]{1,0:T(8,128)(2,1)S(1)}, bf16[256,896]{1,0:T(8,128)(2,1)S(1)}, u32[]{:S(2)}, u32[]{:S(2)}) collective-permute-start(bf16[256,896]{1,0:T(8,128)(2,1)S(1)} %bitcast.18), channel_id=1, source_target_pairs={{0,32},{32,64},{64,96},{96,0},{1,33},{33,65},{65,97},{97,1},{2,34}... | collective-permute-start | bytes 1376264 | tf_op jit(solution)/shard_map/ppermute | solution.py:260
  51.1 21.3 %collective-permute-start.7 = (bf16[256,896]{1,0:T(8,128)(2,1)S(1)}, bf16[256,896]{1,0:T(8,128)(2,1)S(1)}, u32[]{:S(2)}, u32[]{:S(2)}) collective-permute-start(bf16[256,896]{1,0:T(8,128)(2,1)S(1)} %bitcast.19), channel_id=1, source_target_pairs={{0,64},{32,96},{64,0},{96,32},{1,65},{33,97},{65,1},{97,33},{2,66}... | collective-permute-start | bytes 1376264 | tf_op jit(solution)/shard_map/ppermute | solution.py:260
  55.7 19.2 %collective-permute-start.8 = (bf16[256,896]{1,0:T(8,128)(2,1)S(1)}, bf16[256,896]{1,0:T(8,128)(2,1)S(1)}, u32[]{:S(2)}, u32[]{:S(2)}) collective-permute-start(bf16[256,896]{1,0:T(8,128)(2,1)S(1)} %bitcast.20), channel_id=1, source_target_pairs={{0,96},{32,0},{64,32},{96,64},{1,97},{33,1},{65,33},{97,65},{2,98}... | collective-permute-start | bytes 1376264 | tf_op jit(solution)/shard_map/ppermute | solution.py:260
  74.8 7.8 %collective-permute-start.9 = (bf16[7168,128]{1,0:T(8,128)(2,1)}, bf16[7168,128]{1,0:T(8,128)(2,1)S(1)}, u32[]{:S(2)}, u32[]{:S(2)}) collective-permute-start(bf16[7168,128]{1,0:T(8,128)(2,1)} %collective-permute-done.3.w2), channel_id=1, source_target_pairs={{0,128},{128,0},{256,384},{384,256},{1,129},{129,1},{257,385},{385... | collective-permute-start | bytes 5505032 | tf_op jit(solution)/shard_map/ppermute | solution.py:264
  78.3 31.7 %collective-permute-start.15 = (bf16[224,2048]{1,0:T(8,128)(2,1)S(1)}, bf16[224,2048]{1,0:T(8,128)(2,1)}, u32[]{:S(2)}, u32[]{:S(2)}) collective-permute-start(bf16[224,2048]{1,0:T(8,128)(2,1)S(1)} %bitcast.23), channel_id=1, source_target_pairs={{0,256},{128,384},{256,0},{384,128},{1,257},{129,385},{257,1},{385... | collective-permute-start | bytes 2752520 | tf_op jit(solution)/shard_map/ppermute | solution.py:264
  88.6 21.4 %all-to-all-start.1 = ((bf16[4,256,512]{2,1,0:T(8,128)(2,1)}), bf16[4,256,512]{2,1,0:T(8,128)(2,1)S(1)}, u32[]{:S(2)}, u32[]{:S(2)}) async-start(bf16[4,256,512]{2,1,0:T(8,128)(2,1)} %shard_map.150), calls=%async_computation.1 | async-start | bytes 2097152 | tf_op jit(solution)/shard_map/all_to_all | solution.py:341
  92.7 17.3 %collective-permute-start.10 = (bf16[1152,128]{1,0:T(8,128)(2,1)}, bf16[1152,128]{1,0:T(8,128)(2,1)S(1)}, u32[]{:S(2)}, u32[]{:S(2)}) collective-permute-start(bf16[1152,128]{1,0:T(8,128)(2,1)} %bitcast.8.m0), channel_id=1, source_target_pairs={{0,256},{128,384},{256,0},{384,128},{1,257},{129,385},{257,1},{385... | collective-permute-start | bytes 884744 | tf_op jit(solution)/shard_map/ppermute | solution.py:264
  110.0 5.0 %collective-permute-start.16 = (bf16[224,2048]{1,0:T(8,128)(2,1)}, bf16[224,2048]{1,0:T(8,128)(2,1)S(1)}, u32[]{:S(2)}, u32[]{:S(2)}) collective-permute-start(bf16[224,2048]{1,0:T(8,128)(2,1)} %collective-permute-done.15.d2), channel_id=1, source_target_pairs={{0,128},{128,0},{256,384},{384,256},{1,129},{129,1},{257,385},{385... | collective-permute-start | bytes 2752520 | tf_op jit(solution)/shard_map/ppermute | solution.py:264
  118.5 18.0 %copy-start.1 = (bf16[6,128,576]{1,2,0:T(8,128)(2,1)S(1)}, bf16[6,128,576]{1,2,0:T(8,128)(2,1)}, u32[]{:S(2)}) copy-start(bf16[6,128,576]{1,2,0:T(8,128)(2,1)} %param.15) | copy-start | bytes 2654212
  118.5 18.0 %copy-start.5 = (s32[1,6]{1,0:T(1,128)S(1)}, s32[1,6]{1,0:T(1,128)}, u32[]{:S(2)}) copy-start(s32[1,6]{1,0:T(1,128)} %param.16) | copy-start | bytes 76
  119.5 41.7 %all-to-all-start.2 = ((bf16[128,2,896]{2,1,0:T(2,128)(2,1)}), bf16[128,2,896]{2,1,0:T(2,128)(2,1)S(1)}, u32[]{:S(2)}, u32[]{:S(2)}) async-start(bf16[128,2,896]{2,1,0:T(2,128)(2,1)} %reshape.38), calls=%async_computation.2 | async-start | bytes 917504 | tf_op jit(solution)/shard_map/all_to_all | solution.py:357
  132.7 3.8 %collective-permute-start.11 = (bf16[1152,128]{1,0:T(8,128)(2,1)S(1)}, bf16[1152,128]{1,0:T(8,128)(2,1)S(1)}, u32[]{:S(2)}, u32[]{:S(2)}) collective-permute-start(bf16[1152,128]{1,0:T(8,128)(2,1)S(1)} %collective-permute-done.10.m2), channel_id=1, source_target_pairs={{0,128},{128,0},{256,384},{384,256},{1,129},{129,1},{257,385},{385... | collective-permute-start | bytes 884744 | tf_op jit(solution)/shard_map/ppermute | solution.py:264
  136.5 24.9 %copy-start.3 = (s32[16,2]{0,1:T(2,128)S(1)}, s32[16,2]{0,1:T(2,128)}, u32[]{:S(2)}) copy-start(s32[16,2]{0,1:T(2,128)} %param.23) | copy-start | bytes 388
  136.5 24.9 %copy-start.4 = (f32[16,2]{0,1:T(2,128)S(1)}, f32[16,2]{0,1:T(2,128)}, u32[]{:S(2)}) copy-start(f32[16,2]{0,1:T(2,128)} %param.24) | copy-start | bytes 388
  139.9 9.3 %collective-permute-start.12 = (bf16[96,640]{1,0:T(8,128)(2,1)S(1)}, bf16[96,640]{1,0:T(8,128)(2,1)S(1)}, u32[]{:S(2)}, u32[]{:S(2)}) collective-permute-start(bf16[96,640]{1,0:T(8,128)(2,1)S(1)} %get-tuple-element.45), channel_id=1, source_target_pairs={{0,96},{32,0},{64,32},{96,64},{1,97},{33,1},{65,33},{97,65},{2,98}... | collective-permute-start | bytes 368648 | tf_op jit(solution)/shard_map/ppermute | solution.py:260
  144.4 8.8 %collective-permute-start.13 = (bf16[96,640]{1,0:T(8,128)(2,1)S(1)}, bf16[96,640]{1,0:T(8,128)(2,1)S(1)}, u32[]{:S(2)}, u32[]{:S(2)}) collective-permute-start(bf16[96,640]{1,0:T(8,128)(2,1)S(1)} %get-tuple-element.46), channel_id=1, source_target_pairs={{0,64},{32,96},{64,0},{96,32},{1,65},{33,97},{65,1},{97,33},{2,66}... | collective-permute-start | bytes 368648 | tf_op jit(solution)/shard_map/ppermute | solution.py:260
  146.5 10.8 %collective-permute-start.14 = (bf16[96,640]{1,0:T(8,128)(2,1)S(1)}, bf16[96,640]{1,0:T(8,128)(2,1)S(1)}, u32[]{:S(2)}, u32[]{:S(2)}) collective-permute-start(bf16[96,640]{1,0:T(8,128)(2,1)S(1)} %get-tuple-element.47), channel_id=1, source_target_pairs={{0,32},{32,64},{64,96},{96,0},{1,33},{33,65},{65,97},{97,1},{2,34}... | collective-permute-start | bytes 368648 | tf_op jit(solution)/shard_map/ppermute | solution.py:260
  (4 other events, 39.5 us)

commit v5 on v4

--- a/solution.py
+++ b/solution.py
@@ -14,6 +14,7 @@
 CAP = 2
 N_TP = 4
 N_DP = 4
+BLOCK_SHIFTS = (0, 2, 1, 3)
 
 score_scale = 0.07216878364870322
 neg_fill = -1e30
@@ -78,7 +79,7 @@
     depth, part = w0.shape[0] // 2, w0.shape[1]
     count, quarter = b0.shape
     slots = count // 4
-    for k, b in enumerate((b0, b1, b2, b3)):
+    for k, b in zip(BLOCK_SHIFTS, (b0, b1, b2, b3)):
         base = pl.multiple_of(((rank_tp + N_TP - k) % N_TP) * slots, slots)
         block = b[...]
         row = iota((count, count), 0)
@@ -323,7 +324,7 @@
     pages_c = swap(pages, 1)
     arrived, down_c, pages_c, where, near = after((arrived, down_c, pages_c, where, near))
 
-    blocks = [shift(arrived, k) for k in (1, 2, 3)]
+    blocks = [shift(arrived, k) for k in BLOCK_SHIFTS[1:]]
     first_x, first_c, far, *blocks = after((first_x, first_c, far, *blocks))
     asks = [near, far]
     first_xc = swap(first_x, 1)

time: 165 us -> 163 us (0.988)
  waiting for transfers between devices: 49.2 us -> 47.5 us
  transfers between devices with their start and end apart: 20 -> 20, of which waited for: 11 -> 10; matrix products, arithmetic and copies ran while one was open for 1% -> 1% of each run, Pallas kernels for 6% -> 6%
where the time goes in v5:
time: 163 us; the launch traced here: 161 us
  starting transfers between devices  89.7 us (55%)
  waiting for transfers between devices  47.5 us (29%)
  Pallas kernels  17.5 us (11%)
  between operations  2.89 us (2%)
  local copies, waits for them, and re-layouts  2.79 us (2%)
    ppermute x9, waiting for transfers between devices, swap(): return lax.ppermute(x, 'dp', [(i, i ^ bit) for i in range(N_DP)])  28.2 us
    ppermute x9, starting transfers between devices, swap(): return lax.ppermute(x, 'dp', [(i, i ^ bit) for i in range(N_DP)])  28 us
    ppermute x8, starting transfers between devices, shift(): return lax.ppermute(x, 'tp', [(i, (i + k) % N_TP) for i in range(N_TP)])  27.2 us
    all_to_all x1, starting transfers between devices, per_device(): lax.all_to_all(sent.reshape(ranks_ep, CAP * 4, quarter), 'ep', split_axis...  17 us
    all_to_all x1, starting transfers between devices, per_device(): lax.all_to_all(expert_out.reshape(N_TP * ranks_ep, CAP, N_DP * cols), ('t...  13.7 us
    ppermute x8, waiting for transfers between devices, shift(): return lax.ppermute(x, 'tp', [(i, (i + k) % N_TP) for i in range(N_TP)])  13.6 us
    pallas_call x1, Pallas kernels, per_device(): pl.pallas_call(hidden_kernel, out_shape=jax.ShapeDtypeStruct((N_TP, rows,...  5.92 us
    all_to_all x1, starting transfers between devices, per_device(): lax.all_to_all(hidden, 'tp', split_axis=0, concat_axis=0, tiled=True)  3.84 us
  transfers between devices with their start and end apart: 20, of which 10 were waited for; matrix products, arithmetic and copies ran while one was open for 1% of the time, Pallas kernels for 6%

profile of v5, /device:TPU:1, one launch (start us, length us, event | category | flops | bytes accessed | tf_op | source)
XLA Modules:
  0.0 161.1 jit_solution(7313648611516446182)
XLA Ops:
  3.1 17.0 %all-to-all-start = ((bf16[32,8,896]{2,1,0:T(8,128)(2,1)}), bf16[32,8,896]{2,1,0:T(8,128)(2,1)S(1)}, u32[]{:S(2)}, u32[]{:S(2)}) async-start(bf16[32,8,896]{2,1,0:T(8,128)(2,1)} %bitcast.34), calls=%async_computation | async-start | bytes 917504 | tf_op jit(solution)/shard_map/all_to_all | solution.py:308
  21.6 4.4 %collective-permute-start.3 = (bf16[7168,128]{1,0:T(8,128)(2,1)S(1)}, bf16[7168,128]{1,0:T(8,128)(2,1)}, u32[]{:S(2)}, u32[]{:S(2)}) collective-permute-start(bf16[7168,128]{1,0:T(8,128)(2,1)S(1)} %constant_dynamic-update-slice_fusion.w0), channel_id=1, source_target_pairs={{0,256},{128,384},{256,0},{384,128},{1,257},{129,385},{257,1},{385... | collective-permute-start | bytes 5505032 | tf_op jit(solution)/shard_map/ppermute | solution.py:265
  26.0 3.1 %collective-permute-start.4 = (bf16[7168,128]{1,0:T(8,128)(2,1)S(1)}, bf16[7168,128]{1,0:T(8,128)(2,1)}, u32[]{:S(2)}, u32[]{:S(2)}) collective-permute-start(bf16[7168,128]{1,0:T(8,128)(2,1)S(1)} %constant_dynamic-update-slice_fusion.w0), channel_id=1, source_target_pairs={{0,128},{128,0},{256,384},{384,256},{1,129},{129,1},{257,385},{385... | collective-permute-start | bytes 5505032 | tf_op jit(solution)/shard_map/ppermute | solution.py:265
  31.1 3.2 %collective-permute-start.2 = (bf16[96,576]{1,0:T(8,128)(2,1)S(1)}, bf16[96,576]{1,0:T(8,128)(2,1)S(1)}, u32[]{:S(2)}, u32[]{:S(2)}) collective-permute-start(bf16[96,576]{1,0:T(8,128)(2,1)S(1)} %bitcast.26), channel_id=1, source_target_pairs={{0,32},{32,64},{64,96},{96,0},{1,33},{33,65},{65,97},{97,1},{2,34}... | collective-permute-start | bytes 331784 | tf_op jit(solution)/shard_map/ppermute | solution.py:261
  39.6 3.4 %collective-permute-start.5 = (bf16[192,576]{1,0:T(8,128)(2,1)}, bf16[192,576]{1,0:T(8,128)(2,1)}, u32[]{:S(2)}, u32[]{:S(2)}) collective-permute-start(bf16[192,576]{1,0:T(8,128)(2,1)} %pad_maximum_fusion), channel_id=1, source_target_pairs={{0,64},{32,96},{64,0},{96,32},{1,65},{33,97},{65,1},{97,33},{2,66}... | collective-permute-start | bytes 663560 | tf_op jit(solution)/shard_map/ppermute | solution.py:261
  45.1 2.9 %all-to-all-done = bf16[32,8,896]{2,1,0:T(8,128)(2,1)S(1)} async-done(((bf16[32,8,896]{2,1,0:T(8,128)(2,1)}), bf16[32,8,896]{2,1,0:T(8,128)(2,1)S(1)}, u32[]{:S(2)}, u32[]{:S(2)}) %all-to-all-start) | async-done | bytes 458784 | tf_op jit(solution)/shard_map/all_to_all | solution.py:308
  47.9 4.8 %collective-permute-start.6 = (bf16[256,896]{1,0:T(8,128)(2,1)S(1)}, bf16[256,896]{1,0:T(8,128)(2,1)S(1)}, u32[]{:S(2)}, u32[]{:S(2)}) collective-permute-start(bf16[256,896]{1,0:T(8,128)(2,1)S(1)} %bitcast.18), channel_id=1, source_target_pairs={{0,64},{32,96},{64,0},{96,32},{1,65},{33,97},{65,1},{97,33},{2,66}... | collective-permute-start | bytes 1376264 | tf_op jit(solution)/shard_map/ppermute | solution.py:261
  55.1 4.2 %collective-permute-start.8 = (bf16[256,896]{1,0:T(8,128)(2,1)S(1)}, bf16[256,896]{1,0:T(8,128)(2,1)S(1)}, u32[]{:S(2)}, u32[]{:S(2)}) collective-permute-start(bf16[256,896]{1,0:T(8,128)(2,1)S(1)} %bitcast.20), channel_id=1, source_target_pairs={{0,96},{32,0},{64,32},{96,64},{1,97},{33,1},{65,33},{97,65},{2,98}... | collective-permute-start | bytes 1376264 | tf_op jit(solution)/shard_map/ppermute | solution.py:261
  59.3 10.7 %collective-permute-done.3.w2 = bf16[7168,128]{1,0:T(8,128)(2,1)} collective-permute-done((bf16[7168,128]{1,0:T(8,128)(2,1)S(1)}, bf16[7168,128]{1,0:T(8,128)(2,1)}, u32[]{:S(2)}, u32[]{:S(2)}) %collective-permute-start.3) | collective-permute-done | bytes 1835040 | tf_op jit(solution)/shard_map/ppermute | solution.py:265
  70.0 3.6 %collective-permute-done.7.b2 = bf16[256,896]{1,0:T(8,128)(2,1)S(1)} collective-permute-done((bf16[256,896]{1,0:T(8,128)(2,1)S(1)}, bf16[256,896]{1,0:T(8,128)(2,1)S(1)}, u32[]{:S(2)}, u32[]{:S(2)}) %collective-permute-start.7) | collective-permute-done | bytes 458784 | tf_op jit(solution)/shard_map/ppermute | solution.py:261
  73.6 2.7 %collective-permute-start.9 = (bf16[7168,128]{1,0:T(8,128)(2,1)}, bf16[7168,128]{1,0:T(8,128)(2,1)S(1)}, u32[]{:S(2)}, u32[]{:S(2)}) collective-permute-start(bf16[7168,128]{1,0:T(8,128)(2,1)} %collective-permute-done.3.w2), channel_id=1, source_target_pairs={{0,128},{128,0},{256,384},{384,256},{1,129},{129,1},{257,385},{385... | collective-permute-start | bytes 5505032 | tf_op jit(solution)/shard_map/ppermute | solution.py:265
  76.3 4.4 %collective-permute-start.15 = (bf16[224,2048]{1,0:T(8,128)(2,1)S(1)}, bf16[224,2048]{1,0:T(8,128)(2,1)}, u32[]{:S(2)}, u32[]{:S(2)}) collective-permute-start(bf16[224,2048]{1,0:T(8,128)(2,1)S(1)} %bitcast.23), channel_id=1, source_target_pairs={{0,256},{128,384},{256,0},{384,128},{1,257},{129,385},{257,1},{385... | collective-permute-start | bytes 2752520 | tf_op jit(solution)/shard_map/ppermute | solution.py:265
  80.7 5.9 %shard_map.150 = bf16[4,256,512]{2,1,0:T(8,128)(2,1)} custom-call(s32[5]{0:T(128)S(1)} %stack.11.where_ref, bf16[256,896]{1,0:T(8,128)(2,1)S(1)} %bitcast.21, bf16[256,896]{1,0:T(8,128)(2,1)S(1)} %collective-permute-done.6.b1, bf16[256,896]{1,0:T(8,128)(2,1)S(1)} %collective-permute-done.7.b2, bf16[256,896]{1,0:T(8,128)(2,1)S(1)} %collective-permute-done.8.b3, ...), custom_call_target="tpu_custom_call" | custom-call | tf_op jit(solution)/shard_map/pallas_call | solution.py:333
  86.6 3.8 %all-to-all-start.1 = ((bf16[4,256,512]{2,1,0:T(8,128)(2,1)}), bf16[4,256,512]{2,1,0:T(8,128)(2,1)S(1)}, u32[]{:S(2)}, u32[]{:S(2)}) async-start(bf16[4,256,512]{2,1,0:T(8,128)(2,1)} %shard_map.150), calls=%async_computation.1 | async-start | bytes 2097152 | tf_op jit(solution)/shard_map/all_to_all | solution.py:342
  90.5 3.6 %collective-permute-start.10 = (bf16[1152,128]{1,0:T(8,128)(2,1)}, bf16[1152,128]{1,0:T(8,128)(2,1)S(1)}, u32[]{:S(2)}, u32[]{:S(2)}) collective-permute-start(bf16[1152,128]{1,0:T(8,128)(2,1)} %bitcast.8.m0), channel_id=1, source_target_pairs={{0,256},{128,384},{256,0},{384,128},{1,257},{129,385},{257,1},{385... | collective-permute-start | bytes 884744 | tf_op jit(solution)/shard_map/ppermute | solution.py:265
  94.1 14.0 %collective-permute-done.10.m2 = bf16[1152,128]{1,0:T(8,128)(2,1)S(1)} collective-permute-done((bf16[1152,128]{1,0:T(8,128)(2,1)}, bf16[1152,128]{1,0:T(8,128)(2,1)S(1)}, u32[]{:S(2)}, u32[]{:S(2)}) %collective-permute-start.10) | collective-permute-done | bytes 294944 | tf_op jit(solution)/shard_map/ppermute | solution.py:265
  113.0 3.5 %shard_map.153 = bf16[256,896]{1,0:T(8,128)(2,1)S(1)} custom-call(s32[5]{0:T(128)S(1)} %stack.11.where_ref, bf16[4,256,512]{2,1,0:T(8,128)(2,1)S(1)} %all-to-all-done.1.parts, bf16[224,2048]{1,0:T(8,128)(2,1)S(1)} %bitcast.24, bf16[224,2048]{1,0:T(8,128)(2,1)} %collective-permute-done.d1, bf16[224,2048]{1,0:T(8,128)(2,1)} %collective-permute-done.15.d2, ...), custom_call_target="tpu_custom_call" | custom-call | tf_op jit(solution)/shard_map/pallas_call | solution.py:346
  117.5 13.7 %all-to-all-start.2 = ((bf16[128,2,896]{2,1,0:T(2,128)(2,1)}), bf16[128,2,896]{2,1,0:T(2,128)(2,1)S(1)}, u32[]{:S(2)}, u32[]{:S(2)}) async-start(bf16[128,2,896]{2,1,0:T(2,128)(2,1)} %reshape.38), calls=%async_computation.2 | async-start | bytes 917504 | tf_op jit(solution)/shard_map/all_to_all | solution.py:358
  135.0 3.5 %shard_map.151 = (bf16[96,640]{1,0:T(8,128)(2,1)S(1)}, bf16[96,640]{1,0:T(8,128)(2,1)S(1)}, bf16[96,640]{1,0:T(8,128)(2,1)S(1)}, bf16[96,640]{1,0:T(8,128)(2,1)S(1)}) custom-call(s32[5]{0:T(128)S(1)} %stack.11.where_ref, s32[6]{0:T(128)S(1)} %bitcast.32, s32[3]{0:T(128)S(1)} %bitcast.33, bf16[96,576]{1,0:T(8,128)(2,1)S(1)} %bitcast.28, ...), custom_call_target="tpu_custom_call" | custom-call | tf_op jit(solution)/shard_map/pallas_call | solution.py:367
  138.5 4.5 %collective-permute-start.12 = (bf16[96,640]{1,0:T(8,128)(2,1)S(1)}, bf16[96,640]{1,0:T(8,128)(2,1)S(1)}, u32[]{:S(2)}, u32[]{:S(2)}) collective-permute-start(bf16[96,640]{1,0:T(8,128)(2,1)S(1)} %get-tuple-element.45), channel_id=1, source_target_pairs={{0,96},{32,0},{64,32},{96,64},{1,97},{33,1},{65,33},{97,65},{2,98}... | collective-permute-start | bytes 368648 | tf_op jit(solution)/shard_map/ppermute | solution.py:261
  145.1 2.7 %collective-permute-start.14 = (bf16[96,640]{1,0:T(8,128)(2,1)S(1)}, bf16[96,640]{1,0:T(8,128)(2,1)S(1)}, u32[]{:S(2)}, u32[]{:S(2)}) collective-permute-start(bf16[96,640]{1,0:T(8,128)(2,1)S(1)} %get-tuple-element.47), channel_id=1, source_target_pairs={{0,32},{32,64},{64,96},{96,0},{1,33},{33,65},{65,97},{97,1},{2,34}... | collective-permute-start | bytes 368648 | tf_op jit(solution)/shard_map/ppermute | solution.py:261
  147.8 4.1 %collective-permute-done.13.p2 = bf16[96,640]{1,0:T(8,128)(2,1)S(1)} collective-permute-done((bf16[96,640]{1,0:T(8,128)(2,1)S(1)}, bf16[96,640]{1,0:T(8,128)(2,1)S(1)}, u32[]{:S(2)}, u32[]{:S(2)}) %collective-permute-start.13) | collective-permute-done | bytes 122912 | tf_op jit(solution)/shard_map/ppermute | solution.py:261
  151.9 4.0 %collective-permute-done.14.p3 = bf16[96,640]{1,0:T(8,128)(2,1)S(1)} collective-permute-done((bf16[96,640]{1,0:T(8,128)(2,1)S(1)}, bf16[96,640]{1,0:T(8,128)(2,1)S(1)}, u32[]{:S(2)}, u32[]{:S(2)}) %collective-permute-start.14) | collective-permute-done | bytes 122912 | tf_op jit(solution)/shard_map/ppermute | solution.py:261
  156.9 2.9 %all-to-all-done.2 = bf16[128,2,896]{2,1,0:T(2,128)(2,1)S(1)} async-done(((bf16[128,2,896]{2,1,0:T(2,128)(2,1)}), bf16[128,2,896]{2,1,0:T(2,128)(2,1)S(1)}, u32[]{:S(2)}, u32[]{:S(2)}) %all-to-all-start.2) | async-done | bytes 458784 | tf_op jit(solution)/shard_map/all_to_all | solution.py:358
  (44 shorter events, 27.6 us)
Async XLA Ops:
  3.1 44.9 %all-to-all-start = ((bf16[32,8,896]{2,1,0:T(8,128)(2,1)}), bf16[32,8,896]{2,1,0:T(8,128)(2,1)S(1)}, u32[]{:S(2)}, u32[]{:S(2)}) async-start(bf16[32,8,896]{2,1,0:T(8,128)(2,1)} %bitcast.34), calls=%async_computation | async-start | bytes 917504 | tf_op jit(solution)/shard_map/all_to_all | solution.py:308
  21.6 48.4 %collective-permute-start.3 = (bf16[7168,128]{1,0:T(8,128)(2,1)S(1)}, bf16[7168,128]{1,0:T(8,128)(2,1)}, u32[]{:S(2)}, u32[]{:S(2)}) collective-permute-start(bf16[7168,128]{1,0:T(8,128)(2,1)S(1)} %constant_dynamic-update-slice_fusion.w0), channel_id=1, source_target_pairs={{0,256},{128,384},{256,0},{384,128},{1,257},{129,385},{257,1},{385... | collective-permute-start | bytes 5505032 | tf_op jit(solution)/shard_map/ppermute | solution.py:265
  26.0 44.0 %collective-permute-start.4 = (bf16[7168,128]{1,0:T(8,128)(2,1)S(1)}, bf16[7168,128]{1,0:T(8,128)(2,1)}, u32[]{:S(2)}, u32[]{:S(2)}) collective-permute-start(bf16[7168,128]{1,0:T(8,128)(2,1)S(1)} %constant_dynamic-update-slice_fusion.w0), channel_id=1, source_target_pairs={{0,128},{128,0},{256,384},{384,256},{1,129},{129,1},{257,385},{385... | collective-permute-start | bytes 5505032 | tf_op jit(solution)/shard_map/ppermute | solution.py:265
  29.1 15.9 %collective-permute-start = (bf16[224,2048]{1,0:T(8,128)(2,1)S(1)}, bf16[224,2048]{1,0:T(8,128)(2,1)}, u32[]{:S(2)}, u32[]{:S(2)}) collective-permute-start(bf16[224,2048]{1,0:T(8,128)(2,1)S(1)} %bitcast.22), channel_id=1, source_target_pairs={{0,128},{128,0},{256,384},{384,256},{1,129},{129,1},{257,385},{385... | collective-permute-start | bytes 2752520 | tf_op jit(solution)/shard_map/ppermute | solution.py:265
  31.1 7.7 %collective-permute-start.2 = (bf16[96,576]{1,0:T(8,128)(2,1)S(1)}, bf16[96,576]{1,0:T(8,128)(2,1)S(1)}, u32[]{:S(2)}, u32[]{:S(2)}) collective-permute-start(bf16[96,576]{1,0:T(8,128)(2,1)S(1)} %bitcast.26), channel_id=1, source_target_pairs={{0,32},{32,64},{64,96},{96,0},{1,33},{33,65},{65,97},{97,1},{2,34}... | collective-permute-start | bytes 331784 | tf_op jit(solution)/shard_map/ppermute | solution.py:261
  34.3 10.8 %collective-permute-start.1 = (bf16[1152,128]{1,0:T(8,128)(2,1)}, bf16[1152,128]{1,0:T(8,128)(2,1)}, u32[]{:S(2)}, u32[]{:S(2)}) collective-permute-start(bf16[1152,128]{1,0:T(8,128)(2,1)} %bitcast.8.m0), channel_id=1, source_target_pairs={{0,128},{128,0},{256,384},{384,256},{1,129},{129,1},{257,385},{385... | collective-permute-start | bytes 884744 | tf_op jit(solution)/shard_map/ppermute | solution.py:265
  39.6 15.5 %collective-permute-start.5 = (bf16[192,576]{1,0:T(8,128)(2,1)}, bf16[192,576]{1,0:T(8,128)(2,1)}, u32[]{:S(2)}, u32[]{:S(2)}) collective-permute-start(bf16[192,576]{1,0:T(8,128)(2,1)} %pad_maximum_fusion), channel_id=1, source_target_pairs={{0,64},{32,96},{64,0},{96,32},{1,65},{33,97},{65,1},{97,33},{2,66}... | collective-permute-start | bytes 663560 | tf_op jit(solution)/shard_map/ppermute | solution.py:261
  47.9 22.1 %collective-permute-start.6 = (bf16[256,896]{1,0:T(8,128)(2,1)S(1)}, bf16[256,896]{1,0:T(8,128)(2,1)S(1)}, u32[]{:S(2)}, u32[]{:S(2)}) collective-permute-start(bf16[256,896]{1,0:T(8,128)(2,1)S(1)} %bitcast.18), channel_id=1, source_target_pairs={{0,64},{32,96},{64,0},{96,32},{1,65},{33,97},{65,1},{97,33},{2,66}... | collective-permute-start | bytes 1376264 | tf_op jit(solution)/shard_map/ppermute | solution.py:261
  52.7 20.8 %collective-permute-start.7 = (bf16[256,896]{1,0:T(8,128)(2,1)S(1)}, bf16[256,896]{1,0:T(8,128)(2,1)S(1)}, u32[]{:S(2)}, u32[]{:S(2)}) collective-permute-start(bf16[256,896]{1,0:T(8,128)(2,1)S(1)} %bitcast.19), channel_id=1, source_target_pairs={{0,32},{32,64},{64,96},{96,0},{1,33},{33,65},{65,97},{97,1},{2,34}... | collective-permute-start | bytes 1376264 | tf_op jit(solution)/shard_map/ppermute | solution.py:261
  55.1 18.5 %collective-permute-start.8 = (bf16[256,896]{1,0:T(8,128)(2,1)S(1)}, bf16[256,896]{1,0:T(8,128)(2,1)S(1)}, u32[]{:S(2)}, u32[]{:S(2)}) collective-permute-start(bf16[256,896]{1,0:T(8,128)(2,1)S(1)} %bitcast.20), channel_id=1, source_target_pairs={{0,96},{32,0},{64,32},{96,64},{1,97},{33,1},{65,33},{97,65},{2,98}... | collective-permute-start | bytes 1376264 | tf_op jit(solution)/shard_map/ppermute | solution.py:261
  73.6 7.1 %collective-permute-start.9 = (bf16[7168,128]{1,0:T(8,128)(2,1)}, bf16[7168,128]{1,0:T(8,128)(2,1)S(1)}, u32[]{:S(2)}, u32[]{:S(2)}) collective-permute-start(bf16[7168,128]{1,0:T(8,128)(2,1)} %collective-permute-done.3.w2), channel_id=1, source_target_pairs={{0,128},{128,0},{256,384},{384,256},{1,129},{129,1},{257,385},{385... | collective-permute-start | bytes 5505032 | tf_op jit(solution)/shard_map/ppermute | solution.py:265
  76.3 31.7 %collective-permute-start.15 = (bf16[224,2048]{1,0:T(8,128)(2,1)S(1)}, bf16[224,2048]{1,0:T(8,128)(2,1)}, u32[]{:S(2)}, u32[]{:S(2)}) collective-permute-start(bf16[224,2048]{1,0:T(8,128)(2,1)S(1)} %bitcast.23), channel_id=1, source_target_pairs={{0,256},{128,384},{256,0},{384,128},{1,257},{129,385},{257,1},{385... | collective-permute-start | bytes 2752520 | tf_op jit(solution)/shard_map/ppermute | solution.py:265
  86.6 21.4 %all-to-all-start.1 = ((bf16[4,256,512]{2,1,0:T(8,128)(2,1)}), bf16[4,256,512]{2,1,0:T(8,128)(2,1)S(1)}, u32[]{:S(2)}, u32[]{:S(2)}) async-start(bf16[4,256,512]{2,1,0:T(8,128)(2,1)} %shard_map.150), calls=%async_computation.1 | async-start | bytes 2097152 | tf_op jit(solution)/shard_map/all_to_all | solution.py:342
  90.5 17.5 %collective-permute-start.10 = (bf16[1152,128]{1,0:T(8,128)(2,1)}, bf16[1152,128]{1,0:T(8,128)(2,1)S(1)}, u32[]{:S(2)}, u32[]{:S(2)}) collective-permute-start(bf16[1152,128]{1,0:T(8,128)(2,1)} %bitcast.8.m0), channel_id=1, source_target_pairs={{0,256},{128,384},{256,0},{384,128},{1,257},{129,385},{257,1},{385... | collective-permute-start | bytes 884744 | tf_op jit(solution)/shard_map/ppermute | solution.py:265
  108.0 5.0 %collective-permute-start.16 = (bf16[224,2048]{1,0:T(8,128)(2,1)}, bf16[224,2048]{1,0:T(8,128)(2,1)S(1)}, u32[]{:S(2)}, u32[]{:S(2)}) collective-permute-start(bf16[224,2048]{1,0:T(8,128)(2,1)} %collective-permute-done.15.d2), channel_id=1, source_target_pairs={{0,128},{128,0},{256,384},{384,256},{1,129},{129,1},{257,385},{385... | collective-permute-start | bytes 2752520 | tf_op jit(solution)/shard_map/ppermute | solution.py:265
  116.6 18.4 %copy-start.1 = (bf16[6,128,576]{1,2,0:T(8,128)(2,1)S(1)}, bf16[6,128,576]{1,2,0:T(8,128)(2,1)}, u32[]{:S(2)}) copy-start(bf16[6,128,576]{1,2,0:T(8,128)(2,1)} %param.15) | copy-start | bytes 2654212
  116.6 18.4 %copy-start.5 = (s32[1,6]{1,0:T(1,128)S(1)}, s32[1,6]{1,0:T(1,128)}, u32[]{:S(2)}) copy-start(s32[1,6]{1,0:T(1,128)} %param.16) | copy-start | bytes 76
  117.5 42.2 %all-to-all-start.2 = ((bf16[128,2,896]{2,1,0:T(2,128)(2,1)}), bf16[128,2,896]{2,1,0:T(2,128)(2,1)S(1)}, u32[]{:S(2)}, u32[]{:S(2)}) async-start(bf16[128,2,896]{2,1,0:T(2,128)(2,1)} %reshape.38), calls=%async_computation.2 | async-start | bytes 917504 | tf_op jit(solution)/shard_map/all_to_all | solution.py:358
  131.2 3.8 %collective-permute-start.11 = (bf16[1152,128]{1,0:T(8,128)(2,1)S(1)}, bf16[1152,128]{1,0:T(8,128)(2,1)S(1)}, u32[]{:S(2)}, u32[]{:S(2)}) collective-permute-start(bf16[1152,128]{1,0:T(8,128)(2,1)S(1)} %collective-permute-done.10.m2), channel_id=1, source_target_pairs={{0,128},{128,0},{256,384},{384,256},{1,129},{129,1},{257,385},{385... | collective-permute-start | bytes 884744 | tf_op jit(solution)/shard_map/ppermute | solution.py:265
  135.0 24.9 %copy-start.3 = (s32[16,2]{0,1:T(2,128)S(1)}, s32[16,2]{0,1:T(2,128)}, u32[]{:S(2)}) copy-start(s32[16,2]{0,1:T(2,128)} %param.23) | copy-start | bytes 388
  135.0 24.9 %copy-start.4 = (f32[16,2]{0,1:T(2,128)S(1)}, f32[16,2]{0,1:T(2,128)}, u32[]{:S(2)}) copy-start(f32[16,2]{0,1:T(2,128)} %param.24) | copy-start | bytes 388
  138.5 9.3 %collective-permute-start.12 = (bf16[96,640]{1,0:T(8,128)(2,1)S(1)}, bf16[96,640]{1,0:T(8,128)(2,1)S(1)}, u32[]{:S(2)}, u32[]{:S(2)}) collective-permute-start(bf16[96,640]{1,0:T(8,128)(2,1)S(1)} %get-tuple-element.45), channel_id=1, source_target_pairs={{0,96},{32,0},{64,32},{96,64},{1,97},{33,1},{65,33},{97,65},{2,98}... | collective-permute-start | bytes 368648 | tf_op jit(solution)/shard_map/ppermute | solution.py:261
  143.1 8.9 %collective-permute-start.13 = (bf16[96,640]{1,0:T(8,128)(2,1)S(1)}, bf16[96,640]{1,0:T(8,128)(2,1)S(1)}, u32[]{:S(2)}, u32[]{:S(2)}) collective-permute-start(bf16[96,640]{1,0:T(8,128)(2,1)S(1)} %get-tuple-element.46), channel_id=1, source_target_pairs={{0,64},{32,96},{64,0},{96,32},{1,65},{33,97},{65,1},{97,33},{2,66}... | collective-permute-start | bytes 368648 | tf_op jit(solution)/shard_map/ppermute | solution.py:261
  145.1 10.8 %collective-permute-start.14 = (bf16[96,640]{1,0:T(8,128)(2,1)S(1)}, bf16[96,640]{1,0:T(8,128)(2,1)S(1)}, u32[]{:S(2)}, u32[]{:S(2)}) collective-permute-start(bf16[96,640]{1,0:T(8,128)(2,1)S(1)} %get-tuple-element.47), channel_id=1, source_target_pairs={{0,32},{32,64},{64,96},{96,0},{1,33},{33,65},{65,97},{97,1},{2,34}... | collective-permute-start | bytes 368648 | tf_op jit(solution)/shard_map/ppermute | solution.py:261
  (4 other events, 40.0 us)

commit v6 on v5

--- a/solution.py
+++ b/solution.py
@@ -395,7 +395,7 @@
         in_specs=[VMEM] * 4,
         out_specs=VMEM,
         compiler_params=params(16),
-    )(parts[0], *[shift(parts[k], -k) for k in (1, 2, 3)])
+    )(parts[0], *[shift(parts[k], -k) for k in BLOCK_SHIFTS[1:]])
     attn_out = merged.reshape(3, heads, KV_RANK)
     moe_out = pl.pallas_call(
         combine_kernel,

time: 163 us -> 163 us (level)
    ppermute x8, waiting for transfers between devices: 13.6 us -> 10.2 us  [shift(): return lax.ppermute(x, 'tp', [(i, (i + k) % N_TP) for i in range(N_TP)])]
    all_to_all x1, waiting for transfers between devices: 2.88 us -> 5.75 us  [per_device(): lax.all_to_all(expert_out.reshape(N_TP * ranks_ep, CAP, N_DP * cols), ('t...]
where the time goes in v6:
time: 163 us; the launch traced here: 161 us
  starting transfers between devices  90.4 us (55%)
  waiting for transfers between devices  47 us (29%)
  Pallas kernels  17.3 us (11%)
  between operations  2.89 us (2%)
  local copies, waits for them, and re-layouts  2.79 us (2%)
    ppermute x9, waiting for transfers between devices, swap(): return lax.ppermute(x, 'dp', [(i, i ^ bit) for i in range(N_DP)])  28.2 us
    ppermute x9, starting transfers between devices, swap(): return lax.ppermute(x, 'dp', [(i, i ^ bit) for i in range(N_DP)])  28 us
    ppermute x8, starting transfers between devices, shift(): return lax.ppermute(x, 'tp', [(i, (i + k) % N_TP) for i in range(N_TP)])  27.8 us
    all_to_all x1, starting transfers between devices, per_device(): lax.all_to_all(sent.reshape(ranks_ep, CAP * 4, quarter), 'ep', split_axis...  17 us
    all_to_all x1, starting transfers between devices, per_device(): lax.all_to_all(expert_out.reshape(N_TP * ranks_ep, CAP, N_DP * cols), ('t...  13.7 us
    ppermute x8, waiting for transfers between devices, shift(): return lax.ppermute(x, 'tp', [(i, (i + k) % N_TP) for i in range(N_TP)])  10.2 us
    pallas_call x1, Pallas kernels, per_device(): pl.pallas_call(hidden_kernel, out_shape=jax.ShapeDtypeStruct((N_TP, rows,...  5.92 us
    all_to_all x1, waiting for transfers between devices, per_device(): lax.all_to_all(expert_out.reshape(N_TP * ranks_ep, CAP, N_DP * cols), ('t...  5.75 us
  transfers between devices with their start and end apart: 20, of which 10 were waited for; matrix products, arithmetic and copies ran while one was open for 1% of the time, Pallas kernels for 6%

profile of v6, /device:TPU:1, one launch (start us, length us, event | category | flops | bytes accessed | tf_op | source)
XLA Modules:
  0.0 161.1 jit_solution(125000090776209613)
XLA Ops:
  3.1 17.0 %all-to-all-start = ((bf16[32,8,896]{2,1,0:T(8,128)(2,1)}), bf16[32,8,896]{2,1,0:T(8,128)(2,1)S(1)}, u32[]{:S(2)}, u32[]{:S(2)}) async-start(bf16[32,8,896]{2,1,0:T(8,128)(2,1)} %bitcast.34), calls=%async_computation | async-start | bytes 917504 | tf_op jit(solution)/shard_map/all_to_all | solution.py:308
  21.6 4.4 %collective-permute-start.3 = (bf16[7168,128]{1,0:T(8,128)(2,1)S(1)}, bf16[7168,128]{1,0:T(8,128)(2,1)}, u32[]{:S(2)}, u32[]{:S(2)}) collective-permute-start(bf16[7168,128]{1,0:T(8,128)(2,1)S(1)} %constant_dynamic-update-slice_fusion.w0), channel_id=1, source_target_pairs={{0,256},{128,384},{256,0},{384,128},{1,257},{129,385},{257,1},{385... | collective-permute-start | bytes 5505032 | tf_op jit(solution)/shard_map/ppermute | solution.py:265
  26.0 3.1 %collective-permute-start.4 = (bf16[7168,128]{1,0:T(8,128)(2,1)S(1)}, bf16[7168,128]{1,0:T(8,128)(2,1)}, u32[]{:S(2)}, u32[]{:S(2)}) collective-permute-start(bf16[7168,128]{1,0:T(8,128)(2,1)S(1)} %constant_dynamic-update-slice_fusion.w0), channel_id=1, source_target_pairs={{0,128},{128,0},{256,384},{384,256},{1,129},{129,1},{257,385},{385... | collective-permute-start | bytes 5505032 | tf_op jit(solution)/shard_map/ppermute | solution.py:265
  31.1 3.2 %collective-permute-start.2 = (bf16[96,576]{1,0:T(8,128)(2,1)S(1)}, bf16[96,576]{1,0:T(8,128)(2,1)S(1)}, u32[]{:S(2)}, u32[]{:S(2)}) collective-permute-start(bf16[96,576]{1,0:T(8,128)(2,1)S(1)} %bitcast.26), channel_id=1, source_target_pairs={{0,32},{32,64},{64,96},{96,0},{1,33},{33,65},{65,97},{97,1},{2,34}... | collective-permute-start | bytes 331784 | tf_op jit(solution)/shard_map/ppermute | solution.py:261
  34.3 2.7 %collective-permute-start.1 = (bf16[1152,128]{1,0:T(8,128)(2,1)}, bf16[1152,128]{1,0:T(8,128)(2,1)}, u32[]{:S(2)}, u32[]{:S(2)}) collective-permute-start(bf16[1152,128]{1,0:T(8,128)(2,1)} %bitcast.8.m0), channel_id=1, source_target_pairs={{0,128},{128,0},{256,384},{384,256},{1,129},{129,1},{257,385},{385... | collective-permute-start | bytes 884744 | tf_op jit(solution)/shard_map/ppermute | solution.py:265
  39.6 3.4 %collective-permute-start.5 = (bf16[192,576]{1,0:T(8,128)(2,1)}, bf16[192,576]{1,0:T(8,128)(2,1)}, u32[]{:S(2)}, u32[]{:S(2)}) collective-permute-start(bf16[192,576]{1,0:T(8,128)(2,1)} %pad_maximum_fusion), channel_id=1, source_target_pairs={{0,64},{32,96},{64,0},{96,32},{1,65},{33,97},{65,1},{97,33},{2,66}... | collective-permute-start | bytes 663560 | tf_op jit(solution)/shard_map/ppermute | solution.py:261
  45.1 2.9 %all-to-all-done = bf16[32,8,896]{2,1,0:T(8,128)(2,1)S(1)} async-done(((bf16[32,8,896]{2,1,0:T(8,128)(2,1)}), bf16[32,8,896]{2,1,0:T(8,128)(2,1)S(1)}, u32[]{:S(2)}, u32[]{:S(2)}) %all-to-all-start) | async-done | bytes 458784 | tf_op jit(solution)/shard_map/all_to_all | solution.py:308
  47.9 4.8 %collective-permute-start.6 = (bf16[256,896]{1,0:T(8,128)(2,1)S(1)}, bf16[256,896]{1,0:T(8,128)(2,1)S(1)}, u32[]{:S(2)}, u32[]{:S(2)}) collective-permute-start(bf16[256,896]{1,0:T(8,128)(2,1)S(1)} %bitcast.18), channel_id=1, source_target_pairs={{0,64},{32,96},{64,0},{96,32},{1,65},{33,97},{65,1},{97,33},{2,66}... | collective-permute-start | bytes 1376264 | tf_op jit(solution)/shard_map/ppermute | solution.py:261
  55.1 4.2 %collective-permute-start.8 = (bf16[256,896]{1,0:T(8,128)(2,1)S(1)}, bf16[256,896]{1,0:T(8,128)(2,1)S(1)}, u32[]{:S(2)}, u32[]{:S(2)}) collective-permute-start(bf16[256,896]{1,0:T(8,128)(2,1)S(1)} %bitcast.20), channel_id=1, source_target_pairs={{0,96},{32,0},{64,32},{96,64},{1,97},{33,1},{65,33},{97,65},{2,98}... | collective-permute-start | bytes 1376264 | tf_op jit(solution)/shard_map/ppermute | solution.py:261
  59.3 10.7 %collective-permute-done.3.w2 = bf16[7168,128]{1,0:T(8,128)(2,1)} collective-permute-done((bf16[7168,128]{1,0:T(8,128)(2,1)S(1)}, bf16[7168,128]{1,0:T(8,128)(2,1)}, u32[]{:S(2)}, u32[]{:S(2)}) %collective-permute-start.3) | collective-permute-done | bytes 1835040 | tf_op jit(solution)/shard_map/ppermute | solution.py:265
  70.0 3.6 %collective-permute-done.7.b2 = bf16[256,896]{1,0:T(8,128)(2,1)S(1)} collective-permute-done((bf16[256,896]{1,0:T(8,128)(2,1)S(1)}, bf16[256,896]{1,0:T(8,128)(2,1)S(1)}, u32[]{:S(2)}, u32[]{:S(2)}) %collective-permute-start.7) | collective-permute-done | bytes 458784 | tf_op jit(solution)/shard_map/ppermute | solution.py:261
  73.6 2.7 %collective-permute-start.9 = (bf16[7168,128]{1,0:T(8,128)(2,1)}, bf16[7168,128]{1,0:T(8,128)(2,1)S(1)}, u32[]{:S(2)}, u32[]{:S(2)}) collective-permute-start(bf16[7168,128]{1,0:T(8,128)(2,1)} %collective-permute-done.3.w2), channel_id=1, source_target_pairs={{0,128},{128,0},{256,384},{384,256},{1,129},{129,1},{257,385},{385... | collective-permute-start | bytes 5505032 | tf_op jit(solution)/shard_map/ppermute | solution.py:265
  76.3 4.4 %collective-permute-start.15 = (bf16[224,2048]{1,0:T(8,128)(2,1)S(1)}, bf16[224,2048]{1,0:T(8,128)(2,1)}, u32[]{:S(2)}, u32[]{:S(2)}) collective-permute-start(bf16[224,2048]{1,0:T(8,128)(2,1)S(1)} %bitcast.23), channel_id=1, source_target_pairs={{0,256},{128,384},{256,0},{384,128},{1,257},{129,385},{257,1},{385... | collective-permute-start | bytes 2752520 | tf_op jit(solution)/shard_map/ppermute | solution.py:265
  80.7 5.9 %shard_map.150 = bf16[4,256,512]{2,1,0:T(8,128)(2,1)} custom-call(s32[5]{0:T(128)S(1)} %stack.11.where_ref, bf16[256,896]{1,0:T(8,128)(2,1)S(1)} %bitcast.21, bf16[256,896]{1,0:T(8,128)(2,1)S(1)} %collective-permute-done.6.b1, bf16[256,896]{1,0:T(8,128)(2,1)S(1)} %collective-permute-done.7.b2, bf16[256,896]{1,0:T(8,128)(2,1)S(1)} %collective-permute-done.8.b3, ...), custom_call_target="tpu_custom_call" | custom-call | tf_op jit(solution)/shard_map/pallas_call | solution.py:333
  86.6 3.8 %all-to-all-start.1 = ((bf16[4,256,512]{2,1,0:T(8,128)(2,1)}), bf16[4,256,512]{2,1,0:T(8,128)(2,1)S(1)}, u32[]{:S(2)}, u32[]{:S(2)}) async-start(bf16[4,256,512]{2,1,0:T(8,128)(2,1)} %shard_map.150), calls=%async_computation.1 | async-start | bytes 2097152 | tf_op jit(solution)/shard_map/all_to_all | solution.py:342
  90.5 3.6 %collective-permute-start.10 = (bf16[1152,128]{1,0:T(8,128)(2,1)}, bf16[1152,128]{1,0:T(8,128)(2,1)S(1)}, u32[]{:S(2)}, u32[]{:S(2)}) collective-permute-start(bf16[1152,128]{1,0:T(8,128)(2,1)} %bitcast.8.m0), channel_id=1, source_target_pairs={{0,256},{128,384},{256,0},{384,128},{1,257},{129,385},{257,1},{385... | collective-permute-start | bytes 884744 | tf_op jit(solution)/shard_map/ppermute | solution.py:265
  94.1 14.0 %collective-permute-done.10.m2 = bf16[1152,128]{1,0:T(8,128)(2,1)S(1)} collective-permute-done((bf16[1152,128]{1,0:T(8,128)(2,1)}, bf16[1152,128]{1,0:T(8,128)(2,1)S(1)}, u32[]{:S(2)}, u32[]{:S(2)}) %collective-permute-start.10) | collective-permute-done | bytes 294944 | tf_op jit(solution)/shard_map/ppermute | solution.py:265
  108.0 2.7 %collective-permute-start.16 = (bf16[224,2048]{1,0:T(8,128)(2,1)}, bf16[224,2048]{1,0:T(8,128)(2,1)S(1)}, u32[]{:S(2)}, u32[]{:S(2)}) collective-permute-start(bf16[224,2048]{1,0:T(8,128)(2,1)} %collective-permute-done.15.d2), channel_id=1, source_target_pairs={{0,128},{128,0},{256,384},{384,256},{1,129},{129,1},{257,385},{385... | collective-permute-start | bytes 2752520 | tf_op jit(solution)/shard_map/ppermute | solution.py:265
  113.0 3.5 %shard_map.153 = bf16[256,896]{1,0:T(8,128)(2,1)S(1)} custom-call(s32[5]{0:T(128)S(1)} %stack.11.where_ref, bf16[4,256,512]{2,1,0:T(8,128)(2,1)S(1)} %all-to-all-done.1.parts, bf16[224,2048]{1,0:T(8,128)(2,1)S(1)} %bitcast.24, bf16[224,2048]{1,0:T(8,128)(2,1)} %collective-permute-done.d1, bf16[224,2048]{1,0:T(8,128)(2,1)} %collective-permute-done.15.d2, ...), custom_call_target="tpu_custom_call" | custom-call | tf_op jit(solution)/shard_map/pallas_call | solution.py:346
  117.5 13.7 %all-to-all-start.2 = ((bf16[128,2,896]{2,1,0:T(2,128)(2,1)}), bf16[128,2,896]{2,1,0:T(2,128)(2,1)S(1)}, u32[]{:S(2)}, u32[]{:S(2)}) async-start(bf16[128,2,896]{2,1,0:T(2,128)(2,1)} %reshape.38), calls=%async_computation.2 | async-start | bytes 917504 | tf_op jit(solution)/shard_map/all_to_all | solution.py:358
  135.0 3.4 %shard_map.151 = (bf16[96,640]{1,0:T(8,128)(2,1)S(1)}, bf16[96,640]{1,0:T(8,128)(2,1)S(1)}, bf16[96,640]{1,0:T(8,128)(2,1)S(1)}, bf16[96,640]{1,0:T(8,128)(2,1)S(1)}) custom-call(s32[5]{0:T(128)S(1)} %stack.11.where_ref, s32[6]{0:T(128)S(1)} %bitcast.32, s32[3]{0:T(128)S(1)} %bitcast.33, bf16[96,576]{1,0:T(8,128)(2,1)S(1)} %bitcast.28, ...), custom_call_target="tpu_custom_call" | custom-call | tf_op jit(solution)/shard_map/pallas_call | solution.py:367
  138.4 4.6 %collective-permute-start.12 = (bf16[96,640]{1,0:T(8,128)(2,1)S(1)}, bf16[96,640]{1,0:T(8,128)(2,1)S(1)}, u32[]{:S(2)}, u32[]{:S(2)}) collective-permute-start(bf16[96,640]{1,0:T(8,128)(2,1)S(1)} %get-tuple-element.45), channel_id=1, source_target_pairs={{0,64},{32,96},{64,0},{96,32},{1,65},{33,97},{65,1},{97,33},{2,66}... | collective-permute-start | bytes 368648 | tf_op jit(solution)/shard_map/ppermute | solution.py:261
  145.6 2.7 %collective-permute-start.14 = (bf16[96,640]{1,0:T(8,128)(2,1)S(1)}, bf16[96,640]{1,0:T(8,128)(2,1)S(1)}, u32[]{:S(2)}, u32[]{:S(2)}) collective-permute-start(bf16[96,640]{1,0:T(8,128)(2,1)S(1)} %get-tuple-element.47), channel_id=1, source_target_pairs={{0,32},{32,64},{64,96},{96,0},{1,33},{33,65},{65,97},{97,1},{2,34}... | collective-permute-start | bytes 368648 | tf_op jit(solution)/shard_map/ppermute | solution.py:261
  154.0 5.8 %all-to-all-done.2 = bf16[128,2,896]{2,1,0:T(2,128)(2,1)S(1)} async-done(((bf16[128,2,896]{2,1,0:T(2,128)(2,1)}), bf16[128,2,896]{2,1,0:T(2,128)(2,1)S(1)}, u32[]{:S(2)}, u32[]{:S(2)}) %all-to-all-start.2) | async-done | bytes 458784 | tf_op jit(solution)/shard_map/all_to_all | solution.py:358
  (44 shorter events, 27.5 us)
Async XLA Ops:
  3.1 44.9 %all-to-all-start = ((bf16[32,8,896]{2,1,0:T(8,128)(2,1)}), bf16[32,8,896]{2,1,0:T(8,128)(2,1)S(1)}, u32[]{:S(2)}, u32[]{:S(2)}) async-start(bf16[32,8,896]{2,1,0:T(8,128)(2,1)} %bitcast.34), calls=%async_computation | async-start | bytes 917504 | tf_op jit(solution)/shard_map/all_to_all | solution.py:308
  21.6 48.4 %collective-permute-start.3 = (bf16[7168,128]{1,0:T(8,128)(2,1)S(1)}, bf16[7168,128]{1,0:T(8,128)(2,1)}, u32[]{:S(2)}, u32[]{:S(2)}) collective-permute-start(bf16[7168,128]{1,0:T(8,128)(2,1)S(1)} %constant_dynamic-update-slice_fusion.w0), channel_id=1, source_target_pairs={{0,256},{128,384},{256,0},{384,128},{1,257},{129,385},{257,1},{385... | collective-permute-start | bytes 5505032 | tf_op jit(solution)/shard_map/ppermute | solution.py:265
  26.0 44.0 %collective-permute-start.4 = (bf16[7168,128]{1,0:T(8,128)(2,1)S(1)}, bf16[7168,128]{1,0:T(8,128)(2,1)}, u32[]{:S(2)}, u32[]{:S(2)}) collective-permute-start(bf16[7168,128]{1,0:T(8,128)(2,1)S(1)} %constant_dynamic-update-slice_fusion.w0), channel_id=1, source_target_pairs={{0,128},{128,0},{256,384},{384,256},{1,129},{129,1},{257,385},{385... | collective-permute-start | bytes 5505032 | tf_op jit(solution)/shard_map/ppermute | solution.py:265
  29.1 15.9 %collective-permute-start = (bf16[224,2048]{1,0:T(8,128)(2,1)S(1)}, bf16[224,2048]{1,0:T(8,128)(2,1)}, u32[]{:S(2)}, u32[]{:S(2)}) collective-permute-start(bf16[224,2048]{1,0:T(8,128)(2,1)S(1)} %bitcast.22), channel_id=1, source_target_pairs={{0,128},{128,0},{256,384},{384,256},{1,129},{129,1},{257,385},{385... | collective-permute-start | bytes 2752520 | tf_op jit(solution)/shard_map/ppermute | solution.py:265
  31.1 7.7 %collective-permute-start.2 = (bf16[96,576]{1,0:T(8,128)(2,1)S(1)}, bf16[96,576]{1,0:T(8,128)(2,1)S(1)}, u32[]{:S(2)}, u32[]{:S(2)}) collective-permute-start(bf16[96,576]{1,0:T(8,128)(2,1)S(1)} %bitcast.26), channel_id=1, source_target_pairs={{0,32},{32,64},{64,96},{96,0},{1,33},{33,65},{65,97},{97,1},{2,34}... | collective-permute-start | bytes 331784 | tf_op jit(solution)/shard_map/ppermute | solution.py:261
  34.3 10.8 %collective-permute-start.1 = (bf16[1152,128]{1,0:T(8,128)(2,1)}, bf16[1152,128]{1,0:T(8,128)(2,1)}, u32[]{:S(2)}, u32[]{:S(2)}) collective-permute-start(bf16[1152,128]{1,0:T(8,128)(2,1)} %bitcast.8.m0), channel_id=1, source_target_pairs={{0,128},{128,0},{256,384},{384,256},{1,129},{129,1},{257,385},{385... | collective-permute-start | bytes 884744 | tf_op jit(solution)/shard_map/ppermute | solution.py:265
  39.6 15.5 %collective-permute-start.5 = (bf16[192,576]{1,0:T(8,128)(2,1)}, bf16[192,576]{1,0:T(8,128)(2,1)}, u32[]{:S(2)}, u32[]{:S(2)}) collective-permute-start(bf16[192,576]{1,0:T(8,128)(2,1)} %pad_maximum_fusion), channel_id=1, source_target_pairs={{0,64},{32,96},{64,0},{96,32},{1,65},{33,97},{65,1},{97,33},{2,66}... | collective-permute-start | bytes 663560 | tf_op jit(solution)/shard_map/ppermute | solution.py:261
  47.9 22.1 %collective-permute-start.6 = (bf16[256,896]{1,0:T(8,128)(2,1)S(1)}, bf16[256,896]{1,0:T(8,128)(2,1)S(1)}, u32[]{:S(2)}, u32[]{:S(2)}) collective-permute-start(bf16[256,896]{1,0:T(8,128)(2,1)S(1)} %bitcast.18), channel_id=1, source_target_pairs={{0,64},{32,96},{64,0},{96,32},{1,65},{33,97},{65,1},{97,33},{2,66}... | collective-permute-start | bytes 1376264 | tf_op jit(solution)/shard_map/ppermute | solution.py:261
  52.7 20.8 %collective-permute-start.7 = (bf16[256,896]{1,0:T(8,128)(2,1)S(1)}, bf16[256,896]{1,0:T(8,128)(2,1)S(1)}, u32[]{:S(2)}, u32[]{:S(2)}) collective-permute-start(bf16[256,896]{1,0:T(8,128)(2,1)S(1)} %bitcast.19), channel_id=1, source_target_pairs={{0,32},{32,64},{64,96},{96,0},{1,33},{33,65},{65,97},{97,1},{2,34}... | collective-permute-start | bytes 1376264 | tf_op jit(solution)/shard_map/ppermute | solution.py:261
  55.1 18.5 %collective-permute-start.8 = (bf16[256,896]{1,0:T(8,128)(2,1)S(1)}, bf16[256,896]{1,0:T(8,128)(2,1)S(1)}, u32[]{:S(2)}, u32[]{:S(2)}) collective-permute-start(bf16[256,896]{1,0:T(8,128)(2,1)S(1)} %bitcast.20), channel_id=1, source_target_pairs={{0,96},{32,0},{64,32},{96,64},{1,97},{33,1},{65,33},{97,65},{2,98}... | collective-permute-start | bytes 1376264 | tf_op jit(solution)/shard_map/ppermute | solution.py:261
  73.6 7.1 %collective-permute-start.9 = (bf16[7168,128]{1,0:T(8,128)(2,1)}, bf16[7168,128]{1,0:T(8,128)(2,1)S(1)}, u32[]{:S(2)}, u32[]{:S(2)}) collective-permute-start(bf16[7168,128]{1,0:T(8,128)(2,1)} %collective-permute-done.3.w2), channel_id=1, source_target_pairs={{0,128},{128,0},{256,384},{384,256},{1,129},{129,1},{257,385},{385... | collective-permute-start | bytes 5505032 | tf_op jit(solution)/shard_map/ppermute | solution.py:265
  76.3 31.7 %collective-permute-start.15 = (bf16[224,2048]{1,0:T(8,128)(2,1)S(1)}, bf16[224,2048]{1,0:T(8,128)(2,1)}, u32[]{:S(2)}, u32[]{:S(2)}) collective-permute-start(bf16[224,2048]{1,0:T(8,128)(2,1)S(1)} %bitcast.23), channel_id=1, source_target_pairs={{0,256},{128,384},{256,0},{384,128},{1,257},{129,385},{257,1},{385... | collective-permute-start | bytes 2752520 | tf_op jit(solution)/shard_map/ppermute | solution.py:265
  86.6 21.4 %all-to-all-start.1 = ((bf16[4,256,512]{2,1,0:T(8,128)(2,1)}), bf16[4,256,512]{2,1,0:T(8,128)(2,1)S(1)}, u32[]{:S(2)}, u32[]{:S(2)}) async-start(bf16[4,256,512]{2,1,0:T(8,128)(2,1)} %shard_map.150), calls=%async_computation.1 | async-start | bytes 2097152 | tf_op jit(solution)/shard_map/all_to_all | solution.py:342
  90.5 17.5 %collective-permute-start.10 = (bf16[1152,128]{1,0:T(8,128)(2,1)}, bf16[1152,128]{1,0:T(8,128)(2,1)S(1)}, u32[]{:S(2)}, u32[]{:S(2)}) collective-permute-start(bf16[1152,128]{1,0:T(8,128)(2,1)} %bitcast.8.m0), channel_id=1, source_target_pairs={{0,256},{128,384},{256,0},{384,128},{1,257},{129,385},{257,1},{385... | collective-permute-start | bytes 884744 | tf_op jit(solution)/shard_map/ppermute | solution.py:265
  108.0 5.0 %collective-permute-start.16 = (bf16[224,2048]{1,0:T(8,128)(2,1)}, bf16[224,2048]{1,0:T(8,128)(2,1)S(1)}, u32[]{:S(2)}, u32[]{:S(2)}) collective-permute-start(bf16[224,2048]{1,0:T(8,128)(2,1)} %collective-permute-done.15.d2), channel_id=1, source_target_pairs={{0,128},{128,0},{256,384},{384,256},{1,129},{129,1},{257,385},{385... | collective-permute-start | bytes 2752520 | tf_op jit(solution)/shard_map/ppermute | solution.py:265
  116.6 18.4 %copy-start.1 = (bf16[6,128,576]{1,2,0:T(8,128)(2,1)S(1)}, bf16[6,128,576]{1,2,0:T(8,128)(2,1)}, u32[]{:S(2)}) copy-start(bf16[6,128,576]{1,2,0:T(8,128)(2,1)} %param.15) | copy-start | bytes 2654212
  116.6 18.4 %copy-start.5 = (s32[1,6]{1,0:T(1,128)S(1)}, s32[1,6]{1,0:T(1,128)}, u32[]{:S(2)}) copy-start(s32[1,6]{1,0:T(1,128)} %param.16) | copy-start | bytes 76
  117.5 42.2 %all-to-all-start.2 = ((bf16[128,2,896]{2,1,0:T(2,128)(2,1)}), bf16[128,2,896]{2,1,0:T(2,128)(2,1)S(1)}, u32[]{:S(2)}, u32[]{:S(2)}) async-start(bf16[128,2,896]{2,1,0:T(2,128)(2,1)} %reshape.38), calls=%async_computation.2 | async-start | bytes 917504 | tf_op jit(solution)/shard_map/all_to_all | solution.py:358
  131.2 3.8 %collective-permute-start.11 = (bf16[1152,128]{1,0:T(8,128)(2,1)S(1)}, bf16[1152,128]{1,0:T(8,128)(2,1)S(1)}, u32[]{:S(2)}, u32[]{:S(2)}) collective-permute-start(bf16[1152,128]{1,0:T(8,128)(2,1)S(1)} %collective-permute-done.10.m2), channel_id=1, source_target_pairs={{0,128},{128,0},{256,384},{384,256},{1,129},{129,1},{257,385},{385... | collective-permute-start | bytes 884744 | tf_op jit(solution)/shard_map/ppermute | solution.py:265
  135.0 24.9 %copy-start.3 = (s32[16,2]{0,1:T(2,128)S(1)}, s32[16,2]{0,1:T(2,128)}, u32[]{:S(2)}) copy-start(s32[16,2]{0,1:T(2,128)} %param.23) | copy-start | bytes 388
  135.0 24.9 %copy-start.4 = (f32[16,2]{0,1:T(2,128)S(1)}, f32[16,2]{0,1:T(2,128)}, u32[]{:S(2)}) copy-start(f32[16,2]{0,1:T(2,128)} %param.24) | copy-start | bytes 388
  138.4 9.9 %collective-permute-start.12 = (bf16[96,640]{1,0:T(8,128)(2,1)S(1)}, bf16[96,640]{1,0:T(8,128)(2,1)S(1)}, u32[]{:S(2)}, u32[]{:S(2)}) collective-permute-start(bf16[96,640]{1,0:T(8,128)(2,1)S(1)} %get-tuple-element.45), channel_id=1, source_target_pairs={{0,64},{32,96},{64,0},{96,32},{1,65},{33,97},{65,1},{97,33},{2,66}... | collective-permute-start | bytes 368648 | tf_op jit(solution)/shard_map/ppermute | solution.py:261
  143.0 7.7 %collective-permute-start.13 = (bf16[96,640]{1,0:T(8,128)(2,1)S(1)}, bf16[96,640]{1,0:T(8,128)(2,1)S(1)}, u32[]{:S(2)}, u32[]{:S(2)}) collective-permute-start(bf16[96,640]{1,0:T(8,128)(2,1)S(1)} %get-tuple-element.46), channel_id=1, source_target_pairs={{0,96},{32,0},{64,32},{96,64},{1,97},{33,1},{65,33},{97,65},{2,98}... | collective-permute-start | bytes 368648 | tf_op jit(solution)/shard_map/ppermute | solution.py:261
  145.6 7.5 %collective-permute-start.14 = (bf16[96,640]{1,0:T(8,128)(2,1)S(1)}, bf16[96,640]{1,0:T(8,128)(2,1)S(1)}, u32[]{:S(2)}, u32[]{:S(2)}) collective-permute-start(bf16[96,640]{1,0:T(8,128)(2,1)S(1)} %get-tuple-element.47), channel_id=1, source_target_pairs={{0,32},{32,64},{64,96},{96,0},{1,33},{33,65},{65,97},{97,1},{2,34}... | collective-permute-start | bytes 368648 | tf_op jit(solution)/shard_map/ppermute | solution.py:261
  (4 other events, 40.0 us)
